TPU v7x, 32 devices: a whole 2x2x4 slice. The times are simulated.
32 devices in a mesh: poles: 2 (over y), row: 8 (over z, x), col: 2 (over core).
Axes of the slice: x: 2, y: 2, z: 4, core: 2. Of those that a mesh axis runs over, the one named last changes fastest.
Arguments:
- ainv_top: bfloat16 [2048, 1024], P(('poles', 'row', 'col')), parts along dimension 0, as said below
- l_parent: bfloat16 [16, 1024, 512], P(('poles', 'row'), None, 'col'), parts along dimension 0, may hold values from -0.25 to 0.25
- dinv_parent: bfloat16 [16, 512, 512], P(('poles', 'row'), None, 'col'), parts along dimension 0, as said below
- keep_parent: int32 [16, 2], P(('poles', 'row')), parts along dimension 0, may hold values from 0 to 1
- l_child: bfloat16 [32, 1536, 512], P(('poles', 'row'), None, 'col'), parts along dimension 0, may hold values from -0.25 to 0.25
- dinv_child: bfloat16 [32, 512, 512], P(('poles', 'row'), None, 'col'), parts along dimension 0, as said below
- keep_child: int32 [32, 2], P(('poles', 'row')), parts along dimension 0, may hold values from 0 to 1, as said below
- parent_of: int32 [32], P(('poles', 'row')), parts along dimension 0, may hold values from 0 to 7, as said below
Outputs:
- parent_diag: bfloat16 [16, 512, 512], P(('poles', 'row'), None, 'col'), parts along dimension 0
- child_column: bfloat16 [32, 1536, 512], P(('poles', 'row'), None, 'col'), parts along dimension 0
- child_diag: bfloat16 [32, 512, 512], P(('poles', 'row'), None, 'col'), parts along dimension 0
There are 2 independent parts, one for each index of `poles`. A program takes and returns all parts, laid end to end along the dimension named above; each array names one. Nothing has to cross between parts.
Inputs may be any that keep to these rules, and one draw needn't show every extreme that they name: `ainv_top`: symmetric. `dinv_parent`: each block symmetric. `dinv_child`: each block symmetric. `keep_child`: a lower-level supernode keeps a top block only where its parent keeps it. `parent_of`: the parent of a supernode held by row index r is upper-level supernode number r + d with |d| <= 1; the first supernode of each row index has |d| = 1 wherever r + d stays in range.
All inputs are finite; a program needn't handle non-finite values.
Results may differ from a plain program's by a relative error of at most 0.0051.
Values may be sent and summed in bfloat16 or wider, within the bound.
No kernel may reach another device: no remote copies, remote signals or barrier semaphores. Data moves between devices by JAX's collectives and lax.ppermute only.
A program may use at most 64 MiB of HBM per device.

v0:
```python
import jax
import jax.numpy as jnp
from jax import lax
from jax.sharding import PartitionSpec as P

HOP = 1


def extended(x, sides, width):
    for axis, dim in sides:
        devices, length = (lax.axis_size(axis), x.shape[dim])
        up = [(i, (i + 1) % devices) for i in range(devices - 1)]
        down = [(j, i) for i, j in up]
        last = lax.slice_in_dim(x, length - width, length, axis=dim)
        leading = lax.slice_in_dim(x, 0, width, axis=dim)
        before = lax.ppermute(last, axis, up)
        after = lax.ppermute(leading, axis, down)
        x = jnp.concatenate([before, x, after], axis=dim)
    return x


def local(ainv_top, l_parent, dinv_parent, keep_parent, l_child, dinv_child, keep_child, parent_of):
    width = dinv_parent.shape[1]
    parent_rows = jnp.repeat(keep_parent, width, axis=1).astype(jnp.bfloat16)
    x_parent = l_parent * parent_rows[:, :, None]
    child_ones = jnp.ones((keep_child.shape[0], width), jnp.int32)
    child_rows = jnp.concatenate(
        [child_ones, jnp.repeat(keep_child, width, axis=1)], axis=1
    ).astype(jnp.bfloat16)
    x_child = l_child * child_rows[:, :, None]
    panels = jnp.concatenate([x_parent, x_child[:, width:, :]], axis=0)
    tops = jnp.einsum(
        "nj,mjc->mnc",
        lax.all_gather(ainv_top, ("row", "col"), axis=0, tiled=True),
        panels,
        preferred_element_type=jnp.float32,
    )
    g_parent = (-tops[:1]).astype(jnp.bfloat16)
    full_parent, full_child = (
        lax.all_gather(x_parent, "col", axis=2, tiled=True),
        lax.all_gather(x_child, "col", axis=2, tiled=True),
    )
    parent_diag = (
        dinv_parent.astype(jnp.float32)
        - jnp.einsum("mic,mid->mcd", full_parent, g_parent, preferred_element_type=jnp.float32)
    ).astype(jnp.bfloat16)
    column = jnp.concatenate([parent_diag, g_parent], axis=1)
    nearest = parent_of - lax.axis_index("row") + HOP
    full_column = lax.all_gather(column, "col", axis=2, tiled=True)
    near_full = extended(full_column, (("row", 0),), HOP)
    chosen = jnp.take(near_full, nearest, axis=0)
    own_rows = x_child[:, :width, :]
    upper_rows = x_child[:, width:, :]
    product = jnp.einsum("mij,mjc->mic", chosen, own_rows, preferred_element_type=jnp.float32)
    upper = jnp.einsum(
        "mji,mjc->mic", chosen[:, width:, :], upper_rows, preferred_element_type=jnp.float32
    )
    product = product + jnp.concatenate([upper, tops[1:]], axis=1)
    child_column = (-(product * child_rows[:, :, None].astype(jnp.float32))).astype(jnp.bfloat16)
    child_diag = (
        dinv_child.astype(jnp.float32)
        - jnp.einsum("mic,mid->mcd", full_child, child_column, preferred_element_type=jnp.float32)
    ).astype(jnp.bfloat16)
    return (parent_diag, child_column, child_diag)


def solution(mesh):
    placed = (
        P(("poles", "row", "col"), None),
        P(("poles", "row"), None, "col"),
        P(("poles", "row"), None, "col"),
        P(("poles", "row"), None),
        P(("poles", "row"), None, "col"),
        P(("poles", "row"), None, "col"),
        P(("poles", "row"), None),
        P(("poles", "row")),
    )
    return jax.shard_map(
        local,
        mesh=mesh,
        in_specs=placed,
        out_specs=(
            P(("poles", "row"), None, "col"),
            P(("poles", "row"), None, "col"),
            P(("poles", "row"), None, "col"),
        ),
        check_vma=False,
    )
```

profile of v0, /device:TPU:3, one launch (start us, length us, event | category | flops | bytes accessed | tf_op | source)
XLA Modules:
  0.0 171.7 jit_solution(14915612216930613284)
XLA Ops:
  7.9 1.2 copy.12
  9.9 0.8 broadcast_multiply_fusion.1
  10.9 1.7 copy.13
  12.8 1.1 slice.23
  14.1 38.2 %all-gather.7.cloned.1.call-done = bf16[1024,1024]{1,0:T(8,128)(2,1)} async-done(((bf16[64,1024]{1,0:T(8,128)(2,1)}), bf16[1024,1024]{1,0:T(8,128)(2,1)}) %all-gather.7.cloned.1.call-update) | async-done | bytes 2097168 | tf_op jit(solution)/shard_map/all_gather | solution.py:34
  52.3 3.7 %fusion.7 = f32[3,1024,256]{1,2,0:T(8,128)S(1)} fusion(bf16[1024,1024]{1,0:T(8,128)(2,1)} %all-gather.7.cloned.1.call-done, bf16[2,1024,256]{1,2,0:T(8,128)(2,1)} %slice.23, bf16[1,1024,256]{1,2,0:T(8,128)(2,1)S(1)} %copy-done.3), kind=kOutput, calls=%fused_computation.11 | convolution fusion | flops 1611399168 | bytes 6815744 | tf_op jit(solution)/shard_map/nj,mjc->mnc/dot_general | solution.py:32
  56.1 1.6 copy-done.2
  57.8 5.7 %all-gather.5.cloned.1.call-done = bf16[1,1024,512]{1,2,0:T(8,128)(2,1)} async-done(((bf16[1,1024,256]{1,2,0:T(8,128)(2,1)}), bf16[1,1024,512]{1,2,0:T(8,128)(2,1)}) %all-gather.5.cloned.1.call-update) | async-done | bytes 1048592 | tf_op jit(solution)/shard_map/all_gather | solution.py:40
  63.5 1.7 fusion.15
  65.2 0.9 pad_maximum_fusion.1
  66.2 11.1 %all-gather.9.cloned.1.call-done = bf16[1,1536,512]{1,2,0:T(8,128)(2,1)} async-done(((bf16[1,1536,256]{1,2,0:T(8,128)(2,1)}), bf16[1,1536,512]{1,2,0:T(8,128)(2,1)}) %all-gather.9.cloned.1.call-update) | async-done | bytes 1572880 | tf_op jit(solution)/shard_map/all_gather | solution.py:49
  77.3 1.9 %collective-permute-start.1 = (bf16[1,1536,512]{1,2,0:T(8,128)(2,1)}, bf16[1,1536,512]{1,2,0:T(8,128)(2,1)S(1)}, u32[]{:S(2)}, u32[]{:S(2)}) collective-permute-start(bf16[1,1536,512]{1,2,0:T(8,128)(2,1)} %all-gather.9.cloned.1.call-done), channel_id=1, source_target_pairs={{2,0},{4,2},{6,4},{8,6},{10,8},{12,10},{14,12},{3,1},{5,3},{7,5},{... | collective-permute-start | bytes 4718600 | tf_op jit(solution)/shard_map/ppermute | solution.py:17
  79.2 4.3 %collective-permute-start = (bf16[1,1536,512]{1,2,0:T(8,128)(2,1)}, bf16[1,1536,512]{1,2,0:T(8,128)(2,1)S(1)}, u32[]{:S(2)}, u32[]{:S(2)}) collective-permute-start(bf16[1,1536,512]{1,2,0:T(8,128)(2,1)} %all-gather.9.cloned.1.call-done), channel_id=1, source_target_pairs={{0,2},{2,4},{4,6},{6,8},{8,10},{10,12},{12,14},{1,3},{3,5},{5,7},{... | collective-permute-start | bytes 4718600 | tf_op jit(solution)/shard_map/ppermute | solution.py:16
  83.6 0.8 copy.21
  84.4 31.7 %collective-permute-done.1 = bf16[1,1536,512]{1,2,0:T(8,128)(2,1)S(1)} collective-permute-done((bf16[1,1536,512]{1,2,0:T(8,128)(2,1)}, bf16[1,1536,512]{1,2,0:T(8,128)(2,1)S(1)}, u32[]{:S(2)}, u32[]{:S(2)}) %collective-permute-start.1) | collective-permute-done | bytes 1572896 | tf_op jit(solution)/shard_map/ppermute | solution.py:17
  116.1 34.2 %collective-permute-done = bf16[1,1536,512]{1,2,0:T(8,128)(2,1)S(1)} collective-permute-done((bf16[1,1536,512]{1,2,0:T(8,128)(2,1)}, bf16[1,1536,512]{1,2,0:T(8,128)(2,1)S(1)}, u32[]{:S(2)}, u32[]{:S(2)}) %collective-permute-start) | collective-permute-done | bytes 1572896 | tf_op jit(solution)/shard_map/ppermute | solution.py:16
  150.3 2.4 %pad_maximum_fusion = bf16[3,1536,512]{1,2,0:T(8,128)(2,1)} fusion(bf16[1,1536,512]{1,2,0:T(8,128)(2,1)S(1)} %collective-permute-done.1, bf16[1,1536,512]{1,2,0:T(8,128)(2,1)S(1)} %copy-done.4, bf16[1,1536,512]{1,2,0:T(8,128)(2,1)S(1)} %collective-permute-done), kind=kLoop, calls=%fused_computation.1 | loop fusion | flops 4718592 | bytes 9437184 | tf_op jit(solution)/shard_map/concatenate | solution.py:18
  152.8 3.1 %gather_fusion = bf16[2,1536,512]{1,2,0:T(8,128)(2,1)S(1)} fusion(bf16[3,1536,512]{1,2,0:T(8,128)(2,1)} %pad_maximum_fusion, s32[1024]{0:T(1024)S(1)} %pad_clamp_fusion), kind=kCustom, calls=%fused_computation | custom fusion | bytes 6291464 | tf_op jit(solution)/shard_map/jit(_take)/gather | solution.py:51
  156.2 1.0 copy-done.1
  157.3 0.7 fusion.3
  158.0 0.9 slice-done
  158.9 1.1 fusion.2
  160.0 1.6 copy.22
  161.5 3.7 %fusion.13 = bf16[2,512,256]{2,1,0:T(8,128)(2,1)} fusion(bf16[2,1536,512]{1,2,0:T(8,128)(2,1)} %all-gather.11.cloned.1.call-done, bf16[2,1536,256]{1,2,0:T(8,128)(2,1)S(1)} %fusion.2, bf16[2,512,256]{2,1,0:T(8,128)(2,1)S(1)} %copy-done.7), kind=kOutput, calls=%fused_computation.16 | convolution fusion | flops 806092800 | bytes 5767168 | tf_op jit(solution)/shard_map/mic,mid->mcd/dot_general | solution.py:62
  (39 shorter events, 2.5 us)
Async XLA Ops:
  7.2 45.2 %all-gather.7.cloned.1.call-start = ((), (), s32[]{:S(2)}) async-start(), calls=%async_computation.1 | async-start | bytes 2228224 | tf_op jit(solution)/shard_map/all_gather | solution.py:34
  7.9 55.6 %all-gather.5.cloned.1.call-start = ((), (), s32[]{:S(2)}) async-start(), calls=%async_computation | async-start | bytes 1572864 | tf_op jit(solution)/shard_map/all_gather | solution.py:40
  10.8 1.8 %copy-start.8 = (s32[2,2]{1,0:T(2,128)S(1)}, s32[2,2]{1,0:T(2,128)}, u32[]{:S(2)}) copy-start(s32[2,2]{1,0:T(2,128)} %param.14) | copy-start | bytes 52
  10.8 66.5 %all-gather.9.cloned.1.call-start = ((), (), s32[]{:S(2)}) async-start(), calls=%async_computation.2 | async-start | bytes 2359296 | tf_op jit(solution)/shard_map/all_gather | solution.py:49
  12.7 1.3 copy-start.5
  12.8 43.3 %copy-start = (bf16[2,1536,256]{1,2,0:T(8,128)(2,1)}, bf16[2,1536,256]{1,2,0:T(8,128)(2,1)S(1)}, u32[]{:S(2)}) copy-start(bf16[2,1536,256]{1,2,0:T(8,128)(2,1)S(1)} %broadcast_multiply_fusion) | copy-start | bytes 4718596
  12.8 39.5 %copy-start.3 = (bf16[1,1024,256]{1,2,0:T(8,128)(2,1)S(1)}, bf16[1,1024,256]{1,2,0:T(8,128)(2,1)}, u32[]{:S(2)}) copy-start(bf16[1,1024,256]{1,2,0:T(8,128)(2,1)} %broadcast_multiply_fusion.1) | copy-start | bytes 1572868
  56.1 1.6 copy-start.2
  65.2 18.3 %copy-start.6 = (s32[2]{0:T(128)S(1)}, s32[2]{0:T(128)}, u32[]{:S(2)}) copy-start(s32[2]{0:T(128)} %param.15) | copy-start | bytes 28
  66.2 95.3 %all-gather.11.cloned.1.call-start = ((), (), s32[]{:S(2)}) async-start(), calls=%async_computation.3 | async-start | bytes 4718592 | tf_op jit(solution)/shard_map/all_gather | solution.py:41
  77.3 38.8 %collective-permute-start.1 = (bf16[1,1536,512]{1,2,0:T(8,128)(2,1)}, bf16[1,1536,512]{1,2,0:T(8,128)(2,1)S(1)}, u32[]{:S(2)}, u32[]{:S(2)}) collective-permute-start(bf16[1,1536,512]{1,2,0:T(8,128)(2,1)} %all-gather.9.cloned.1.call-done), channel_id=1, source_target_pairs={{2,0},{4,2},{6,4},{8,6},{10,8},{12,10},{14,12},{3,1},{5,3},{7,5},{... | collective-permute-start | bytes 4718600 | tf_op jit(solution)/shard_map/ppermute | solution.py:17
  79.2 71.1 %collective-permute-start = (bf16[1,1536,512]{1,2,0:T(8,128)(2,1)}, bf16[1,1536,512]{1,2,0:T(8,128)(2,1)S(1)}, u32[]{:S(2)}, u32[]{:S(2)}) collective-permute-start(bf16[1,1536,512]{1,2,0:T(8,128)(2,1)} %all-gather.9.cloned.1.call-done), channel_id=1, source_target_pairs={{0,2},{2,4},{4,6},{6,8},{8,10},{10,12},{12,14},{1,3},{3,5},{5,7},{... | collective-permute-start | bytes 4718600 | tf_op jit(solution)/shard_map/ppermute | solution.py:16
  84.4 65.9 %copy-start.4 = (bf16[1,1536,512]{1,2,0:T(8,128)(2,1)S(1)}, bf16[1,1536,512]{1,2,0:T(8,128)(2,1)}, u32[]{:S(2)}) copy-start(bf16[1,1536,512]{1,2,0:T(8,128)(2,1)} %all-gather.9.cloned.1.call-done) | copy-start | bytes 4718596
  155.9 1.4 copy-start.1
  157.3 1.6 slice-start
  159.9 1.6 copy-start.7
Sparse Core Ops, SparseCore 0:
  10.2 42.1 all-gather.6
  54.4 9.0 all-gather.4
  66.3 10.9 all-gather.8
  83.6 12.9 all-gather.10
where the time goes:
time: 173 us; the launch traced here: 172 us
  waiting for transfers between devices  122 us (71%)
  between operations  14 us (8%)
  local copies, waits for them, and re-layouts  13.4 us (8%)
  matrix products  10.9 us (6%)
  starting transfers between devices  6.33 us (4%)
  other arithmetic  5.44 us (3%)
    all_gather x1, waiting for transfers between devices, local(): lax.all_gather(ainv_top, ('row', 'col'), axis=0, tiled=True)  38.2 us
    ppermute x1, waiting for transfers between devices, extended(): before = lax.ppermute(last, axis, up)  34.2 us
    ppermute x1, waiting for transfers between devices, extended(): after = lax.ppermute(leading, axis, down)  31.7 us
    all_gather x1, waiting for transfers between devices, local(): full_column = lax.all_gather(column, 'col', axis=2, tiled=True)  11.1 us
    unnamed x27, local copies, waits for them, and re-layouts  8.39 us
    all_gather x1, waiting for transfers between devices, local(): lax.all_gather(x_parent, 'col', axis=2, tiled=True)  5.68 us
    ppermute x1, starting transfers between devices, extended(): before = lax.ppermute(last, axis, up)  4.26 us
    dot_general x1, matrix products, local(): jnp.einsum('nj,mjc->mnc', lax.all_gather(ainv_top, ('row', 'col'), axis=0...  3.74 us
  transfers between devices with their start and end apart: 6, of which 5 were waited for; matrix products, arithmetic and copies ran while one was open for 12% of the time, Pallas kernels for 0%

commit v1 on v0

v1 whole, which is shorter than its diff:
```python
import functools

import jax
import jax.numpy as jnp
from jax import lax
from jax.experimental import pallas as pl
from jax.experimental.pallas import tpu as pltpu
from jax.sharding import PartitionSpec as P

DIRECT = 4
F32 = jnp.float32
BF16 = jnp.bfloat16


def dot(a, b):
    return jnp.dot(a, b, preferred_element_type=F32)


def dot_t(a, b):
    return lax.dot_general(a, b, (((0,), (0,)), ((), ())), preferred_element_type=F32)


def kernel(
    place_ref,
    slot_ref,
    keep_ref,
    *refs,
    pieces,
):
    n_a = len(pieces)
    a_refs, refs = refs[:n_a], refs[n_a:]
    (
        xp, xp_o, xs, xs_o, xf, xf_o,
        dp, dp_o, ds, ds_o, df, df_o,
        lc, lc_o, dc,
        pd_out, cc_out, cd_out,
        a, x, d, c, dcv, g, v, t, pd, cc, cd,
        sem, out_sem,
    ) = refs
    half = lc.shape[-1]
    width = 2 * half
    tops = xp.shape[0]
    me = place_ref[0]
    mine = pl.multiple_of(me * half, half)
    other = pl.multiple_of((1 - me) * half, half)
    copies = []

    def start(src, dst):
        copy = pltpu.make_async_copy(src, dst, sem.at[len(copies)])
        copy.start()
        copies.append(copy)

    def start_rows(src, dst):
        start(src.at[pl.ds(mine, half)], dst.at[pl.ds(0, half)])
        start(src.at[pl.ds(other, half)], dst.at[pl.ds(half, half)])

    cols = (pl.ds(0, half), pl.ds(half, half))
    for slot, (left, right) in enumerate(((xp, xp_o), (xs, xs_o), (xf, xf_o))):
        start(left, x.at[slot, :, cols[0]])
        start(right, x.at[slot, :, cols[1]])
    for k in range(lc.shape[0]):
        for side, src in enumerate((lc, lc_o)):
            start_rows(src.at[k], c.at[k, side])
            start(src.at[k, pl.ds(width, tops)], c.at[k, side, pl.ds(width, tops)])
    for ref, piece in zip(a_refs, pieces):
        if piece is None:
            start(ref, a)
            continue
        planes = ref.shape[0]
        block = ref.shape[1]
        flip_pair, flip_core = piece
        pair = 1 - place_ref[2] if flip_pair else place_ref[2]
        core = 1 - me if flip_core else me
        for k in range(planes):
            plane = lax.rem(place_ref[1] + planes - k, planes)
            row = pl.multiple_of(((plane * 2 + pair) * 2 + core) * block, block)
            start(ref.at[k], a.at[pl.ds(row, block)])
    for slot, (left, right) in enumerate(((dp, dp_o), (ds, ds_o), (df, df_o))):
        start_rows(left, d.at[slot, :, cols[0]])
        start_rows(right, d.at[slot, :, cols[1]])
    for k in range(lc.shape[0]):
        start_rows(dc.at[k], dcv.at[k])
    for copy in copies:
        copy.wait()

    step = half
    for i in range(tops // step):
        rows = pl.ds(i * step, step)
        g[rows, :] = (-dot(a[rows, :], x[0, :, :half])).astype(BF16)
    for i in range(2):
        rows = pl.ds(i * half, half)
        pd[rows, :] = (
            d[0, rows, :half].astype(F32) - dot_t(x[0, :, rows], g[...])
        ).astype(BF16)
    outs = []

    def finish(src, dst):
        copy = pltpu.make_async_copy(src, dst, out_sem.at[len(outs)])
        copy.start()
        outs.append(copy)

    def finish_rows(src, dst):
        finish(src.at[pl.ds(0, half)], dst.at[pl.ds(mine, half)])
        finish(src.at[pl.ds(half, half)], dst.at[pl.ds(other, half)])

    finish_rows(pd, pd_out)

    for k in range(lc.shape[0]):
        slot = slot_ref[k]
        u = c[k, 0, pl.ds(0, width), :]
        for i in range(tops // step):
            rows = pl.ds(i * step, step)
            kept = keep_ref[k, i * step // width] > 0
            w = c[k, 0, pl.ds(width + i * step, step), :].astype(F32)
            v[rows, :] = (
                dot(x[slot, rows, :], u) - jnp.where(kept, w, 0.0)
            ).astype(BF16)
        for i in range(tops // step):
            rows = pl.ds(i * step, step)
            kept = keep_ref[k, i * step // width] > 0
            tile = dot(a[rows, :], v[...]).astype(BF16)
            t[rows, :] = tile
            cc[k, pl.ds(width + i * step, step), :] = jnp.where(kept, tile, jnp.zeros_like(tile))
        for i in range(2):
            rows = pl.ds(i * half, half)
            y = dot(d[slot, rows, :], u) + dot_t(x[slot, :, rows], t[...])
            cc[k, rows, :] = (-y).astype(BF16)
        finish_rows(cc.at[k], cc_out.at[k])
        finish(cc.at[k, pl.ds(width, tops)], cc_out.at[k, pl.ds(width, tops)])
        for side in range(2):
            rows = pl.ds(side * half, half)
            cd[k, rows, :] = (
                dcv[k, rows, :].astype(F32) - dot_t(c[k, side], cc[k])
            ).astype(BF16)
        finish_rows(cd.at[k], cd_out.at[k])
    for copy in outs:
        copy.wait()


def local(ainv_top, l_parent, dinv_parent, keep_parent, l_child, dinv_child, keep_child, parent_of):
    devices = lax.axis_size("row")
    planes = devices // 2
    row = lax.axis_index("row")
    swap = [(i, i ^ 1) for i in range(devices)]
    onward = [(i, i - 2 if i % 2 else i + 2) for i in range(devices)]
    onward = [(i, j) for i, j in onward if 0 <= j < devices]
    cores = [(0, 1), (1, 0)]

    def swapped(x):
        return lax.ppermute(x, "row", swap)

    def crossed(x):
        return lax.ppermute(x, "col", cores)

    half = l_parent.shape[2]
    width = 2 * half
    tops = l_parent.shape[1]
    children = l_child.shape[0]
    rows = jnp.repeat(keep_parent[0], width).astype(BF16)
    xp = l_parent[0] * rows[:, None]
    dp = dinv_parent[0]
    xs = swapped(xp)
    if planes <= DIRECT:
        arrived = [ainv_top]
        for k in range(1, planes):
            arrived.append(
                lax.ppermute(ainv_top, "row", [(i, (i + 2 * k) % devices) for i in range(devices)])
            )
        near = jnp.stack(arrived)
        far = swapped(near)
        a_parts = [near, crossed(near), far, crossed(far)]
        pieces = [(False, False), (False, True), (True, False), (True, True)]
    else:
        a_parts = [lax.all_gather(ainv_top, ("row", "col"), axis=0, tiled=True)]
        pieces = [None]
    ds = swapped(dp)
    xf = lax.ppermute(xs, "row", onward)
    df = lax.ppermute(ds, "row", onward)
    operands = [
        xp, crossed(xp), xs, crossed(xs), xf, crossed(xf),
        dp, crossed(dp), ds, crossed(ds), df, crossed(df),
        l_child, crossed(l_child), dinv_child,
    ]
    place = jnp.stack([lax.axis_index("col"), row // 2, row % 2]).astype(jnp.int32)
    slot = jnp.where(parent_of == row, 0, jnp.where(parent_of == row ^ 1, 1, 2)).astype(jnp.int32)
    smem = pl.BlockSpec(memory_space=pltpu.SMEM)
    hbm = pl.BlockSpec(memory_space=pl.ANY)
    parent_diag, child_column, child_diag = pl.pallas_call(
        functools.partial(kernel, pieces=pieces),
        out_shape=(
            jax.ShapeDtypeStruct((width, half), BF16),
            jax.ShapeDtypeStruct(l_child.shape, BF16),
            jax.ShapeDtypeStruct(dinv_child.shape, BF16),
        ),
        in_specs=[smem] * 3 + [hbm] * (len(a_parts) + len(operands)),
        out_specs=(hbm,) * 3,
        scratch_shapes=[
            pltpu.VMEM((tops, tops), BF16),
            pltpu.VMEM((3, tops, width), BF16),
            pltpu.VMEM((3, width, width), BF16),
            pltpu.VMEM((children, 2, width + tops, half), BF16),
            pltpu.VMEM((children, width, half), BF16),
            pltpu.VMEM((tops, half), BF16),
            pltpu.VMEM((tops, half), BF16),
            pltpu.VMEM((tops, half), BF16),
            pltpu.VMEM((width, half), BF16),
            pltpu.VMEM((children, width + tops, half), BF16),
            pltpu.VMEM((children, width, half), BF16),
            pltpu.SemaphoreType.DMA((64,)),
            pltpu.SemaphoreType.DMA((16,)),
        ],
        compiler_params=pltpu.CompilerParams(vmem_limit_bytes=32 << 20),
    )(place, slot, keep_child, *a_parts, *operands)
    return parent_diag[None], child_column, child_diag


def solution(mesh):
    blocks = P(("poles", "row"), None, "col")
    placed = (
        P(("poles", "row", "col"), None),
        blocks,
        blocks,
        P(("poles", "row"), None),
        blocks,
        blocks,
        P(("poles", "row"), None),
        P(("poles", "row")),
    )
    return jax.shard_map(
        local, mesh=mesh, in_specs=placed, out_specs=(blocks,) * 3, check_vma=False
    )
```

time: 173 us -> 67.1 us (0.39)
  waiting for transfers between devices: 122 us -> 29 us
  between operations: 14 us -> 0.82 us
  matrix products: 10.9 us -> 0 us
  starting transfers between devices: 6.33 us -> 16.9 us
  Pallas kernels: 0 us -> 9.69 us
  local copies, waits for them, and re-layouts: 13.4 us -> 7.13 us
  other arithmetic: 5.44 us -> 3.07 us
    all_gather x4 -> x0, waiting for transfers between devices: 55 us -> none  [the longest x1 38.2 us: local(): lax.all_gather(ainv_top, ('row', 'col'), axis=0, tiled=True)]
    ppermute x2 -> x17, waiting for transfers between devices: 65.9 us -> 29 us  [the longest x3 16.2 us: local(): lax.ppermute(ainv_top, 'row', [(i, (i + 2 * k) % devices) for i in range(...]
    dot_general x5 -> x0, matrix products: 10.9 us -> none  [the longest x1 3.74 us: local(): jnp.einsum('nj,mjc->mnc', lax.all_gather(ainv_top, ('row', 'col'), axis=0...]
    ppermute x2 -> x17, starting transfers between devices: 6.17 us -> 16.9 us  [the longest x3 6.92 us: local(): lax.ppermute(ainv_top, 'row', [(i, (i + 2 * k) % devices) for i in range(...]
    pallas_call x0 -> x1, Pallas kernels: none -> 9.69 us  [local(): pl.pallas_call(functools.partial(kernel, pieces=pieces), out_shape=(jax.S...]
    concatenate x2 -> x0, other arithmetic: 3.37 us -> none  [the longest x1 2.44 us: extended(): x = jnp.concatenate([before, x, after], axis=dim)]
    gather x1 -> x0, local copies, waits for them, and re-layouts: 3.08 us -> none  [local(): chosen = jnp.take(near_full, nearest, axis=0)]
    slice x3 -> x0, local copies, waits for them, and re-layouts: 1.98 us -> none  [the longest x1 1.13 us: local(): panels = jnp.concatenate([x_parent, x_child[:, width:, :]], axis=0)]
  transfers between devices with their start and end apart: 6 -> 17, of which waited for: 5 -> 5; matrix products, arithmetic and copies ran while one was open for 12% -> 5% of each run, Pallas kernels for 0% -> 0%
where the time goes in v1:
time: 67.1 us; the launch traced here: 66.7 us
  waiting for transfers between devices  29 us (43%)
  starting transfers between devices  16.9 us (25%)
  Pallas kernels  9.69 us (14%)
  local copies, waits for them, and re-layouts  7.13 us (11%)
  other arithmetic  3.07 us (5%)
  between operations  0.82 us (1%)
    ppermute x3, waiting for transfers between devices, local(): lax.ppermute(ainv_top, 'row', [(i, (i + 2 * k) % devices) for i in range(...  16.2 us
    ppermute x3, waiting for transfers between devices, swapped(): return lax.ppermute(x, 'row', swap)  9.82 us
    pallas_call x1, Pallas kernels, local(): pl.pallas_call(functools.partial(kernel, pieces=pieces), out_shape=(jax.S...  9.69 us
    unnamed x28, local copies, waits for them, and re-layouts  7.13 us
    ppermute x3, starting transfers between devices, local(): lax.ppermute(ainv_top, 'row', [(i, (i + 2 * k) % devices) for i in range(...  6.92 us
    ppermute x9, starting transfers between devices, crossed(): return lax.ppermute(x, 'col', cores)  5.92 us
    ppermute x9, waiting for transfers between devices, crossed(): return lax.ppermute(x, 'col', cores)  2.18 us
    ppermute x3, starting transfers between devices, swapped(): return lax.ppermute(x, 'row', swap)  1.53 us
  transfers between devices with their start and end apart: 17, of which 5 were waited for; matrix products, arithmetic and copies ran while one was open for 5% of the time, Pallas kernels for 0%

profile of v1, /device:TPU:3, one launch (start us, length us, event | category | flops | bytes accessed | tf_op | source)
XLA Modules:
  0.0 66.7 jit_solution(11322754877514231758)
XLA Ops:
  1.6 1.2 %bitcast_multiply_fusion.refs_4_ = bf16[1024,256]{1,0:T(8,128)(2,1)S(1)} fusion(bf16[1,1024,256]{2,1,0:T(8,128)(2,1)} %param.9, bf16[1024]{0:T(1024)(128)(2,1)S(1)} %bitcast.23), kind=kLoop, calls=%fused_computation.1 | loop fusion | flops 262144 | bytes 1050624 | tf_op jit(solution)/shard_map/mul | solution.py:160
  2.9 1.4 %collective-permute-start.7 = (bf16[1024,256]{1,0:T(8,128)(2,1)S(1)}, bf16[1024,256]{1,0:T(8,128)(2,1)}, u32[]{:S(2)}, u32[]{:S(2)}) collective-permute-start(bf16[1024,256]{1,0:T(8,128)(2,1)S(1)} %bitcast_multiply_fusion.refs_4_), channel_id=1, source_target_pairs={{0,2},{2,0},{4,6},{6,4},{8,10},{10,8},{12,14},{14,12},{1,3},{3,1},... | collective-permute-start | bytes 1572872 | tf_op jit(solution)/shard_map/ppermute | solution.py:150
  4.3 1.2 %collective-permute-start.16 = (bf16[2,1536,256]{2,1,0:T(8,128)(2,1)}, bf16[2,1536,256]{2,1,0:T(8,128)(2,1)}, u32[]{:S(2)}, u32[]{:S(2)}) collective-permute-start(bf16[2,1536,256]{2,1,0:T(8,128)(2,1)} %refs_16_.1), channel_id=1, source_target_pairs={{0,1},{1,0},{2,3},{3,2},{4,5},{5,4},{6,7},{7,6},{8,9},{9,8},{10,11... | collective-permute-start | bytes 4718600 | tf_op jit(solution)/shard_map/ppermute | solution.py:153
  5.5 1.3 %collective-permute-start = (bf16[64,1024]{1,0:T(8,128)(2,1)}, bf16[64,1024]{1,0:T(8,128)(2,1)S(1)}, u32[]{:S(2)}, u32[]{:S(2)}) collective-permute-start(bf16[64,1024]{1,0:T(8,128)(2,1)} %param.8), channel_id=1, source_target_pairs={{0,4},{2,6},{4,8},{6,10},{8,12},{10,14},{12,0},{14,2},{1,5},{3,7},... | collective-permute-start | bytes 393224 | tf_op jit(solution)/shard_map/ppermute | solution.py:167
  6.8 2.0 %collective-permute-start.2 = (bf16[64,1024]{1,0:T(8,128)(2,1)}, bf16[64,1024]{1,0:T(8,128)(2,1)S(1)}, u32[]{:S(2)}, u32[]{:S(2)}) collective-permute-start(bf16[64,1024]{1,0:T(8,128)(2,1)} %param.8), channel_id=1, source_target_pairs={{0,12},{2,14},{4,0},{6,2},{8,4},{10,6},{12,8},{14,10},{1,13},{3,15... | collective-permute-start | bytes 393224 | tf_op jit(solution)/shard_map/ppermute | solution.py:167
  8.8 4.0 %collective-permute-done = bf16[64,1024]{1,0:T(8,128)(2,1)S(1)} collective-permute-done((bf16[64,1024]{1,0:T(8,128)(2,1)}, bf16[64,1024]{1,0:T(8,128)(2,1)S(1)}, u32[]{:S(2)}, u32[]{:S(2)}) %collective-permute-start) | collective-permute-done | bytes 131104 | tf_op jit(solution)/shard_map/ppermute | solution.py:167
  12.8 1.0 %collective-permute-start.11 = (bf16[512,256]{1,0:T(8,128)(2,1)}, bf16[512,256]{1,0:T(8,128)(2,1)S(1)}, u32[]{:S(2)}, u32[]{:S(2)}) collective-permute-start(bf16[512,256]{1,0:T(8,128)(2,1)} %bitcast.17), channel_id=1, source_target_pairs={{0,1},{1,0},{2,3},{3,2},{4,5},{5,4},{6,7},{7,6},{8,9},{9,8},{10,11... | collective-permute-start | bytes 786440 | tf_op jit(solution)/shard_map/ppermute | solution.py:153
  13.8 1.3 %collective-permute-start.14 = (bf16[512,256]{1,0:T(8,128)(2,1)S(1)}, bf16[512,256]{1,0:T(8,128)(2,1)S(1)}, u32[]{:S(2)}, u32[]{:S(2)}) collective-permute-start(bf16[512,256]{1,0:T(8,128)(2,1)S(1)} %collective-permute-done.12.refs_12_), channel_id=1, source_target_pairs={{0,4},{4,8},{6,2},{8,12},{10,6},{14,10},{1,5},{5,9},{7,3},{9,13},{... | collective-permute-start | bytes 786440 | tf_op jit(solution)/shard_map/ppermute | solution.py:178
  15.1 3.6 %collective-permute-start.1 = (bf16[64,1024]{1,0:T(8,128)(2,1)}, bf16[64,1024]{1,0:T(8,128)(2,1)S(1)}, u32[]{:S(2)}, u32[]{:S(2)}) collective-permute-start(bf16[64,1024]{1,0:T(8,128)(2,1)} %param.8), channel_id=1, source_target_pairs={{0,8},{2,10},{4,12},{6,14},{8,0},{10,2},{12,4},{14,6},{1,9},{3,11}... | collective-permute-start | bytes 393224 | tf_op jit(solution)/shard_map/ppermute | solution.py:167
  18.7 12.2 %collective-permute-done.1 = bf16[64,1024]{1,0:T(8,128)(2,1)S(1)} collective-permute-done((bf16[64,1024]{1,0:T(8,128)(2,1)}, bf16[64,1024]{1,0:T(8,128)(2,1)S(1)}, u32[]{:S(2)}, u32[]{:S(2)}) %collective-permute-start.1) | collective-permute-done | bytes 131104 | tf_op jit(solution)/shard_map/ppermute | solution.py:167
  31.5 1.0 %pad_maximum_fusion.refs_0_ = bf16[4,64,1024]{2,1,0:T(8,128)(2,1)S(1)} fusion(bf16[1,64,1024]{2,1,0:T(8,128)(2,1)S(1)} %bitcast.21, bf16[1,64,1024]{2,1,0:T(8,128)(2,1)S(1)} %bitcast.22, bf16[1,64,1024]{2,1,0:T(8,128)(2,1)S(1)} %bitcast.20, bf16[1,64,1024]{2,1,0:T(8,128)(2,1)} %bitcast.19), kind=kLoop, calls=%fused_computation | loop fusion | flops 786432 | bytes 1048576 | tf_op jit(solution)/shard_map/stack | solution.py:169
  33.3 1.3 %collective-permute-start.9 = (bf16[1024,256]{1,0:T(8,128)(2,1)}, bf16[1024,256]{1,0:T(8,128)(2,1)}, u32[]{:S(2)}, u32[]{:S(2)}) collective-permute-start(bf16[1024,256]{1,0:T(8,128)(2,1)} %collective-permute-done.7.refs_6_), channel_id=1, source_target_pairs={{0,4},{4,8},{6,2},{8,12},{10,6},{14,10},{1,5},{5,9},{7,3},{9,13},{... | collective-permute-start | bytes 1572872 | tf_op jit(solution)/shard_map/ppermute | solution.py:177
  35.8 0.8 %copy-done.2 = bf16[1024,256]{1,0:T(8,128)(2,1)} copy-done((bf16[1024,256]{1,0:T(8,128)(2,1)}, bf16[1024,256]{1,0:T(8,128)(2,1)S(1)}, u32[]{:S(2)}) %copy-start.2) | copy-done | bytes 524312
  36.6 9.8 %collective-permute-done.4.refs_2_ = bf16[4,64,1024]{2,1,0:T(8,128)(2,1)} collective-permute-done((bf16[4,64,1024]{2,1,0:T(8,128)(2,1)S(1)}, bf16[4,64,1024]{2,1,0:T(8,128)(2,1)}, u32[]{:S(2)}, u32[]{:S(2)}) %collective-permute-start.4) | collective-permute-done | bytes 524320 | tf_op jit(solution)/shard_map/ppermute | solution.py:150
  46.4 1.3 %collective-permute-start.5 = (bf16[4,64,1024]{2,1,0:T(8,128)(2,1)}, bf16[4,64,1024]{2,1,0:T(8,128)(2,1)}, u32[]{:S(2)}, u32[]{:S(2)}) collective-permute-start(bf16[4,64,1024]{2,1,0:T(8,128)(2,1)} %collective-permute-done.4.refs_2_), channel_id=1, source_target_pairs={{0,1},{1,0},{2,3},{3,2},{4,5},{5,4},{6,7},{7,6},{8,9},{9,8},{10,11... | collective-permute-start | bytes 1572872 | tf_op jit(solution)/shard_map/ppermute | solution.py:153
  47.7 0.9 %collective-permute-done.9.refs_8_ = bf16[1024,256]{1,0:T(8,128)(2,1)} collective-permute-done((bf16[1024,256]{1,0:T(8,128)(2,1)}, bf16[1024,256]{1,0:T(8,128)(2,1)}, u32[]{:S(2)}, u32[]{:S(2)}) %collective-permute-start.9) | collective-permute-done | bytes 524320 | tf_op jit(solution)/shard_map/ppermute | solution.py:177
  48.6 1.3 %collective-permute-start.10 = (bf16[1024,256]{1,0:T(8,128)(2,1)}, bf16[1024,256]{1,0:T(8,128)(2,1)}, u32[]{:S(2)}, u32[]{:S(2)}) collective-permute-start(bf16[1024,256]{1,0:T(8,128)(2,1)} %collective-permute-done.9.refs_8_), channel_id=1, source_target_pairs={{0,1},{1,0},{2,3},{3,2},{4,5},{5,4},{6,7},{7,6},{8,9},{9,8},{10,11... | collective-permute-start | bytes 1572872 | tf_op jit(solution)/shard_map/ppermute | solution.py:153
  49.9 2.2 %collective-permute-done.15.refs_15_ = bf16[512,256]{1,0:T(8,128)(2,1)} collective-permute-done((bf16[512,256]{1,0:T(8,128)(2,1)}, bf16[512,256]{1,0:T(8,128)(2,1)}, u32[]{:S(2)}, u32[]{:S(2)}) %collective-permute-start.15) | collective-permute-done | bytes 262176 | tf_op jit(solution)/shard_map/ppermute | solution.py:153
  52.2 1.0 %copy-done.3 = bf16[1024,256]{1,0:T(8,128)(2,1)S(1)} copy-done((bf16[1024,256]{1,0:T(8,128)(2,1)S(1)}, bf16[1024,256]{1,0:T(8,128)(2,1)}, u32[]{:S(2)}) %copy-start.3) | copy-done | bytes 524312
  53.2 0.9 %copy-done.4 = bf16[1,512,256]{2,1,0:T(8,128)(2,1)S(1)} copy-done((bf16[1,512,256]{2,1,0:T(8,128)(2,1)S(1)}, bf16[1,512,256]{2,1,0:T(8,128)(2,1)}, u32[]{:S(2)}) %copy-start.4) | copy-done | bytes 262168
  54.2 0.9 %copy-done.6 = bf16[512,256]{1,0:T(8,128)(2,1)S(1)} copy-done((bf16[512,256]{1,0:T(8,128)(2,1)S(1)}, bf16[512,256]{1,0:T(8,128)(2,1)}, u32[]{:S(2)}) %copy-start.6) | copy-done | bytes 262168
  55.1 0.9 %copy-done.8 = bf16[512,256]{1,0:T(8,128)(2,1)S(1)} copy-done((bf16[512,256]{1,0:T(8,128)(2,1)S(1)}, bf16[512,256]{1,0:T(8,128)(2,1)}, u32[]{:S(2)}) %copy-start.8) | copy-done | bytes 262168
  56.1 0.9 %copy-done.10 = bf16[512,256]{1,0:T(8,128)(2,1)S(1)} copy-done((bf16[512,256]{1,0:T(8,128)(2,1)S(1)}, bf16[512,256]{1,0:T(8,128)(2,1)}, u32[]{:S(2)}) %copy-start.10) | copy-done | bytes 262168
  57.0 9.7 %shard_map.103 = (bf16[512,256]{1,0:T(8,128)(2,1)}, bf16[2,1536,256]{2,1,0:T(8,128)(2,1)}, bf16[2,512,256]{2,1,0:T(8,128)(2,1)}) custom-call(s32[3]{0:T(128)S(1)} %pad_add_fusion.place_ref, s32[2]{0:T(128)S(1)} %compare_select_fusion.1.slot_ref, s32[2,2]{1,0:T(2,128)S(1)} %copy-done.11, bf16[4,64,1024]{2,1,0:T(8,128)(2,1)S(1)} %pad_maximum_fusion.refs_0_, ...), custom_call_target="tpu_custom_call" | custom-call | tf_op jit(solution)/shard_map/pallas_call | solution.py:188
  (44 shorter events, 3.7 us)
Async XLA Ops:
  0.6 51.5 %copy-start = (bf16[2,1536,256]{2,1,0:T(8,128)(2,1)S(1)}, bf16[2,1536,256]{2,1,0:T(8,128)(2,1)}, u32[]{:S(2)}) copy-start(bf16[2,1536,256]{2,1,0:T(8,128)(2,1)} %refs_16_.1) | copy-start | bytes 4718596
  0.6 49.3 %copy-start.12 = (s32[2]{0:T(128)S(1)}, s32[2]{0:T(128)}, u32[]{:S(2)}) copy-start(s32[2]{0:T(128)} %param.15) | copy-start | bytes 28
  0.7 51.5 %copy-start.11 = (s32[2,2]{1,0:T(2,128)S(1)}, s32[2,2]{1,0:T(2,128)}, u32[]{:S(2)}) copy-start(s32[2,2]{1,0:T(2,128)} %keep_ref.1) | copy-start | bytes 52
  0.7 51.5 %copy-start.1 = (bf16[2,512,256]{2,1,0:T(8,128)(2,1)S(1)}, bf16[2,512,256]{2,1,0:T(8,128)(2,1)}, u32[]{:S(2)}) copy-start(bf16[2,512,256]{2,1,0:T(8,128)(2,1)} %refs_18_.1) | copy-start | bytes 1572868
  0.7 13.2 %collective-permute-start.12 = (bf16[512,256]{1,0:T(8,128)(2,1)}, bf16[512,256]{1,0:T(8,128)(2,1)S(1)}, u32[]{:S(2)}, u32[]{:S(2)}) collective-permute-start(bf16[512,256]{1,0:T(8,128)(2,1)} %bitcast.16), channel_id=1, source_target_pairs={{0,2},{2,0},{4,6},{6,4},{8,10},{10,8},{12,14},{14,12},{1,3},{3,1},... | collective-permute-start | bytes 786440 | tf_op jit(solution)/shard_map/ppermute | solution.py:150
  2.9 30.4 %collective-permute-start.7 = (bf16[1024,256]{1,0:T(8,128)(2,1)S(1)}, bf16[1024,256]{1,0:T(8,128)(2,1)}, u32[]{:S(2)}, u32[]{:S(2)}) collective-permute-start(bf16[1024,256]{1,0:T(8,128)(2,1)S(1)} %bitcast_multiply_fusion.refs_4_), channel_id=1, source_target_pairs={{0,2},{2,0},{4,6},{6,4},{8,10},{10,8},{12,14},{14,12},{1,3},{3,1},... | collective-permute-start | bytes 1572872 | tf_op jit(solution)/shard_map/ppermute | solution.py:150
  4.3 47.9 %collective-permute-start.16 = (bf16[2,1536,256]{2,1,0:T(8,128)(2,1)}, bf16[2,1536,256]{2,1,0:T(8,128)(2,1)}, u32[]{:S(2)}, u32[]{:S(2)}) collective-permute-start(bf16[2,1536,256]{2,1,0:T(8,128)(2,1)} %refs_16_.1), channel_id=1, source_target_pairs={{0,1},{1,0},{2,3},{3,2},{4,5},{5,4},{6,7},{7,6},{8,9},{9,8},{10,11... | collective-permute-start | bytes 4718600 | tf_op jit(solution)/shard_map/ppermute | solution.py:153
  5.5 7.3 %collective-permute-start = (bf16[64,1024]{1,0:T(8,128)(2,1)}, bf16[64,1024]{1,0:T(8,128)(2,1)S(1)}, u32[]{:S(2)}, u32[]{:S(2)}) collective-permute-start(bf16[64,1024]{1,0:T(8,128)(2,1)} %param.8), channel_id=1, source_target_pairs={{0,4},{2,6},{4,8},{6,10},{8,12},{10,14},{12,0},{14,2},{1,5},{3,7},... | collective-permute-start | bytes 393224 | tf_op jit(solution)/shard_map/ppermute | solution.py:167
  6.8 8.3 %collective-permute-start.2 = (bf16[64,1024]{1,0:T(8,128)(2,1)}, bf16[64,1024]{1,0:T(8,128)(2,1)S(1)}, u32[]{:S(2)}, u32[]{:S(2)}) collective-permute-start(bf16[64,1024]{1,0:T(8,128)(2,1)} %param.8), channel_id=1, source_target_pairs={{0,12},{2,14},{4,0},{6,2},{8,4},{10,6},{12,8},{14,10},{1,13},{3,15... | collective-permute-start | bytes 393224 | tf_op jit(solution)/shard_map/ppermute | solution.py:167
  12.8 19.7 %collective-permute-start.11 = (bf16[512,256]{1,0:T(8,128)(2,1)}, bf16[512,256]{1,0:T(8,128)(2,1)S(1)}, u32[]{:S(2)}, u32[]{:S(2)}) collective-permute-start(bf16[512,256]{1,0:T(8,128)(2,1)} %bitcast.17), channel_id=1, source_target_pairs={{0,1},{1,0},{2,3},{3,2},{4,5},{5,4},{6,7},{7,6},{8,9},{9,8},{10,11... | collective-permute-start | bytes 786440 | tf_op jit(solution)/shard_map/ppermute | solution.py:153
  13.8 19.4 %collective-permute-start.14 = (bf16[512,256]{1,0:T(8,128)(2,1)S(1)}, bf16[512,256]{1,0:T(8,128)(2,1)S(1)}, u32[]{:S(2)}, u32[]{:S(2)}) collective-permute-start(bf16[512,256]{1,0:T(8,128)(2,1)S(1)} %collective-permute-done.12.refs_12_), channel_id=1, source_target_pairs={{0,4},{4,8},{6,2},{8,12},{10,6},{14,10},{1,5},{5,9},{7,3},{9,13},{... | collective-permute-start | bytes 786440 | tf_op jit(solution)/shard_map/ppermute | solution.py:178
  15.1 15.8 %collective-permute-start.1 = (bf16[64,1024]{1,0:T(8,128)(2,1)}, bf16[64,1024]{1,0:T(8,128)(2,1)S(1)}, u32[]{:S(2)}, u32[]{:S(2)}) collective-permute-start(bf16[64,1024]{1,0:T(8,128)(2,1)} %param.8), channel_id=1, source_target_pairs={{0,8},{2,10},{4,12},{6,14},{8,0},{10,2},{12,4},{14,6},{1,9},{3,11}... | collective-permute-start | bytes 393224 | tf_op jit(solution)/shard_map/ppermute | solution.py:167
  30.9 3.7 %collective-permute-start.13 = (bf16[512,256]{1,0:T(8,128)(2,1)S(1)}, bf16[512,256]{1,0:T(8,128)(2,1)S(1)}, u32[]{:S(2)}, u32[]{:S(2)}) collective-permute-start(bf16[512,256]{1,0:T(8,128)(2,1)S(1)} %collective-permute-done.12.refs_12_), channel_id=1, source_target_pairs={{0,1},{1,0},{2,3},{3,2},{4,5},{5,4},{6,7},{7,6},{8,9},{9,8},{10,11... | collective-permute-start | bytes 786440 | tf_op jit(solution)/shard_map/ppermute | solution.py:153
  33.2 2.6 %collective-permute-start.6 = (bf16[1024,256]{1,0:T(8,128)(2,1)S(1)}, bf16[1024,256]{1,0:T(8,128)(2,1)S(1)}, u32[]{:S(2)}, u32[]{:S(2)}) collective-permute-start(bf16[1024,256]{1,0:T(8,128)(2,1)S(1)} %bitcast_multiply_fusion.refs_4_), channel_id=1, source_target_pairs={{0,1},{1,0},{2,3},{3,2},{4,5},{5,4},{6,7},{7,6},{8,9},{9,8},{10,11... | collective-permute-start | bytes 1572872 | tf_op jit(solution)/shard_map/ppermute | solution.py:153
  33.2 13.2 %copy-start.7 = (bf16[512,256]{1,0:T(8,128)(2,1)}, bf16[512,256]{1,0:T(8,128)(2,1)S(1)}, u32[]{:S(2)}) copy-start(bf16[512,256]{1,0:T(8,128)(2,1)S(1)} %collective-permute-done.14.refs_14_) | copy-start | bytes 786436
  33.2 13.2 %collective-permute-start.4 = (bf16[4,64,1024]{2,1,0:T(8,128)(2,1)S(1)}, bf16[4,64,1024]{2,1,0:T(8,128)(2,1)}, u32[]{:S(2)}, u32[]{:S(2)}) collective-permute-start(bf16[4,64,1024]{2,1,0:T(8,128)(2,1)S(1)} %pad_maximum_fusion.refs_0_), channel_id=1, source_target_pairs={{0,2},{2,0},{4,6},{6,4},{8,10},{10,8},{12,14},{14,12},{1,3},{3,1},... | collective-permute-start | bytes 1572872 | tf_op jit(solution)/shard_map/ppermute | solution.py:150
  33.3 15.3 %collective-permute-start.9 = (bf16[1024,256]{1,0:T(8,128)(2,1)}, bf16[1024,256]{1,0:T(8,128)(2,1)}, u32[]{:S(2)}, u32[]{:S(2)}) collective-permute-start(bf16[1024,256]{1,0:T(8,128)(2,1)} %collective-permute-done.7.refs_6_), channel_id=1, source_target_pairs={{0,4},{4,8},{6,2},{8,12},{10,6},{14,10},{1,5},{5,9},{7,3},{9,13},{... | collective-permute-start | bytes 1572872 | tf_op jit(solution)/shard_map/ppermute | solution.py:177
  35.3 14.5 %collective-permute-start.3 = (bf16[4,64,1024]{2,1,0:T(8,128)(2,1)S(1)}, bf16[4,64,1024]{2,1,0:T(8,128)(2,1)}, u32[]{:S(2)}, u32[]{:S(2)}) collective-permute-start(bf16[4,64,1024]{2,1,0:T(8,128)(2,1)S(1)} %pad_maximum_fusion.refs_0_), channel_id=1, source_target_pairs={{0,1},{1,0},{2,3},{3,2},{4,5},{5,4},{6,7},{7,6},{8,9},{9,8},{10,11... | collective-permute-start | bytes 1572872 | tf_op jit(solution)/shard_map/ppermute | solution.py:153
  36.5 15.6 %collective-permute-start.8 = (bf16[1024,256]{1,0:T(8,128)(2,1)}, bf16[1024,256]{1,0:T(8,128)(2,1)}, u32[]{:S(2)}, u32[]{:S(2)}) collective-permute-start(bf16[1024,256]{1,0:T(8,128)(2,1)} %collective-permute-done.7.refs_6_), channel_id=1, source_target_pairs={{0,1},{1,0},{2,3},{3,2},{4,5},{5,4},{6,7},{7,6},{8,9},{9,8},{10,11... | collective-permute-start | bytes 1572872 | tf_op jit(solution)/shard_map/ppermute | solution.py:153
  46.4 5.7 %collective-permute-start.5 = (bf16[4,64,1024]{2,1,0:T(8,128)(2,1)}, bf16[4,64,1024]{2,1,0:T(8,128)(2,1)}, u32[]{:S(2)}, u32[]{:S(2)}) collective-permute-start(bf16[4,64,1024]{2,1,0:T(8,128)(2,1)} %collective-permute-done.4.refs_2_), channel_id=1, source_target_pairs={{0,1},{1,0},{2,3},{3,2},{4,5},{5,4},{6,7},{7,6},{8,9},{9,8},{10,11... | collective-permute-start | bytes 1572872 | tf_op jit(solution)/shard_map/ppermute | solution.py:153
  48.6 3.5 %collective-permute-start.10 = (bf16[1024,256]{1,0:T(8,128)(2,1)}, bf16[1024,256]{1,0:T(8,128)(2,1)}, u32[]{:S(2)}, u32[]{:S(2)}) collective-permute-start(bf16[1024,256]{1,0:T(8,128)(2,1)} %collective-permute-done.9.refs_8_), channel_id=1, source_target_pairs={{0,1},{1,0},{2,3},{3,2},{4,5},{5,4},{6,7},{7,6},{8,9},{9,8},{10,11... | collective-permute-start | bytes 1572872 | tf_op jit(solution)/shard_map/ppermute | solution.py:153
  49.9 2.3 %collective-permute-start.15 = (bf16[512,256]{1,0:T(8,128)(2,1)}, bf16[512,256]{1,0:T(8,128)(2,1)}, u32[]{:S(2)}, u32[]{:S(2)}) collective-permute-start(bf16[512,256]{1,0:T(8,128)(2,1)} %copy-done.7), channel_id=1, source_target_pairs={{0,1},{1,0},{2,3},{3,2},{4,5},{5,4},{6,7},{7,6},{8,9},{9,8},{10,11... | collective-permute-start | bytes 786440 | tf_op jit(solution)/shard_map/ppermute | solution.py:153
  52.2 1.0 %copy-start.3 = (bf16[1024,256]{1,0:T(8,128)(2,1)S(1)}, bf16[1024,256]{1,0:T(8,128)(2,1)}, u32[]{:S(2)}) copy-start(bf16[1024,256]{1,0:T(8,128)(2,1)} %copy-done.2) | copy-start | bytes 1572868
  53.2 0.9 %copy-start.4 = (bf16[1,512,256]{2,1,0:T(8,128)(2,1)S(1)}, bf16[1,512,256]{2,1,0:T(8,128)(2,1)}, u32[]{:S(2)}) copy-start(bf16[1,512,256]{2,1,0:T(8,128)(2,1)} %param.10) | copy-start | bytes 786436
  (6 other events, 5.1 us)

commit v2 on v0

v2 whole, which is shorter than its diff:
```python
import jax
import jax.numpy as jnp
from jax import lax
from jax.experimental import pallas as pl
from jax.experimental.pallas import tpu as pltpu
from jax.sharding import PartitionSpec as P

DIRECT = 4
F32 = jnp.float32
BF16 = jnp.bfloat16
SEQUENCES = (
    (1, (
        "swapped 0",
        "swapped 1",
    )),
    (1, (
        "swapped 0",
        "far",
    )),
    (1, (
        "swapped 0",
        "a 2",
    )),
)


def dot(a, b):
    return jnp.dot(a, b, preferred_element_type=F32)


def dot_t(a, b):
    return lax.dot_general(a, b, (((0,), (0,)), ((), ())), preferred_element_type=F32)


class Loads:
    def __init__(self, sem):
        self.sem, self.used = sem, 0

    def start(self, src, dst):
        copy = pltpu.make_async_copy(src, dst, self.sem.at[self.used])
        self.used += 1
        copy.start()
        return copy

    def choose(self, which, srcs, dst):
        sem = self.sem.at[self.used]
        self.used += 1
        for k, src in enumerate(srcs):

            @pl.when(which == k)
            def _(src=src):
                pltpu.make_async_copy(src, dst, sem).start()

        return pltpu.make_async_copy(srcs[0], dst, sem)


def wait(copies):
    for copy in copies:
        copy.wait()


def pack_kernel(keep_ref, factor, inverse, *refs):
    parts, whole, sem = refs[:-2], refs[-2], refs[-1]
    width = inverse.shape[0]
    share = width // len(parts)
    loads = Loads(sem)
    copies = [
        (
            loads.start(factor.at[pl.ds(i * width, width)], part.at[pl.ds(0, width)]),
            loads.start(inverse.at[pl.ds(i * share, share)], part.at[pl.ds(width, share)]),
        )
        for i, part in enumerate(parts)
    ]
    for i, part in enumerate(parts):
        wait(copies[i])

        @pl.when(keep_ref[0, i] == 0)
        def _(part=part):
            part[pl.ds(0, width), :] = jnp.zeros((width, part.shape[1]), part.dtype)

        whole[i] = part[...]


def copy_top(place_ref, near, near_o, far, far_o, a):
    planes, block = near.shape[:2]
    span = 2 * block
    me, pair = place_ref[0], place_ref[2]
    for k in range(planes):
        plane = lax.rem(place_ref[1] + planes - k, planes)
        for ref, core in ((near, me), (near_o, 1 - me)):
            row = pl.multiple_of(((plane * 2 + pair) * 2 + core) * block, block)
            a[pl.ds(row, block), :] = ref[k]
        for ref, core in ((far, me), (far_o, 1 - me)):
            row = pl.multiple_of(((plane * 2 + 1 - pair) * 2 + core) * block, block)
            for j in range(planes):
                col = pl.multiple_of((2 * j + 1 - pair) * span, span)
                a[pl.ds(row, block), pl.ds(col, span)] = ref[k, :, j * span : (j + 1) * span]
    for i in range(planes):
        for j in range(planes):
            mine = pl.multiple_of((2 * i + pair) * span, span)
            theirs = pl.multiple_of((2 * j + 1 - pair) * span, span)
            a[pl.ds(theirs, span), pl.ds(mine, span)] = a[pl.ds(mine, span), pl.ds(theirs, span)].T


def sides_of(place_ref, half):
    mine = pl.multiple_of(place_ref[0] * half, half)
    other = pl.multiple_of((1 - place_ref[0]) * half, half)
    return pl.ds(mine, half), pl.ds(other, half)


def parent_kernel(place_ref, *refs):
    own, own_o, dp, pd, a, g = refs[-6:]
    width, half = dp.shape
    parts = own.shape[0]
    if len(refs) == 10:
        copy_top(place_ref, *refs[:4], a)
    else:
        a[...] = refs[0][...]
    head = pl.ds(0, width)
    total = dot(a[:, :width], own[0, head, :])
    for j in range(1, parts):
        total += dot(a[:, j * width : (j + 1) * width], own[j, head, :])
    g[...] = total.astype(BF16)
    for r, at in zip((own, own_o), sides_of(place_ref, half)):
        y = dp[at, :].astype(F32)
        for j in range(parts):
            y += dot_t(r[j, head, :], g[j * width : (j + 1) * width, :])
        pd[at, :] = y.astype(BF16)


def child_kernel(place_ref, slot_ref, keep_ref, a, lc, lc_o, dc, own, own_o, *refs):
    parts = own.shape[0]
    swapped, beyond, refs = refs[:parts], refs[parts : 2 * parts], refs[2 * parts :]
    swapped_o, beyond_o, cc_out, cd_out, x, v, t, cc, cd, sem = refs
    children, _, half = lc.shape
    width = 2 * half
    tops = a.shape[0]
    head, below, tail = pl.ds(0, width), pl.ds(width, tops), pl.ds(width, half)
    ends = sides_of(place_ref, half)
    holds = (place_ref[0], 1 - place_ref[0])
    loads = Loads(sem)
    chosen, outs = [], []
    for k in range(children):
        chosen.append([])
        for j in range(parts):
            for i, srcs in enumerate(
                (
                    (own.at[j], swapped[j], beyond[j]),
                    (own_o.at[j], swapped_o.at[j], beyond_o.at[j]),
                )
            ):
                chosen[k].append(loads.choose(slot_ref[k], srcs, x.at[k, i, j]))
    for k in range(children):
        wait(chosen[k])
        for j in range(parts):
            rows = pl.ds(j * width, width)
            w = lc[k, pl.ds(width + j * width, width), :].astype(F32)
            part = dot(x[k, 0, j, head, :], lc[k, ends[0], :])
            part += dot(x[k, 1, j, head, :], lc[k, ends[1], :])
            v[k, rows, :] = (part - jnp.where(keep_ref[k, j] > 0, w, 0.0)).astype(BF16)
    for k in range(children):
        t[k] = dot(a[...], v[k]).astype(BF16)
    for k in range(children):
        for i in range(2):
            y = dot(x[k, 0, holds[i], tail, :], lc[k, ends[0], :])
            y += dot(x[k, 1, holds[i], tail, :], lc[k, ends[1], :])
            for j in range(parts):
                y += dot_t(x[k, i, j, head, :], t[k, j * width : (j + 1) * width, :])
            cc[k, ends[i], :] = (-y).astype(BF16)
        outs.append(loads.start(cc.at[k], cc_out.at[k, head]))
        for j in range(parts):

            @pl.when(keep_ref[k, j] == 0)
            def _(k=k, j=j):
                t[k, pl.ds(j * width, width), :] = jnp.zeros((width, half), BF16)

        outs.append(loads.start(t.at[k], cc_out.at[k, below]))
    for k in range(children):
        for i, r in enumerate((lc, lc_o)):
            y = dot_t(r[k, below, :], t[k]) + dot_t(r[k, head, :], cc[k])
            cd[k, ends[i], :] = (dc[k, ends[i], :].astype(F32) - y).astype(BF16)
        outs.append(loads.start(cd.at[k], cd_out.at[k]))
    wait(outs)


def local(ainv_top, l_parent, dinv_parent, keep_parent, l_child, dinv_child, keep_child, parent_of):
    devices = lax.axis_size("row")
    planes = devices // 2
    row = lax.axis_index("row")
    swap = [(i, i ^ 1) for i in range(devices)]
    onward = [(i, i - 2 if i % 2 else i + 2) for i in range(devices)]
    onward = [(i, j) for i, j in onward if 0 <= j < devices]
    cores = [(0, 1), (1, 0)]
    half = l_parent.shape[2]
    width = 2 * half
    tops = l_parent.shape[1]
    parts = tops // width
    rows = width + width // parts
    children = l_child.shape[0]
    direct = planes <= DIRECT
    smem = pl.BlockSpec(memory_space=pltpu.SMEM)
    vmem = pl.BlockSpec(memory_space=pltpu.VMEM)
    hbm = pl.BlockSpec(memory_space=pl.ANY)
    packed = jax.ShapeDtypeStruct((rows, half), BF16)
    *own, whole = pl.pallas_call(
        pack_kernel,
        out_shape=(packed,) * parts + (jax.ShapeDtypeStruct((parts, rows, half), BF16),),
        in_specs=[smem] + [hbm] * 2,
        out_specs=(vmem,) * (parts + 1),
        scratch_shapes=[pltpu.SemaphoreType.DMA((2 * parts,))],
        compiler_params=pltpu.CompilerParams(vmem_limit_bytes=60 << 20),
    )(keep_parent, l_parent[0], dinv_parent[0])
    ainv_top, *own = lax.optimization_barrier((ainv_top, *own))
    got = {"own": whole, "c": l_child, "a": ainv_top}
    got.update((f"own {j}", own[j]) for j in range(parts))

    moves = {}
    for j in range(parts):
        moves[f"swapped {j}"] = (f"own {j}", "row", swap)
        moves[f"beyond {j}"] = (f"swapped {j}", "row", onward)
    for name in ("own", "c", "swapped", "beyond"):
        moves[name + " other"] = (name, "col", cores)
    if direct:
        for k in range(1, planes):
            moves[f"a {k}"] = ("a", "row", [(i, (i + 2 * k) % devices) for i in range(devices)])
        moves["far"] = ("sides", "row", swap)
        moves["near other"] = ("near", "col", cores)
        moves["far other"] = ("far", "col", cores)

    def value(name):
        if name in got:
            return got[name]
        if name in ("swapped", "beyond"):
            got[name] = jnp.stack([value(f"{name} {j}") for j in range(parts)])
        elif name in ("near", "sides"):
            near = jnp.stack([got["a"], *(value(f"a {k}") for k in range(1, planes))])
            sides = near.reshape(planes, near.shape[1], planes, 2, -1)
            sides = jnp.where(row % 2 == 0, sides[:, :, :, 0], sides[:, :, :, 1])
            got["near"] = near
            got["sides"] = sides.reshape(planes, near.shape[1], -1)
        else:
            source, axis, pairs = moves[name]
            got[name] = lax.ppermute(value(source), axis, pairs)
        return got[name]

    for window, sequence in SEQUENCES:
        sequence = [name for name in sequence if name in moves]
        for i, name in enumerate(sequence):
            if name in got:
                continue
            source, axis, pairs = moves[name]
            sent = value(source)
            if i >= window:
                sent = lax.optimization_barrier((sent, value(sequence[i - window])))[0]
            got[name] = lax.ppermute(sent, axis, pairs)
    if direct:
        top = [value(name) for name in ("near", "near other", "far", "far other")]
    else:
        top = [lax.all_gather(ainv_top, ("row", "col"), axis=0, tiled=True)]
    place = jnp.stack([lax.axis_index("col"), row // 2, row % 2]).astype(jnp.int32)
    slot = jnp.where(parent_of == row, 0, jnp.where(parent_of == row ^ 1, 1, 2)).astype(jnp.int32)
    parent_diag, full = pl.pallas_call(
        parent_kernel,
        out_shape=(
            jax.ShapeDtypeStruct((width, half), BF16),
            jax.ShapeDtypeStruct((tops, tops), BF16),
        ),
        in_specs=[smem] + [vmem] * (len(top) + 3),
        out_specs=(vmem,) * 2,
        scratch_shapes=[pltpu.VMEM((tops, half), BF16)],
        compiler_params=pltpu.CompilerParams(vmem_limit_bytes=12 << 20),
        cost_estimate=pl.CostEstimate(
            flops=2 * tops * half * (tops + width), bytes_accessed=1 << 20, transcendentals=0
        ),
    )(place, *top, whole, value("own other"), dinv_parent[0])
    sent = [value(f"{name} {j}") for name in ("swapped", "beyond") for j in range(parts)]
    sent += [value("swapped other"), value("beyond other")]
    child_column, child_diag = pl.pallas_call(
        child_kernel,
        out_shape=(
            jax.ShapeDtypeStruct(l_child.shape, BF16),
            jax.ShapeDtypeStruct(dinv_child.shape, BF16),
        ),
        in_specs=[smem] * 3 + [vmem] * 4 + [hbm] * (len(sent) + 2),
        out_specs=(hbm,) * 2,
        scratch_shapes=[
            pltpu.VMEM((children, 2, parts, rows, half), BF16),
            pltpu.VMEM((children, tops, half), BF16),
            pltpu.VMEM((children, tops, half), BF16),
            pltpu.VMEM((children, width, half), BF16),
            pltpu.VMEM((children, width, half), BF16),
            pltpu.SemaphoreType.DMA((24,)),
        ],
        compiler_params=pltpu.CompilerParams(vmem_limit_bytes=20 << 20),
    )(
        place, slot, keep_child, full, l_child, value("c other"), dinv_child,
        whole, value("own other"), *sent,
    )
    return parent_diag[None], child_column, child_diag


def solution(mesh):
    blocks = P(("poles", "row"), None, "col")
    placed = (
        P(("poles", "row", "col"), None),
        blocks,
        blocks,
        P(("poles", "row"), None),
        blocks,
        blocks,
        P(("poles", "row"), None),
        P(("poles", "row")),
    )
    return jax.shard_map(
        local, mesh=mesh, in_specs=placed, out_specs=(blocks,) * 3, check_vma=False
    )
```

time: 173 us -> 60.3 us (0.35)
  the two profiles are of different devices: /device:TPU:3 before, /device:TPU:0 now
where the time goes in v2:
time: 60.3 us; the launch traced here: 60.1 us
  waiting for transfers between devices  20.6 us (34%)
  starting transfers between devices  17.5 us (29%)
  Pallas kernels  15.6 us (26%)
  other arithmetic  3.19 us (5%)
  local copies, waits for them, and re-layouts  2.25 us (4%)
  between operations  0.84 us (1%)
    ppermute x11, starting transfers between devices, value(): got[name] = lax.ppermute(value(source), axis, pairs)  14.4 us
    ppermute x11, waiting for transfers between devices, value(): got[name] = lax.ppermute(value(source), axis, pairs)  14.1 us
    pallas_call x1, Pallas kernels, local(): pl.pallas_call(child_kernel, out_shape=(jax.ShapeDtypeStruct(l_child.shap...  8.05 us
    ppermute x3, waiting for transfers between devices, local(): got[name] = lax.ppermute(sent, axis, pairs)  6.55 us
    pallas_call x1, Pallas kernels, local(): pl.pallas_call(parent_kernel, out_shape=(jax.ShapeDtypeStruct((width, hal...  4.62 us
    ppermute x3, starting transfers between devices, local(): got[name] = lax.ppermute(sent, axis, pairs)  3.12 us
    pallas_call x1, Pallas kernels, local(): pl.pallas_call(pack_kernel, out_shape=(packed,) * parts + (jax.ShapeDtype...  2.96 us
    another operation x2, other arithmetic, value(): got[name] = jnp.stack([value(f'{name} {j}') for j in range(parts)])  2.9 us
  transfers between devices with their start and end apart: 14, of which 6 were waited for; matrix products, arithmetic and copies ran while one was open for 9% of the time, Pallas kernels for 8%

profile of v2, /device:TPU:0, one launch (start us, length us, event | category | flops | bytes accessed | tf_op | source)
XLA Modules:
  0.0 60.1 jit_solution(8957195341460864538)
XLA Ops:
  0.6 3.0 %shard_map.103 = (bf16[768,256]{1,0:T(8,128)(2,1)}, bf16[768,256]{1,0:T(8,128)(2,1)}, bf16[2,768,256]{2,1,0:T(8,128)(2,1)}) custom-call(s32[1,2]{1,0:T(1,128)} %keep_ref.2, bf16[1024,256]{1,0:T(8,128)(2,1)} %bitcast.21, bf16[512,256]{1,0:T(8,128)(2,1)} %bitcast.19), custom_call_target="tpu_custom_call" | custom-call | tf_op jit(solution)/shard_map/pallas_call | solution.py:205
  3.6 5.1 %collective-permute-start.2 = (bf16[64,1024]{1,0:T(8,128)(2,1)}, bf16[64,1024]{1,0:T(8,128)(2,1)S(1)}, u32[]{:S(2)}, u32[]{:S(2)}) collective-permute-start(bf16[64,1024]{1,0:T(8,128)(2,1)} %param.8), channel_id=1, source_target_pairs={{0,12},{2,14},{4,0},{6,2},{8,4},{10,6},{12,8},{14,10},{1,13},{3,15... | collective-permute-start | bytes 393224 | tf_op jit(solution)/shard_map/ppermute | solution.py:243
  8.7 1.0 %collective-permute-start = (bf16[64,1024]{1,0:T(8,128)(2,1)}, bf16[64,1024]{1,0:T(8,128)(2,1)S(1)}, u32[]{:S(2)}, u32[]{:S(2)}) collective-permute-start(bf16[64,1024]{1,0:T(8,128)(2,1)} %param.8), channel_id=1, source_target_pairs={{0,4},{2,6},{4,8},{6,10},{8,12},{10,14},{12,0},{14,2},{1,5},{3,7},... | collective-permute-start | bytes 393224 | tf_op jit(solution)/shard_map/ppermute | solution.py:243
  9.7 1.5 %collective-permute-start.4 = (bf16[768,256]{1,0:T(8,128)(2,1)}, bf16[768,256]{1,0:T(8,128)(2,1)S(1)}, u32[]{:S(2)}, u32[]{:S(2)}) collective-permute-start(bf16[768,256]{1,0:T(8,128)(2,1)} %get-tuple-element.18), channel_id=1, source_target_pairs={{0,2},{2,0},{4,6},{6,4},{8,10},{10,8},{12,14},{14,12},{1,3},{3,1},... | collective-permute-start | bytes 1179656 | tf_op jit(solution)/shard_map/ppermute | solution.py:255
  11.2 1.0 %stack.64 = bf16[1,64,4,2,128]{4,3,2,1,0:T(2,128)(2,1)S(1)} reshape(bf16[64,1024]{1,0:T(8,128)(2,1)} %param.8) | data formatting | bytes 262144 | tf_op jit(solution)/shard_map/stack | solution.py:236
  12.3 0.7 %collective-permute-done.2 = bf16[64,1024]{1,0:T(8,128)(2,1)S(1)} collective-permute-done((bf16[64,1024]{1,0:T(8,128)(2,1)}, bf16[64,1024]{1,0:T(8,128)(2,1)S(1)}, u32[]{:S(2)}, u32[]{:S(2)}) %collective-permute-start.2) | collective-permute-done | bytes 131104 | tf_op jit(solution)/shard_map/ppermute | solution.py:243
  13.0 7.1 %collective-permute-done.1 = bf16[64,1024]{1,0:T(8,128)(2,1)S(1)} collective-permute-done((bf16[64,1024]{1,0:T(8,128)(2,1)}, bf16[64,1024]{1,0:T(8,128)(2,1)S(1)}, u32[]{:S(2)}, u32[]{:S(2)}) %collective-permute-start.1) | collective-permute-done | bytes 131104 | tf_op jit(solution)/shard_map/ppermute | solution.py:243
  20.2 0.1 stack.65
  20.4 1.6 %collective-permute-start.9 = (bf16[768,256]{1,0:T(8,128)(2,1)S(1)}, bf16[768,256]{1,0:T(8,128)(2,1)S(1)}, u32[]{:S(2)}, u32[]{:S(2)}) collective-permute-start(bf16[768,256]{1,0:T(8,128)(2,1)S(1)} %copy-done.7), channel_id=1, source_target_pairs={{0,2},{2,0},{4,6},{6,4},{8,10},{10,8},{12,14},{14,12},{1,3},{3,1},... | collective-permute-start | bytes 1179656 | tf_op jit(solution)/shard_map/ppermute | solution.py:255
  22.0 3.9 %collective-permute-start.10 = (bf16[768,256]{1,0:T(8,128)(2,1)S(1)}, bf16[768,256]{1,0:T(8,128)(2,1)S(1)}, u32[]{:S(2)}, u32[]{:S(2)}) collective-permute-start(bf16[768,256]{1,0:T(8,128)(2,1)S(1)} %collective-permute-done.4.refs_0_), channel_id=1, source_target_pairs={{0,4},{4,8},{6,2},{8,12},{10,6},{14,10},{1,5},{5,9},{7,3},{9,13},{... | collective-permute-start | bytes 1179656 | tf_op jit(solution)/shard_map/ppermute | solution.py:243
  26.0 4.8 %collective-permute-done.9.refs_1_ = bf16[768,256]{1,0:T(8,128)(2,1)S(1)} collective-permute-done((bf16[768,256]{1,0:T(8,128)(2,1)S(1)}, bf16[768,256]{1,0:T(8,128)(2,1)S(1)}, u32[]{:S(2)}, u32[]{:S(2)}) %collective-permute-start.9) | collective-permute-done | bytes 393248 | tf_op jit(solution)/shard_map/ppermute | solution.py:255
  30.8 3.4 %collective-permute-start.11 = (bf16[768,256]{1,0:T(8,128)(2,1)S(1)}, bf16[768,256]{1,0:T(8,128)(2,1)}, u32[]{:S(2)}, u32[]{:S(2)}) collective-permute-start(bf16[768,256]{1,0:T(8,128)(2,1)S(1)} %collective-permute-done.9.refs_1_), channel_id=1, source_target_pairs={{0,4},{4,8},{6,2},{8,12},{10,6},{14,10},{1,5},{5,9},{7,3},{9,13},{... | collective-permute-start | bytes 1179656 | tf_op jit(solution)/shard_map/ppermute | solution.py:243
  34.2 0.1 slice_select_fusion
  34.3 0.8 %select_n.37 = bf16[4,64,512]{2,1,0:T(8,128)(2,1)} reshape(bf16[4,64,4,1,128]{4,2,1,0,3:T(4,128)(2,1)S(1)} %slice_select_fusion) | data formatting | bytes 524288 | tf_op jit(solution)/shard_map/jit(_where)/select_n | solution.py:238
  35.4 1.0 %pad_maximum_fusion = bf16[2,768,256]{2,1,0:T(8,128)(2,1)} fusion(bf16[1,768,256]{2,1,0:T(8,128)(2,1)S(1)} %bitcast.17, bf16[1,768,256]{2,1,0:T(8,128)(2,1)S(1)} %bitcast.16), kind=kLoop, calls=%fused_computation | loop fusion | flops 393216 | bytes 1572864 | tf_op jit(solution)/shard_map/stack | solution.py:234
  36.4 0.4 collective-permute-start.7
  36.8 3.9 %collective-permute-done.11.refs_3_ = bf16[768,256]{1,0:T(8,128)(2,1)} collective-permute-done((bf16[768,256]{1,0:T(8,128)(2,1)S(1)}, bf16[768,256]{1,0:T(8,128)(2,1)}, u32[]{:S(2)}, u32[]{:S(2)}) %collective-permute-start.11) | collective-permute-done | bytes 393248 | tf_op jit(solution)/shard_map/ppermute | solution.py:243
  40.7 1.9 %pad_maximum_fusion.1 = bf16[2,768,256]{2,1,0:T(8,128)(2,1)} fusion(bf16[1,768,256]{2,1,0:T(8,128)(2,1)} %bitcast.13, bf16[1,768,256]{2,1,0:T(8,128)(2,1)S(1)} %bitcast.18), kind=kLoop, calls=%fused_computation.1 | loop fusion | flops 393216 | bytes 1572864 | tf_op jit(solution)/shard_map/stack | solution.py:234
  42.6 1.7 %collective-permute-done.5.refs_2_ = bf16[4,64,512]{2,1,0:T(8,128)(2,1)} collective-permute-done((bf16[4,64,512]{2,1,0:T(8,128)(2,1)}, bf16[4,64,512]{2,1,0:T(8,128)(2,1)}, u32[]{:S(2)}, u32[]{:S(2)}) %collective-permute-start.5) | collective-permute-done | bytes 262176 | tf_op jit(solution)/shard_map/ppermute | solution.py:255
  44.4 0.5 collective-permute-start.6
  44.9 0.1 pad_add_fusion.place_ref
  45.0 2.4 %collective-permute-done.6.refs_3_ = bf16[4,64,512]{2,1,0:T(8,128)(2,1)} collective-permute-done((bf16[4,64,512]{2,1,0:T(8,128)(2,1)}, bf16[4,64,512]{2,1,0:T(8,128)(2,1)}, u32[]{:S(2)}, u32[]{:S(2)}) %collective-permute-start.6) | collective-permute-done | bytes 262176 | tf_op jit(solution)/shard_map/ppermute | solution.py:243
  47.4 4.6 %shard_map.104 = (bf16[512,256]{1,0:T(8,128)(2,1)}, bf16[1024,1024]{1,0:T(8,128)(2,1)S(1)}) custom-call(s32[3]{0:T(128)S(1)} %pad_add_fusion.place_ref, bf16[4,64,1024]{2,1,0:T(8,128)(2,1)S(1)} %pad_maximum_fusion.2.refs_0_, bf16[4,64,1024]{2,1,0:T(8,128)(2,1)} %collective-permute-done.3.refs_1_, bf16[4,64,512]{2,1,0:T(8,128)(2,1)} %collective-permute-done.5.refs_2_, ...), custom_call_target="tpu_custom_call" | custom-call | flops 805306368 | bytes 1048576 | tf_op jit(solution)/shard_map/pallas_call | solution.py:262
  52.0 8.1 %shard_map.105 = (bf16[2,1536,256]{2,1,0:T(8,128)(2,1)}, bf16[2,512,256]{2,1,0:T(8,128)(2,1)}) custom-call(s32[3]{0:T(128)S(1)} %pad_add_fusion.place_ref, s32[2]{0:T(128)S(1)} %compare_select_fusion.1.slot_ref, s32[2,2]{1,0:T(2,128)S(1)} %copy-done.4, bf16[1024,1024]{1,0:T(8,128)(2,1)S(1)} %get-tuple-element.22.a, bf16[2,1536,256]{2,1,0:T(8,128)(2,1)S(1)} %copy-done.1, ...), custom_call_target="tpu_custom_call" | custom-call | tf_op jit(solution)/shard_map/pallas_call | solution.py:278
  (38 shorter events, 0.6 us)
Async XLA Ops:
  3.6 16.8 %copy-start.7 = (bf16[768,256]{1,0:T(8,128)(2,1)S(1)}, bf16[768,256]{1,0:T(8,128)(2,1)}, u32[]{:S(2)}) copy-start(bf16[768,256]{1,0:T(8,128)(2,1)} %get-tuple-element.24) | copy-start | bytes 1179652
  3.6 9.3 %collective-permute-start.2 = (bf16[64,1024]{1,0:T(8,128)(2,1)}, bf16[64,1024]{1,0:T(8,128)(2,1)S(1)}, u32[]{:S(2)}, u32[]{:S(2)}) collective-permute-start(bf16[64,1024]{1,0:T(8,128)(2,1)} %param.8), channel_id=1, source_target_pairs={{0,12},{2,14},{4,0},{6,2},{8,4},{10,6},{12,8},{14,10},{1,13},{3,15... | collective-permute-start | bytes 393224 | tf_op jit(solution)/shard_map/ppermute | solution.py:243
  8.7 11.4 %collective-permute-start.1 = (bf16[64,1024]{1,0:T(8,128)(2,1)}, bf16[64,1024]{1,0:T(8,128)(2,1)S(1)}, u32[]{:S(2)}, u32[]{:S(2)}) collective-permute-start(bf16[64,1024]{1,0:T(8,128)(2,1)} %param.8), channel_id=1, source_target_pairs={{0,8},{2,10},{4,12},{6,14},{8,0},{10,2},{12,4},{14,6},{1,9},{3,11}... | collective-permute-start | bytes 393224 | tf_op jit(solution)/shard_map/ppermute | solution.py:243
  8.7 11.5 %collective-permute-start = (bf16[64,1024]{1,0:T(8,128)(2,1)}, bf16[64,1024]{1,0:T(8,128)(2,1)S(1)}, u32[]{:S(2)}, u32[]{:S(2)}) collective-permute-start(bf16[64,1024]{1,0:T(8,128)(2,1)} %param.8), channel_id=1, source_target_pairs={{0,4},{2,6},{4,8},{6,10},{8,12},{10,14},{12,0},{14,2},{1,5},{3,7},... | collective-permute-start | bytes 393224 | tf_op jit(solution)/shard_map/ppermute | solution.py:243
  9.7 10.6 %collective-permute-start.4 = (bf16[768,256]{1,0:T(8,128)(2,1)}, bf16[768,256]{1,0:T(8,128)(2,1)S(1)}, u32[]{:S(2)}, u32[]{:S(2)}) collective-permute-start(bf16[768,256]{1,0:T(8,128)(2,1)} %get-tuple-element.18), channel_id=1, source_target_pairs={{0,2},{2,0},{4,6},{6,4},{8,10},{10,8},{12,14},{14,12},{1,3},{3,1},... | collective-permute-start | bytes 1179656 | tf_op jit(solution)/shard_map/ppermute | solution.py:255
  11.2 40.8 %collective-permute-start.8 = (bf16[2,1536,256]{2,1,0:T(8,128)(2,1)}, bf16[2,1536,256]{2,1,0:T(8,128)(2,1)}, u32[]{:S(2)}, u32[]{:S(2)}) collective-permute-start(bf16[2,1536,256]{2,1,0:T(8,128)(2,1)} %lc.1), channel_id=1, source_target_pairs={{0,1},{1,0},{2,3},{3,2},{4,5},{5,4},{6,7},{7,6},{8,9},{9,8},{10,11... | collective-permute-start | bytes 4718600 | tf_op jit(solution)/shard_map/ppermute | solution.py:243
  12.2 22.9 %copy-start.5 = (bf16[64,1024]{1,0:T(8,128)(2,1)S(1)}, bf16[64,1024]{1,0:T(8,128)(2,1)}, u32[]{:S(2)}) copy-start(bf16[64,1024]{1,0:T(8,128)(2,1)} %param.8) | copy-start | bytes 393220
  20.4 10.4 %collective-permute-start.9 = (bf16[768,256]{1,0:T(8,128)(2,1)S(1)}, bf16[768,256]{1,0:T(8,128)(2,1)S(1)}, u32[]{:S(2)}, u32[]{:S(2)}) collective-permute-start(bf16[768,256]{1,0:T(8,128)(2,1)S(1)} %copy-done.7), channel_id=1, source_target_pairs={{0,2},{2,0},{4,6},{6,4},{8,10},{10,8},{12,14},{14,12},{1,3},{3,1},... | collective-permute-start | bytes 1179656 | tf_op jit(solution)/shard_map/ppermute | solution.py:255
  22.0 14.3 %collective-permute-start.10 = (bf16[768,256]{1,0:T(8,128)(2,1)S(1)}, bf16[768,256]{1,0:T(8,128)(2,1)S(1)}, u32[]{:S(2)}, u32[]{:S(2)}) collective-permute-start(bf16[768,256]{1,0:T(8,128)(2,1)S(1)} %collective-permute-done.4.refs_0_), channel_id=1, source_target_pairs={{0,4},{4,8},{6,2},{8,12},{10,6},{14,10},{1,5},{5,9},{7,3},{9,13},{... | collective-permute-start | bytes 1179656 | tf_op jit(solution)/shard_map/ppermute | solution.py:243
  30.8 9.9 %collective-permute-start.11 = (bf16[768,256]{1,0:T(8,128)(2,1)S(1)}, bf16[768,256]{1,0:T(8,128)(2,1)}, u32[]{:S(2)}, u32[]{:S(2)}) collective-permute-start(bf16[768,256]{1,0:T(8,128)(2,1)S(1)} %collective-permute-done.9.refs_1_), channel_id=1, source_target_pairs={{0,4},{4,8},{6,2},{8,12},{10,6},{14,10},{1,5},{5,9},{7,3},{9,13},{... | collective-permute-start | bytes 1179656 | tf_op jit(solution)/shard_map/ppermute | solution.py:243
  34.3 2.0 %copy-start = (bf16[2,768,256]{2,1,0:T(8,128)(2,1)S(1)}, bf16[2,768,256]{2,1,0:T(8,128)(2,1)}, u32[]{:S(2)}) copy-start(bf16[2,768,256]{2,1,0:T(8,128)(2,1)} %get-tuple-element.20.refs_4_.own) | copy-start | bytes 2359300
  35.2 9.1 %collective-permute-start.3 = (bf16[4,64,1024]{2,1,0:T(8,128)(2,1)S(1)}, bf16[4,64,1024]{2,1,0:T(8,128)(2,1)}, u32[]{:S(2)}, u32[]{:S(2)}) collective-permute-start(bf16[4,64,1024]{2,1,0:T(8,128)(2,1)S(1)} %pad_maximum_fusion.2.refs_0_), channel_id=1, source_target_pairs={{0,1},{1,0},{2,3},{3,2},{4,5},{5,4},{6,7},{7,6},{8,9},{9,8},{10,11... | collective-permute-start | bytes 1572872 | tf_op jit(solution)/shard_map/ppermute | solution.py:243
  35.3 9.0 %collective-permute-start.5 = (bf16[4,64,512]{2,1,0:T(8,128)(2,1)}, bf16[4,64,512]{2,1,0:T(8,128)(2,1)}, u32[]{:S(2)}, u32[]{:S(2)}) collective-permute-start(bf16[4,64,512]{2,1,0:T(8,128)(2,1)} %select_n.37), channel_id=1, source_target_pairs={{0,2},{2,0},{4,6},{6,4},{8,10},{10,8},{12,14},{14,12},{1,3},{3,1},... | collective-permute-start | bytes 786440 | tf_op jit(solution)/shard_map/ppermute | solution.py:255
  35.4 9.5 %copy-start.6 = (s32[2]{0:T(128)S(1)}, s32[2]{0:T(128)}, u32[]{:S(2)}) copy-start(s32[2]{0:T(128)} %param.15) | copy-start | bytes 28
  35.4 11.9 %copy-start.2 = (bf16[1,512,256]{2,1,0:T(8,128)(2,1)S(1)}, bf16[1,512,256]{2,1,0:T(8,128)(2,1)}, u32[]{:S(2)}) copy-start(bf16[1,512,256]{2,1,0:T(8,128)(2,1)} %param.10) | copy-start | bytes 786436
  36.4 8.6 %collective-permute-start.7 = (bf16[2,768,256]{2,1,0:T(8,128)(2,1)S(1)}, bf16[2,768,256]{2,1,0:T(8,128)(2,1)S(1)}, u32[]{:S(2)}, u32[]{:S(2)}) collective-permute-start(bf16[2,768,256]{2,1,0:T(8,128)(2,1)S(1)} %copy-done), channel_id=1, source_target_pairs={{0,1},{1,0},{2,3},{3,2},{4,5},{5,4},{6,7},{7,6},{8,9},{9,8},{10,11... | collective-permute-start | bytes 2359304 | tf_op jit(solution)/shard_map/ppermute | solution.py:243
  40.7 11.3 %collective-permute-start.12 = (bf16[2,768,256]{2,1,0:T(8,128)(2,1)}, bf16[2,768,256]{2,1,0:T(8,128)(2,1)}, u32[]{:S(2)}, u32[]{:S(2)}) collective-permute-start(bf16[2,768,256]{2,1,0:T(8,128)(2,1)} %pad_maximum_fusion), channel_id=1, source_target_pairs={{0,1},{1,0},{2,3},{3,2},{4,5},{5,4},{6,7},{7,6},{8,9},{9,8},{10,11... | collective-permute-start | bytes 2359304 | tf_op jit(solution)/shard_map/ppermute | solution.py:243
  44.3 7.6 %collective-permute-start.13 = (bf16[2,768,256]{2,1,0:T(8,128)(2,1)}, bf16[2,768,256]{2,1,0:T(8,128)(2,1)}, u32[]{:S(2)}, u32[]{:S(2)}) collective-permute-start(bf16[2,768,256]{2,1,0:T(8,128)(2,1)} %pad_maximum_fusion.1), channel_id=1, source_target_pairs={{0,1},{1,0},{2,3},{3,2},{4,5},{5,4},{6,7},{7,6},{8,9},{9,8},{10,11... | collective-permute-start | bytes 2359304 | tf_op jit(solution)/shard_map/ppermute | solution.py:243
  44.4 3.0 %collective-permute-start.6 = (bf16[4,64,512]{2,1,0:T(8,128)(2,1)}, bf16[4,64,512]{2,1,0:T(8,128)(2,1)}, u32[]{:S(2)}, u32[]{:S(2)}) collective-permute-start(bf16[4,64,512]{2,1,0:T(8,128)(2,1)} %collective-permute-done.5.refs_2_), channel_id=1, source_target_pairs={{0,1},{1,0},{2,3},{3,2},{4,5},{5,4},{6,7},{7,6},{8,9},{9,8},{10,11... | collective-permute-start | bytes 786440 | tf_op jit(solution)/shard_map/ppermute | solution.py:243
  44.9 7.0 %copy-start.1 = (bf16[2,1536,256]{2,1,0:T(8,128)(2,1)S(1)}, bf16[2,1536,256]{2,1,0:T(8,128)(2,1)}, u32[]{:S(2)}) copy-start(bf16[2,1536,256]{2,1,0:T(8,128)(2,1)} %lc.1) | copy-start | bytes 4718596
  45.0 7.0 %copy-start.3 = (bf16[2,512,256]{2,1,0:T(8,128)(2,1)S(1)}, bf16[2,512,256]{2,1,0:T(8,128)(2,1)}, u32[]{:S(2)}) copy-start(bf16[2,512,256]{2,1,0:T(8,128)(2,1)} %dc.1) | copy-start | bytes 1572868
  45.0 7.0 %copy-start.4 = (s32[2,2]{1,0:T(2,128)S(1)}, s32[2,2]{1,0:T(2,128)}, u32[]{:S(2)}) copy-start(s32[2,2]{1,0:T(2,128)} %keep_ref.3) | copy-start | bytes 52

commit v3 on v2

--- a/solution.py
+++ b/solution.py
@@ -1,3 +1,5 @@
+import functools
+
 import jax
 import jax.numpy as jnp
 from jax import lax
@@ -10,16 +12,16 @@
 BF16 = jnp.bfloat16
 SEQUENCES = (
     (1, (
-        "swapped 0",
-        "swapped 1",
+        "near other",
+        "far other",
     )),
     (1, (
-        "swapped 0",
-        "far",
+        "a 2",
+        "c other",
     )),
     (1, (
-        "swapped 0",
         "a 2",
+        "own other",
     )),
 )
 
@@ -81,66 +83,100 @@
         whole[i] = part[...]
 
 
-def copy_top(place_ref, near, near_o, far, far_o, a):
+def load_top(loads, place, near, near_o, far, far_o, a, b):
     planes, block = near.shape[:2]
+    me, at, pair = place
+    copies = []
+    for i, ref in enumerate((far, far_o)):
+        copies.append(loads.start(ref, b.at[i]))
+    for ref, core in ((near, me), (near_o, 1 - me)):
+        for k in range(planes):
+            plane = lax.rem(at + planes - k, planes)
+            row = pl.multiple_of(((plane * 2 + pair) * 2 + core) * block, block)
+            copies.append(loads.start(ref.at[k], a.at[pl.ds(row, block)]))
+    return copies
+
+
+def place_top(place, a, b):
+    me, at, mine_at = place
+    _, planes, block, _ = b.shape
     span = 2 * block
-    me, pair = place_ref[0], place_ref[2]
-    for k in range(planes):
-        plane = lax.rem(place_ref[1] + planes - k, planes)
-        for ref, core in ((near, me), (near_o, 1 - me)):
-            row = pl.multiple_of(((plane * 2 + pair) * 2 + core) * block, block)
-            a[pl.ds(row, block), :] = ref[k]
-        for ref, core in ((far, me), (far_o, 1 - me)):
-            row = pl.multiple_of(((plane * 2 + 1 - pair) * 2 + core) * block, block)
-            for j in range(planes):
-                col = pl.multiple_of((2 * j + 1 - pair) * span, span)
-                a[pl.ds(row, block), pl.ds(col, span)] = ref[k, :, j * span : (j + 1) * span]
-    for i in range(planes):
-        for j in range(planes):
-            mine = pl.multiple_of((2 * i + pair) * span, span)
-            theirs = pl.multiple_of((2 * j + 1 - pair) * span, span)
-            a[pl.ds(theirs, span), pl.ds(mine, span)] = a[pl.ds(mine, span), pl.ds(theirs, span)].T
-
-
-def sides_of(place_ref, half):
-    mine = pl.multiple_of(place_ref[0] * half, half)
-    other = pl.multiple_of((1 - place_ref[0]) * half, half)
+    for pair in range(2):
+
+        @pl.when(mine_at == pair)
+        def _():
+            for k in range(planes):
+                plane = lax.rem(at + planes - k, planes)
+                for i, core in enumerate((me, 1 - me)):
+                    row = pl.multiple_of(((plane * 2 + 1 - pair) * 2 + core) * block, block)
+                    for j in range(planes):
+                        col = (2 * j + 1 - pair) * span
+                        a[pl.ds(row, block), col : col + span] = b[i, k, :, j * span : (j + 1) * span]
+            for i in range(planes):
+                for j in range(planes):
+                    mine = (2 * i + pair) * span
+                    theirs = (2 * j + 1 - pair) * span
+                    a[theirs : theirs + span, mine : mine + span] = a[
+                        mine : mine + span, theirs : theirs + span
+                    ].T
+
+
+def place_of():
+    row = lax.axis_index("row")
+    return lax.axis_index("col"), lax.div(row, 2), lax.rem(row, 2)
+
+
+def sides_of(me, half):
+    mine = pl.multiple_of(me * half, half)
+    other = pl.multiple_of((1 - me) * half, half)
     return pl.ds(mine, half), pl.ds(other, half)
 
 
-def parent_kernel(place_ref, *refs):
-    own, own_o, dp, pd, a, g = refs[-6:]
+def parent_kernel(*refs, direct):
+    place = place_of()
+    if direct:
+        a_refs, refs = refs[:4], refs[4:]
+    else:
+        a_refs, refs = refs[:1], refs[1:]
+    own, own_o, dp, pd, a, b, g, sem = refs
     width, half = dp.shape
     parts = own.shape[0]
-    if len(refs) == 10:
-        copy_top(place_ref, *refs[:4], a)
+    loads = Loads(sem)
+    if direct:
+        wait(load_top(loads, place, *a_refs, a, b))
+        place_top(place, a, b)
     else:
-        a[...] = refs[0][...]
+        loads.start(a_refs[0], a).wait()
     head = pl.ds(0, width)
     total = dot(a[:, :width], own[0, head, :])
     for j in range(1, parts):
         total += dot(a[:, j * width : (j + 1) * width], own[j, head, :])
     g[...] = total.astype(BF16)
-    for r, at in zip((own, own_o), sides_of(place_ref, half)):
+    for r, at in zip((own, own_o), sides_of(place[0], half)):
         y = dp[at, :].astype(F32)
         for j in range(parts):
             y += dot_t(r[j, head, :], g[j * width : (j + 1) * width, :])
         pd[at, :] = y.astype(BF16)
 
 
-def child_kernel(place_ref, slot_ref, keep_ref, a, lc, lc_o, dc, own, own_o, *refs):
+def child_kernel(parent_ref, keep_ref, a, lc, lc_o, dc, own, own_o, *refs):
     parts = own.shape[0]
     swapped, beyond, refs = refs[:parts], refs[parts : 2 * parts], refs[2 * parts :]
-    swapped_o, beyond_o, cc_out, cd_out, x, v, t, cc, cd, sem = refs
+    swapped_o, beyond_o, refs = refs[0], refs[1], refs[2:]
+    cc_out, cd_out, x, co, v, t, cc, cd, sem = refs
     children, _, half = lc.shape
     width = 2 * half
     tops = a.shape[0]
     head, below, tail = pl.ds(0, width), pl.ds(width, tops), pl.ds(width, half)
-    ends = sides_of(place_ref, half)
-    holds = (place_ref[0], 1 - place_ref[0])
+    me, row = lax.axis_index("col"), lax.axis_index("row")
+    ends = sides_of(me, half)
+    holds = (me, 1 - me)
+    pair = row + 1 - 2 * lax.rem(row, 2)
     loads = Loads(sem)
     chosen, outs = [], []
     for k in range(children):
+        parent = parent_ref[k]
+        slot = jnp.where(parent == row, 0, jnp.where(parent == pair, 1, 2))
         chosen.append([])
         for j in range(parts):
             for i, srcs in enumerate(
@@ -149,7 +185,8 @@
                     (own_o.at[j], swapped_o.at[j], beyond_o.at[j]),
                 )
             ):
-                chosen[k].append(loads.choose(slot_ref[k], srcs, x.at[k, i, j]))
+                chosen[k].append(loads.choose(slot, srcs, x.at[k, i, j]))
+    panel_o = loads.start(lc_o, co)
     for k in range(children):
         wait(chosen[k])
         for j in range(parts):
@@ -175,8 +212,9 @@
                 t[k, pl.ds(j * width, width), :] = jnp.zeros((width, half), BF16)
 
         outs.append(loads.start(t.at[k], cc_out.at[k, below]))
-    for k in range(children):
-        for i, r in enumerate((lc, lc_o)):
+    panel_o.wait()
+    for k in range(children):
+        for i, r in enumerate((lc, co)):
             y = dot_t(r[k, below, :], t[k]) + dot_t(r[k, head, :], cc[k])
             cd[k, ends[i], :] = (dc[k, ends[i], :].astype(F32) - y).astype(BF16)
         outs.append(loads.start(cd.at[k], cd_out.at[k]))
@@ -205,7 +243,7 @@
     *own, whole = pl.pallas_call(
         pack_kernel,
         out_shape=(packed,) * parts + (jax.ShapeDtypeStruct((parts, rows, half), BF16),),
-        in_specs=[smem] + [hbm] * 2,
+        in_specs=[smem] + [pl.BlockSpec(memory_space=pltpu.HBM)] * 2,
         out_specs=(vmem,) * (parts + 1),
         scratch_shapes=[pltpu.SemaphoreType.DMA((2 * parts,))],
         compiler_params=pltpu.CompilerParams(vmem_limit_bytes=60 << 20),
@@ -257,22 +295,24 @@
         top = [value(name) for name in ("near", "near other", "far", "far other")]
     else:
         top = [lax.all_gather(ainv_top, ("row", "col"), axis=0, tiled=True)]
-    place = jnp.stack([lax.axis_index("col"), row // 2, row % 2]).astype(jnp.int32)
-    slot = jnp.where(parent_of == row, 0, jnp.where(parent_of == row ^ 1, 1, 2)).astype(jnp.int32)
     parent_diag, full = pl.pallas_call(
-        parent_kernel,
+        functools.partial(parent_kernel, direct=direct),
         out_shape=(
             jax.ShapeDtypeStruct((width, half), BF16),
             jax.ShapeDtypeStruct((tops, tops), BF16),
         ),
-        in_specs=[smem] + [vmem] * (len(top) + 3),
+        in_specs=[hbm] * len(top) + [vmem] * 3,
         out_specs=(vmem,) * 2,
-        scratch_shapes=[pltpu.VMEM((tops, half), BF16)],
+        scratch_shapes=[
+            pltpu.VMEM((2, *top[-1].shape) if direct else (16, half), BF16),
+            pltpu.VMEM((tops, half), BF16),
+            pltpu.SemaphoreType.DMA((4 * devices if direct else 1,)),
+        ],
         compiler_params=pltpu.CompilerParams(vmem_limit_bytes=12 << 20),
         cost_estimate=pl.CostEstimate(
-            flops=2 * tops * half * (tops + width), bytes_accessed=1 << 20, transcendentals=0
+            flops=2 * tops * half * (tops + width), bytes_accessed=8 << 20, transcendentals=0
         ),
-    )(place, *top, whole, value("own other"), dinv_parent[0])
+    )(*top, whole, value("own other"), dinv_parent[0])
     sent = [value(f"{name} {j}") for name in ("swapped", "beyond") for j in range(parts)]
     sent += [value("swapped other"), value("beyond other")]
     child_column, child_diag = pl.pallas_call(
@@ -281,10 +321,11 @@
             jax.ShapeDtypeStruct(l_child.shape, BF16),
             jax.ShapeDtypeStruct(dinv_child.shape, BF16),
         ),
-        in_specs=[smem] * 3 + [vmem] * 4 + [hbm] * (len(sent) + 2),
+        in_specs=[smem] * 2 + [vmem] * 2 + [hbm, vmem] + [hbm] * (len(sent) + 2),
         out_specs=(hbm,) * 2,
         scratch_shapes=[
             pltpu.VMEM((children, 2, parts, rows, half), BF16),
+            pltpu.VMEM(l_child.shape, BF16),
             pltpu.VMEM((children, tops, half), BF16),
             pltpu.VMEM((children, tops, half), BF16),
             pltpu.VMEM((children, width, half), BF16),
@@ -293,7 +334,7 @@
         ],
         compiler_params=pltpu.CompilerParams(vmem_limit_bytes=20 << 20),
     )(
-        place, slot, keep_child, full, l_child, value("c other"), dinv_child,
+        parent_of, keep_child, full, l_child, value("c other"), dinv_child,
         whole, value("own other"), *sent,
     )
     return parent_diag[None], child_column, child_diag

time: 60.3 us -> 56.7 us (0.940)
  the two profiles are of different devices: /device:TPU:0 before, /device:TPU:3 now
where the time goes in v3:
time: 56.7 us; the launch traced here: 56.4 us
  starting transfers between devices  20.8 us (37%)
  waiting for transfers between devices  18.6 us (33%)
  Pallas kernels  14.3 us (25%)
  local copies, waits for them, and re-layouts  1.55 us (3%)
  between operations  0.9 us (2%)
    ppermute x10, waiting for transfers between devices, value(): got[name] = lax.ppermute(value(source), axis, pairs)  15.9 us
    ppermute x10, starting transfers between devices, value(): got[name] = lax.ppermute(value(source), axis, pairs)  13.8 us
    pallas_call x1, Pallas kernels, local(): pl.pallas_call(child_kernel, out_shape=(jax.ShapeDtypeStruct(l_child.shap...  7.14 us
    ppermute x4, starting transfers between devices, local(): got[name] = lax.ppermute(sent, axis, pairs)  7.06 us
    pallas_call x1, Pallas kernels, local(): pl.pallas_call(functools.partial(parent_kernel, direct=direct), out_shape...  4.15 us
    pallas_call x1, Pallas kernels, local(): pl.pallas_call(pack_kernel, out_shape=(packed,) * parts + (jax.ShapeDtype...  2.96 us
    ppermute x4, waiting for transfers between devices, local(): got[name] = lax.ppermute(sent, axis, pairs)  2.7 us
    another operation x5, local copies, waits for them, and re-layouts, value(): near = jnp.stack([got['a'], *(value(f'a {k}') for k in range(1, planes))])  1.25 us
  transfers between devices with their start and end apart: 14, of which 4 were waited for; matrix products, arithmetic and copies ran while one was open for 3% of the time, Pallas kernels for 7%

profile of v3, /device:TPU:3, one launch (start us, length us, event | category | flops | bytes accessed | tf_op | source)
XLA Modules:
  0.0 56.4 jit_solution(8235921669905753069)
XLA Ops:
  0.6 3.0 %shard_map.103 = (bf16[768,256]{1,0:T(8,128)(2,1)}, bf16[768,256]{1,0:T(8,128)(2,1)}, bf16[2,768,256]{2,1,0:T(8,128)(2,1)}) custom-call(s32[1,2]{1,0:T(1,128)} %keep_ref.2, bf16[1024,256]{1,0:T(8,128)(2,1)} %bitcast.19, bf16[512,256]{1,0:T(8,128)(2,1)} %bitcast.17), custom_call_target="tpu_custom_call" | custom-call | tf_op jit(solution)/shard_map/pallas_call | solution.py:243
  3.6 3.4 %collective-permute-start.2 = (bf16[64,1024]{1,0:T(8,128)(2,1)}, bf16[64,1024]{1,0:T(8,128)(2,1)S(1)}, u32[]{:S(2)}, u32[]{:S(2)}) collective-permute-start(bf16[64,1024]{1,0:T(8,128)(2,1)} %param.8), channel_id=1, source_target_pairs={{0,12},{2,14},{4,0},{6,2},{8,4},{10,6},{12,8},{14,10},{1,13},{3,15... | collective-permute-start | bytes 393224 | tf_op jit(solution)/shard_map/ppermute | solution.py:281
  7.0 0.4 collective-permute-start
  7.4 0.3 collective-permute-start.8
  7.7 1.2 %collective-permute-start.9 = (bf16[768,256]{1,0:T(8,128)(2,1)}, bf16[768,256]{1,0:T(8,128)(2,1)S(1)}, u32[]{:S(2)}, u32[]{:S(2)}) collective-permute-start(bf16[768,256]{1,0:T(8,128)(2,1)} %get-tuple-element.26), channel_id=1, source_target_pairs={{0,2},{2,0},{4,6},{6,4},{8,10},{10,8},{12,14},{14,12},{1,3},{3,1},... | collective-permute-start | bytes 1179656 | tf_op jit(solution)/shard_map/ppermute | solution.py:281
  8.9 1.0 %stack.48 = bf16[1,64,4,2,128]{4,3,2,1,0:T(2,128)(2,1)S(1)} reshape(bf16[64,1024]{1,0:T(8,128)(2,1)} %param.8) | data formatting | bytes 262144 | tf_op jit(solution)/shard_map/stack | solution.py:274
  9.9 8.3 %collective-permute-done.1 = bf16[64,1024]{1,0:T(8,128)(2,1)S(1)} collective-permute-done((bf16[64,1024]{1,0:T(8,128)(2,1)}, bf16[64,1024]{1,0:T(8,128)(2,1)S(1)}, u32[]{:S(2)}, u32[]{:S(2)}) %collective-permute-start.1) | collective-permute-done | bytes 131104 | tf_op jit(solution)/shard_map/ppermute | solution.py:281
  18.2 1.2 %collective-permute-start.7 = (bf16[2,1536,256]{2,1,0:T(8,128)(2,1)}, bf16[2,1536,256]{2,1,0:T(8,128)(2,1)}, u32[]{:S(2)}, u32[]{:S(2)}) collective-permute-start(bf16[2,1536,256]{2,1,0:T(8,128)(2,1)} %lc.1), channel_id=1, source_target_pairs={{0,1},{1,0},{2,3},{3,2},{4,5},{5,4},{6,7},{7,6},{8,9},{9,8},{10,11... | collective-permute-start | bytes 4718600 | tf_op jit(solution)/shard_map/ppermute | solution.py:293
  19.8 1.3 %collective-permute-start.10 = (bf16[768,256]{1,0:T(8,128)(2,1)S(1)}, bf16[768,256]{1,0:T(8,128)(2,1)S(1)}, u32[]{:S(2)}, u32[]{:S(2)}) collective-permute-start(bf16[768,256]{1,0:T(8,128)(2,1)S(1)} %collective-permute-done.8.refs_0_), channel_id=1, source_target_pairs={{0,4},{4,8},{6,2},{8,12},{10,6},{14,10},{1,5},{5,9},{7,3},{9,13},{... | collective-permute-start | bytes 1179656 | tf_op jit(solution)/shard_map/ppermute | solution.py:281
  21.1 4.1 %collective-permute-done.9.refs_1_ = bf16[768,256]{1,0:T(8,128)(2,1)S(1)} collective-permute-done((bf16[768,256]{1,0:T(8,128)(2,1)}, bf16[768,256]{1,0:T(8,128)(2,1)S(1)}, u32[]{:S(2)}, u32[]{:S(2)}) %collective-permute-start.9) | collective-permute-done | bytes 393248 | tf_op jit(solution)/shard_map/ppermute | solution.py:281
  25.2 1.3 %collective-permute-start.11 = (bf16[768,256]{1,0:T(8,128)(2,1)S(1)}, bf16[768,256]{1,0:T(8,128)(2,1)S(1)}, u32[]{:S(2)}, u32[]{:S(2)}) collective-permute-start(bf16[768,256]{1,0:T(8,128)(2,1)S(1)} %collective-permute-done.9.refs_1_), channel_id=1, source_target_pairs={{0,4},{4,8},{6,2},{8,12},{10,6},{14,10},{1,5},{5,9},{7,3},{9,13},{... | collective-permute-start | bytes 1179656 | tf_op jit(solution)/shard_map/ppermute | solution.py:281
  26.4 0.1 slice_select_fusion
  26.6 0.1 select_n.22
  26.7 3.2 %collective-permute-start.4 = (bf16[4,64,512]{2,1,0:T(8,128)(2,1)S(1)}, bf16[4,64,512]{2,1,0:T(8,128)(2,1)S(1)}, u32[]{:S(2)}, u32[]{:S(2)}) collective-permute-start(bf16[4,64,512]{2,1,0:T(8,128)(2,1)S(1)} %select_n.22), channel_id=1, source_target_pairs={{0,2},{2,0},{4,6},{6,4},{8,10},{10,8},{12,14},{14,12},{1,3},{3,1},... | collective-permute-start | bytes 786440 | tf_op jit(solution)/shard_map/ppermute | solution.py:281
  30.0 3.1 %collective-permute-start.3 = (bf16[4,64,1024]{2,1,0:T(8,128)(2,1)S(1)}, bf16[4,64,1024]{2,1,0:T(8,128)(2,1)S(1)}, u32[]{:S(2)}, u32[]{:S(2)}) collective-permute-start(bf16[4,64,1024]{2,1,0:T(8,128)(2,1)S(1)} %pad_maximum_fusion.2.refs_0_), channel_id=1, source_target_pairs={{0,1},{1,0},{2,3},{3,2},{4,5},{5,4},{6,7},{7,6},{8,9},{9,8},{10,11... | collective-permute-start | bytes 1572872 | tf_op jit(solution)/shard_map/ppermute | solution.py:293
  33.0 0.1 pad_maximum_fusion
  33.1 2.3 %collective-permute-start.6 = (bf16[2,768,256]{2,1,0:T(8,128)(2,1)S(1)}, bf16[2,768,256]{2,1,0:T(8,128)(2,1)S(1)}, u32[]{:S(2)}, u32[]{:S(2)}) collective-permute-start(bf16[2,768,256]{2,1,0:T(8,128)(2,1)S(1)} %copy-done), channel_id=1, source_target_pairs={{0,1},{1,0},{2,3},{3,2},{4,5},{5,4},{6,7},{7,6},{8,9},{9,8},{10,11... | collective-permute-start | bytes 2359304 | tf_op jit(solution)/shard_map/ppermute | solution.py:293
  35.5 3.5 %collective-permute-done.11.refs_3_ = bf16[768,256]{1,0:T(8,128)(2,1)S(1)} collective-permute-done((bf16[768,256]{1,0:T(8,128)(2,1)S(1)}, bf16[768,256]{1,0:T(8,128)(2,1)S(1)}, u32[]{:S(2)}, u32[]{:S(2)}) %collective-permute-start.11) | collective-permute-done | bytes 393248 | tf_op jit(solution)/shard_map/ppermute | solution.py:281
  39.0 2.6 %collective-permute-start.12 = (bf16[2,768,256]{2,1,0:T(8,128)(2,1)S(1)}, bf16[2,768,256]{2,1,0:T(8,128)(2,1)S(1)}, u32[]{:S(2)}, u32[]{:S(2)}) collective-permute-start(bf16[2,768,256]{2,1,0:T(8,128)(2,1)S(1)} %pad_maximum_fusion), channel_id=1, source_target_pairs={{0,1},{1,0},{2,3},{3,2},{4,5},{5,4},{6,7},{7,6},{8,9},{9,8},{10,11... | collective-permute-start | bytes 2359304 | tf_op jit(solution)/shard_map/ppermute | solution.py:281
  41.6 0.1 pad_maximum_fusion.1
  41.9 0.5 collective-permute-start.5
  42.4 2.7 %collective-permute-done.5.refs_3_ = bf16[4,64,512]{2,1,0:T(8,128)(2,1)S(1)} collective-permute-done((bf16[4,64,512]{2,1,0:T(8,128)(2,1)S(1)}, bf16[4,64,512]{2,1,0:T(8,128)(2,1)S(1)}, u32[]{:S(2)}, u32[]{:S(2)}) %collective-permute-start.5) | collective-permute-done | bytes 262176 | tf_op jit(solution)/shard_map/ppermute | solution.py:293
  45.1 4.2 %shard_map.104 = (bf16[512,256]{1,0:T(8,128)(2,1)}, bf16[1024,1024]{1,0:T(8,128)(2,1)S(1)}) custom-call(bf16[4,64,1024]{2,1,0:T(8,128)(2,1)S(1)} %pad_maximum_fusion.2.refs_0_, bf16[4,64,1024]{2,1,0:T(8,128)(2,1)S(1)} %collective-permute-done.3.refs_1_, bf16[4,64,512]{2,1,0:T(8,128)(2,1)S(1)} %collective-permute-done.4.refs_2_, ...), custom_call_target="tpu_custom_call" | custom-call | flops 805306368 | bytes 8388608 | tf_op jit(solution)/shard_map/pallas_call | solution.py:298
  49.3 7.1 %shard_map.105 = (bf16[2,1536,256]{2,1,0:T(8,128)(2,1)}, bf16[2,512,256]{2,1,0:T(8,128)(2,1)}) custom-call(s32[2]{0:T(128)S(1)} %copy-done.5, s32[2,2]{1,0:T(2,128)S(1)} %copy-done.4, bf16[1024,1024]{1,0:T(8,128)(2,1)S(1)} %get-tuple-element.23.a, bf16[2,1536,256]{2,1,0:T(8,128)(2,1)S(1)} %copy-done.1, bf16[2,1536,256]{2,1,0:T(8,128)(2,1)} %collective-permute-done.7.lc_o, ...), custom_call_target="tpu_custom_call" | custom-call | tf_op jit(solution)/shard_map/pallas_call | solution.py:318
  (34 shorter events, 0.6 us)
Async XLA Ops:
  3.6 16.0 %collective-permute-start.2 = (bf16[64,1024]{1,0:T(8,128)(2,1)}, bf16[64,1024]{1,0:T(8,128)(2,1)S(1)}, u32[]{:S(2)}, u32[]{:S(2)}) collective-permute-start(bf16[64,1024]{1,0:T(8,128)(2,1)} %param.8), channel_id=1, source_target_pairs={{0,12},{2,14},{4,0},{6,2},{8,4},{10,6},{12,8},{14,10},{1,13},{3,15... | collective-permute-start | bytes 393224 | tf_op jit(solution)/shard_map/ppermute | solution.py:281
  7.0 11.2 %collective-permute-start.1 = (bf16[64,1024]{1,0:T(8,128)(2,1)}, bf16[64,1024]{1,0:T(8,128)(2,1)S(1)}, u32[]{:S(2)}, u32[]{:S(2)}) collective-permute-start(bf16[64,1024]{1,0:T(8,128)(2,1)} %param.8), channel_id=1, source_target_pairs={{0,8},{2,10},{4,12},{6,14},{8,0},{10,2},{12,4},{14,6},{1,9},{3,11}... | collective-permute-start | bytes 393224 | tf_op jit(solution)/shard_map/ppermute | solution.py:281
  7.0 12.4 %collective-permute-start = (bf16[64,1024]{1,0:T(8,128)(2,1)}, bf16[64,1024]{1,0:T(8,128)(2,1)S(1)}, u32[]{:S(2)}, u32[]{:S(2)}) collective-permute-start(bf16[64,1024]{1,0:T(8,128)(2,1)} %param.8), channel_id=1, source_target_pairs={{0,4},{2,6},{4,8},{6,10},{8,12},{10,14},{12,0},{14,2},{1,5},{3,7},... | collective-permute-start | bytes 393224 | tf_op jit(solution)/shard_map/ppermute | solution.py:281
  7.4 12.4 %collective-permute-start.8 = (bf16[768,256]{1,0:T(8,128)(2,1)}, bf16[768,256]{1,0:T(8,128)(2,1)S(1)}, u32[]{:S(2)}, u32[]{:S(2)}) collective-permute-start(bf16[768,256]{1,0:T(8,128)(2,1)} %get-tuple-element.25), channel_id=1, source_target_pairs={{0,2},{2,0},{4,6},{6,4},{8,10},{10,8},{12,14},{14,12},{1,3},{3,1},... | collective-permute-start | bytes 1179656 | tf_op jit(solution)/shard_map/ppermute | solution.py:281
  7.7 17.5 %collective-permute-start.9 = (bf16[768,256]{1,0:T(8,128)(2,1)}, bf16[768,256]{1,0:T(8,128)(2,1)S(1)}, u32[]{:S(2)}, u32[]{:S(2)}) collective-permute-start(bf16[768,256]{1,0:T(8,128)(2,1)} %get-tuple-element.26), channel_id=1, source_target_pairs={{0,2},{2,0},{4,6},{6,4},{8,10},{10,8},{12,14},{14,12},{1,3},{3,1},... | collective-permute-start | bytes 1179656 | tf_op jit(solution)/shard_map/ppermute | solution.py:281
  9.9 20.0 %copy-start.6 = (bf16[64,1024]{1,0:T(8,128)(2,1)S(1)}, bf16[64,1024]{1,0:T(8,128)(2,1)}, u32[]{:S(2)}) copy-start(bf16[64,1024]{1,0:T(8,128)(2,1)} %param.8) | copy-start | bytes 393220
  18.2 31.1 %collective-permute-start.7 = (bf16[2,1536,256]{2,1,0:T(8,128)(2,1)}, bf16[2,1536,256]{2,1,0:T(8,128)(2,1)}, u32[]{:S(2)}, u32[]{:S(2)}) collective-permute-start(bf16[2,1536,256]{2,1,0:T(8,128)(2,1)} %lc.1), channel_id=1, source_target_pairs={{0,1},{1,0},{2,3},{3,2},{4,5},{5,4},{6,7},{7,6},{8,9},{9,8},{10,11... | collective-permute-start | bytes 4718600 | tf_op jit(solution)/shard_map/ppermute | solution.py:293
  19.8 13.3 %collective-permute-start.10 = (bf16[768,256]{1,0:T(8,128)(2,1)S(1)}, bf16[768,256]{1,0:T(8,128)(2,1)S(1)}, u32[]{:S(2)}, u32[]{:S(2)}) collective-permute-start(bf16[768,256]{1,0:T(8,128)(2,1)S(1)} %collective-permute-done.8.refs_0_), channel_id=1, source_target_pairs={{0,4},{4,8},{6,2},{8,12},{10,6},{14,10},{1,5},{5,9},{7,3},{9,13},{... | collective-permute-start | bytes 1179656 | tf_op jit(solution)/shard_map/ppermute | solution.py:281
  25.2 13.8 %collective-permute-start.11 = (bf16[768,256]{1,0:T(8,128)(2,1)S(1)}, bf16[768,256]{1,0:T(8,128)(2,1)S(1)}, u32[]{:S(2)}, u32[]{:S(2)}) collective-permute-start(bf16[768,256]{1,0:T(8,128)(2,1)S(1)} %collective-permute-done.9.refs_1_), channel_id=1, source_target_pairs={{0,4},{4,8},{6,2},{8,12},{10,6},{14,10},{1,5},{5,9},{7,3},{9,13},{... | collective-permute-start | bytes 1179656 | tf_op jit(solution)/shard_map/ppermute | solution.py:281
  26.6 6.5 %copy-start = (bf16[2,768,256]{2,1,0:T(8,128)(2,1)S(1)}, bf16[2,768,256]{2,1,0:T(8,128)(2,1)}, u32[]{:S(2)}) copy-start(bf16[2,768,256]{2,1,0:T(8,128)(2,1)} %get-tuple-element.21.refs_4_.own) | copy-start | bytes 2359300
  26.7 15.1 %collective-permute-start.4 = (bf16[4,64,512]{2,1,0:T(8,128)(2,1)S(1)}, bf16[4,64,512]{2,1,0:T(8,128)(2,1)S(1)}, u32[]{:S(2)}, u32[]{:S(2)}) collective-permute-start(bf16[4,64,512]{2,1,0:T(8,128)(2,1)S(1)} %select_n.22), channel_id=1, source_target_pairs={{0,2},{2,0},{4,6},{6,4},{8,10},{10,8},{12,14},{14,12},{1,3},{3,1},... | collective-permute-start | bytes 786440 | tf_op jit(solution)/shard_map/ppermute | solution.py:281
  30.0 11.9 %collective-permute-start.3 = (bf16[4,64,1024]{2,1,0:T(8,128)(2,1)S(1)}, bf16[4,64,1024]{2,1,0:T(8,128)(2,1)S(1)}, u32[]{:S(2)}, u32[]{:S(2)}) collective-permute-start(bf16[4,64,1024]{2,1,0:T(8,128)(2,1)S(1)} %pad_maximum_fusion.2.refs_0_), channel_id=1, source_target_pairs={{0,1},{1,0},{2,3},{3,2},{4,5},{5,4},{6,7},{7,6},{8,9},{9,8},{10,11... | collective-permute-start | bytes 1572872 | tf_op jit(solution)/shard_map/ppermute | solution.py:293
  33.0 12.0 %copy-start.2 = (bf16[1,512,256]{2,1,0:T(8,128)(2,1)S(1)}, bf16[1,512,256]{2,1,0:T(8,128)(2,1)}, u32[]{:S(2)}) copy-start(bf16[1,512,256]{2,1,0:T(8,128)(2,1)} %param.10) | copy-start | bytes 786436
  33.1 11.9 %collective-permute-start.6 = (bf16[2,768,256]{2,1,0:T(8,128)(2,1)S(1)}, bf16[2,768,256]{2,1,0:T(8,128)(2,1)S(1)}, u32[]{:S(2)}, u32[]{:S(2)}) collective-permute-start(bf16[2,768,256]{2,1,0:T(8,128)(2,1)S(1)} %copy-done), channel_id=1, source_target_pairs={{0,1},{1,0},{2,3},{3,2},{4,5},{5,4},{6,7},{7,6},{8,9},{9,8},{10,11... | collective-permute-start | bytes 2359304 | tf_op jit(solution)/shard_map/ppermute | solution.py:293
  39.0 10.2 %collective-permute-start.12 = (bf16[2,768,256]{2,1,0:T(8,128)(2,1)S(1)}, bf16[2,768,256]{2,1,0:T(8,128)(2,1)S(1)}, u32[]{:S(2)}, u32[]{:S(2)}) collective-permute-start(bf16[2,768,256]{2,1,0:T(8,128)(2,1)S(1)} %pad_maximum_fusion), channel_id=1, source_target_pairs={{0,1},{1,0},{2,3},{3,2},{4,5},{5,4},{6,7},{7,6},{8,9},{9,8},{10,11... | collective-permute-start | bytes 2359304 | tf_op jit(solution)/shard_map/ppermute | solution.py:281
  41.7 7.5 %copy-start.1 = (bf16[2,1536,256]{2,1,0:T(8,128)(2,1)S(1)}, bf16[2,1536,256]{2,1,0:T(8,128)(2,1)}, u32[]{:S(2)}) copy-start(bf16[2,1536,256]{2,1,0:T(8,128)(2,1)} %lc.1) | copy-start | bytes 4718596
  41.7 7.5 %copy-start.3 = (bf16[2,512,256]{2,1,0:T(8,128)(2,1)S(1)}, bf16[2,512,256]{2,1,0:T(8,128)(2,1)}, u32[]{:S(2)}) copy-start(bf16[2,512,256]{2,1,0:T(8,128)(2,1)} %dc.1) | copy-start | bytes 1572868
  41.7 7.5 %copy-start.4 = (s32[2,2]{1,0:T(2,128)S(1)}, s32[2,2]{1,0:T(2,128)}, u32[]{:S(2)}) copy-start(s32[2,2]{1,0:T(2,128)} %keep_ref.3) | copy-start | bytes 52
  41.8 7.5 %copy-start.5 = (s32[2]{0:T(128)S(1)}, s32[2]{0:T(128)}, u32[]{:S(2)}) copy-start(s32[2]{0:T(128)} %parent_ref.1) | copy-start | bytes 28
  41.8 7.5 %collective-permute-start.13 = (bf16[2,768,256]{2,1,0:T(8,128)(2,1)S(1)}, bf16[2,768,256]{2,1,0:T(8,128)(2,1)S(1)}, u32[]{:S(2)}, u32[]{:S(2)}) collective-permute-start(bf16[2,768,256]{2,1,0:T(8,128)(2,1)S(1)} %pad_maximum_fusion.1), channel_id=1, source_target_pairs={{0,1},{1,0},{2,3},{3,2},{4,5},{5,4},{6,7},{7,6},{8,9},{9,8},{10,11... | collective-permute-start | bytes 2359304 | tf_op jit(solution)/shard_map/ppermute | solution.py:281
  41.9 3.2 %collective-permute-start.5 = (bf16[4,64,512]{2,1,0:T(8,128)(2,1)S(1)}, bf16[4,64,512]{2,1,0:T(8,128)(2,1)S(1)}, u32[]{:S(2)}, u32[]{:S(2)}) collective-permute-start(bf16[4,64,512]{2,1,0:T(8,128)(2,1)S(1)} %collective-permute-done.4.refs_2_), channel_id=1, source_target_pairs={{0,1},{1,0},{2,3},{3,2},{4,5},{5,4},{6,7},{7,6},{8,9},{9,8},{10,11... | collective-permute-start | bytes 786440 | tf_op jit(solution)/shard_map/ppermute | solution.py:293

commit v4 on v3

--- a/solution.py
+++ b/solution.py
@@ -44,17 +44,6 @@
         copy.start()
         return copy
 
-    def choose(self, which, srcs, dst):
-        sem = self.sem.at[self.used]
-        self.used += 1
-        for k, src in enumerate(srcs):
-
-            @pl.when(which == k)
-            def _(src=src):
-                pltpu.make_async_copy(src, dst, sem).start()
-
-        return pltpu.make_async_copy(srcs[0], dst, sem)
-
 
 def wait(copies):
     for copy in copies:
@@ -62,25 +51,28 @@
 
 
 def pack_kernel(keep_ref, factor, inverse, *refs):
-    parts, whole, sem = refs[:-2], refs[-2], refs[-1]
+    parts, (whole, x, sem) = refs[:-3], refs[-3:]
     width = inverse.shape[0]
     share = width // len(parts)
     loads = Loads(sem)
     copies = [
         (
-            loads.start(factor.at[pl.ds(i * width, width)], part.at[pl.ds(0, width)]),
-            loads.start(inverse.at[pl.ds(i * share, share)], part.at[pl.ds(width, share)]),
+            loads.start(factor.at[pl.ds(i * width, width)], x.at[i, pl.ds(0, width)]),
+            loads.start(inverse.at[pl.ds(i * share, share)], x.at[i, pl.ds(width, share)]),
         )
-        for i, part in enumerate(parts)
+        for i in range(len(parts))
     ]
+    outs = []
     for i, part in enumerate(parts):
         wait(copies[i])
 
         @pl.when(keep_ref[0, i] == 0)
-        def _(part=part):
-            part[pl.ds(0, width), :] = jnp.zeros((width, part.shape[1]), part.dtype)
-
-        whole[i] = part[...]
+        def _(i=i):
+            x[i, pl.ds(0, width), :] = jnp.zeros((width, x.shape[2]), x.dtype)
+
+        outs.append(loads.start(x.at[i], part))
+    outs.append(loads.start(x, whole))
+    wait(outs)
 
 
 def load_top(loads, place, near, near_o, far, far_o, a, b):
@@ -176,16 +168,25 @@
     chosen, outs = [], []
     for k in range(children):
         parent = parent_ref[k]
-        slot = jnp.where(parent == row, 0, jnp.where(parent == pair, 1, 2))
-        chosen.append([])
-        for j in range(parts):
-            for i, srcs in enumerate(
-                (
-                    (own.at[j], swapped[j], beyond[j]),
-                    (own_o.at[j], swapped_o.at[j], beyond_o.at[j]),
-                )
-            ):
-                chosen[k].append(loads.choose(slot, srcs, x.at[k, i, j]))
+        sources = (
+            (parent == row, [own.at[j] for j in range(parts)], own_o),
+            (parent == pair, swapped, swapped_o),
+            (jnp.logical_and(parent != row, parent != pair), beyond, beyond_o),
+        )
+        sems = [sem.at[loads.used + j] for j in range(parts + 1)]
+        loads.used += parts + 1
+        for flag, mine, other in sources:
+
+            @pl.when(flag)
+            def _(k=k, mine=mine, other=other, sems=sems):
+                for j in range(parts):
+                    pltpu.make_async_copy(mine[j], x.at[k, 0, j], sems[j]).start()
+                pltpu.make_async_copy(other, x.at[k, 1], sems[parts]).start()
+
+        chosen.append(
+            [pltpu.make_async_copy(own.at[j], x.at[k, 0, j], sems[j]) for j in range(parts)]
+            + [pltpu.make_async_copy(own_o, x.at[k, 1], sems[parts])]
+        )
     panel_o = loads.start(lc_o, co)
     for k in range(children):
         wait(chosen[k])
@@ -244,8 +245,11 @@
         pack_kernel,
         out_shape=(packed,) * parts + (jax.ShapeDtypeStruct((parts, rows, half), BF16),),
         in_specs=[smem] + [pl.BlockSpec(memory_space=pltpu.HBM)] * 2,
-        out_specs=(vmem,) * (parts + 1),
-        scratch_shapes=[pltpu.SemaphoreType.DMA((2 * parts,))],
+        out_specs=(hbm,) * (parts + 1),
+        scratch_shapes=[
+            pltpu.VMEM((parts, rows, half), BF16),
+            pltpu.SemaphoreType.DMA((3 * parts + 1,)),
+        ],
         compiler_params=pltpu.CompilerParams(vmem_limit_bytes=60 << 20),
     )(keep_parent, l_parent[0], dinv_parent[0])
     ainv_top, *own = lax.optimization_barrier((ainv_top, *own))

time: 56.7 us -> 55.9 us (0.986)
  Pallas kernels: 14.3 us -> 13.5 us
    pallas_call x1, Pallas kernels: 7.14 us -> 6.46 us  [local(): pl.pallas_call(child_kernel, out_shape=(jax.ShapeDtypeStruct(l_child.shap...]
where the time goes in v4:
time: 55.9 us; the launch traced here: 55.7 us
  starting transfers between devices  20.8 us (37%)
  waiting for transfers between devices  18.6 us (33%)
  Pallas kernels  13.5 us (24%)
  local copies, waits for them, and re-layouts  1.55 us (3%)
  between operations  0.9 us (2%)
    ppermute x10, waiting for transfers between devices, value(): got[name] = lax.ppermute(value(source), axis, pairs)  15.9 us
    ppermute x10, starting transfers between devices, value(): got[name] = lax.ppermute(value(source), axis, pairs)  13.7 us
    ppermute x4, starting transfers between devices, local(): got[name] = lax.ppermute(sent, axis, pairs)  7.08 us
    pallas_call x1, Pallas kernels, local(): pl.pallas_call(child_kernel, out_shape=(jax.ShapeDtypeStruct(l_child.shap...  6.46 us
    pallas_call x1, Pallas kernels, local(): pl.pallas_call(functools.partial(parent_kernel, direct=direct), out_shape...  4.16 us
    pallas_call x1, Pallas kernels, local(): pl.pallas_call(pack_kernel, out_shape=(packed,) * parts + (jax.ShapeDtype...  2.87 us
    ppermute x4, waiting for transfers between devices, local(): got[name] = lax.ppermute(sent, axis, pairs)  2.7 us
    another operation x5, local copies, waits for them, and re-layouts, value(): near = jnp.stack([got['a'], *(value(f'a {k}') for k in range(1, planes))])  1.25 us
  transfers between devices with their start and end apart: 14, of which 4 were waited for; matrix products, arithmetic and copies ran while one was open for 3% of the time, Pallas kernels for 7%

profile of v4, /device:TPU:3, one launch (start us, length us, event | category | flops | bytes accessed | tf_op | source)
XLA Modules:
  0.0 55.7 jit_solution(1397209040394449724)
XLA Ops:
  0.6 2.9 %shard_map.103 = (bf16[768,256]{1,0:T(8,128)(2,1)}, bf16[768,256]{1,0:T(8,128)(2,1)}, bf16[2,768,256]{2,1,0:T(8,128)(2,1)}) custom-call(s32[1,2]{1,0:T(1,128)} %keep_ref.2, bf16[1024,256]{1,0:T(8,128)(2,1)} %bitcast.19, bf16[512,256]{1,0:T(8,128)(2,1)} %bitcast.17), custom_call_target="tpu_custom_call" | custom-call | tf_op jit(solution)/shard_map/pallas_call | solution.py:244
  3.5 3.4 %collective-permute-start.2 = (bf16[64,1024]{1,0:T(8,128)(2,1)}, bf16[64,1024]{1,0:T(8,128)(2,1)S(1)}, u32[]{:S(2)}, u32[]{:S(2)}) collective-permute-start(bf16[64,1024]{1,0:T(8,128)(2,1)} %param.8), channel_id=1, source_target_pairs={{0,12},{2,14},{4,0},{6,2},{8,4},{10,6},{12,8},{14,10},{1,13},{3,15... | collective-permute-start | bytes 393224 | tf_op jit(solution)/shard_map/ppermute | solution.py:285
  6.9 0.4 collective-permute-start
  7.3 0.3 collective-permute-start.8
  7.6 1.2 %collective-permute-start.9 = (bf16[768,256]{1,0:T(8,128)(2,1)}, bf16[768,256]{1,0:T(8,128)(2,1)S(1)}, u32[]{:S(2)}, u32[]{:S(2)}) collective-permute-start(bf16[768,256]{1,0:T(8,128)(2,1)} %get-tuple-element.26), channel_id=1, source_target_pairs={{0,2},{2,0},{4,6},{6,4},{8,10},{10,8},{12,14},{14,12},{1,3},{3,1},... | collective-permute-start | bytes 1179656 | tf_op jit(solution)/shard_map/ppermute | solution.py:285
  8.8 1.0 %stack.48 = bf16[1,64,4,2,128]{4,3,2,1,0:T(2,128)(2,1)S(1)} reshape(bf16[64,1024]{1,0:T(8,128)(2,1)} %param.8) | data formatting | bytes 262144 | tf_op jit(solution)/shard_map/stack | solution.py:278
  9.8 8.3 %collective-permute-done.1 = bf16[64,1024]{1,0:T(8,128)(2,1)S(1)} collective-permute-done((bf16[64,1024]{1,0:T(8,128)(2,1)}, bf16[64,1024]{1,0:T(8,128)(2,1)S(1)}, u32[]{:S(2)}, u32[]{:S(2)}) %collective-permute-start.1) | collective-permute-done | bytes 131104 | tf_op jit(solution)/shard_map/ppermute | solution.py:285
  18.1 1.2 %collective-permute-start.7 = (bf16[2,1536,256]{2,1,0:T(8,128)(2,1)}, bf16[2,1536,256]{2,1,0:T(8,128)(2,1)}, u32[]{:S(2)}, u32[]{:S(2)}) collective-permute-start(bf16[2,1536,256]{2,1,0:T(8,128)(2,1)} %lc.1), channel_id=1, source_target_pairs={{0,1},{1,0},{2,3},{3,2},{4,5},{5,4},{6,7},{7,6},{8,9},{9,8},{10,11... | collective-permute-start | bytes 4718600 | tf_op jit(solution)/shard_map/ppermute | solution.py:297
  19.7 1.3 %collective-permute-start.10 = (bf16[768,256]{1,0:T(8,128)(2,1)S(1)}, bf16[768,256]{1,0:T(8,128)(2,1)S(1)}, u32[]{:S(2)}, u32[]{:S(2)}) collective-permute-start(bf16[768,256]{1,0:T(8,128)(2,1)S(1)} %collective-permute-done.8.refs_0_), channel_id=1, source_target_pairs={{0,4},{4,8},{6,2},{8,12},{10,6},{14,10},{1,5},{5,9},{7,3},{9,13},{... | collective-permute-start | bytes 1179656 | tf_op jit(solution)/shard_map/ppermute | solution.py:285
  21.0 4.1 %collective-permute-done.9.refs_1_ = bf16[768,256]{1,0:T(8,128)(2,1)S(1)} collective-permute-done((bf16[768,256]{1,0:T(8,128)(2,1)}, bf16[768,256]{1,0:T(8,128)(2,1)S(1)}, u32[]{:S(2)}, u32[]{:S(2)}) %collective-permute-start.9) | collective-permute-done | bytes 393248 | tf_op jit(solution)/shard_map/ppermute | solution.py:285
  25.0 1.3 %collective-permute-start.11 = (bf16[768,256]{1,0:T(8,128)(2,1)S(1)}, bf16[768,256]{1,0:T(8,128)(2,1)S(1)}, u32[]{:S(2)}, u32[]{:S(2)}) collective-permute-start(bf16[768,256]{1,0:T(8,128)(2,1)S(1)} %collective-permute-done.9.refs_1_), channel_id=1, source_target_pairs={{0,4},{4,8},{6,2},{8,12},{10,6},{14,10},{1,5},{5,9},{7,3},{9,13},{... | collective-permute-start | bytes 1179656 | tf_op jit(solution)/shard_map/ppermute | solution.py:285
  26.3 0.1 slice_select_fusion
  26.5 0.1 select_n.22
  26.6 3.2 %collective-permute-start.4 = (bf16[4,64,512]{2,1,0:T(8,128)(2,1)S(1)}, bf16[4,64,512]{2,1,0:T(8,128)(2,1)S(1)}, u32[]{:S(2)}, u32[]{:S(2)}) collective-permute-start(bf16[4,64,512]{2,1,0:T(8,128)(2,1)S(1)} %select_n.22), channel_id=1, source_target_pairs={{0,2},{2,0},{4,6},{6,4},{8,10},{10,8},{12,14},{14,12},{1,3},{3,1},... | collective-permute-start | bytes 786440 | tf_op jit(solution)/shard_map/ppermute | solution.py:285
  29.8 3.1 %collective-permute-start.3 = (bf16[4,64,1024]{2,1,0:T(8,128)(2,1)S(1)}, bf16[4,64,1024]{2,1,0:T(8,128)(2,1)S(1)}, u32[]{:S(2)}, u32[]{:S(2)}) collective-permute-start(bf16[4,64,1024]{2,1,0:T(8,128)(2,1)S(1)} %pad_maximum_fusion.2.refs_0_), channel_id=1, source_target_pairs={{0,1},{1,0},{2,3},{3,2},{4,5},{5,4},{6,7},{7,6},{8,9},{9,8},{10,11... | collective-permute-start | bytes 1572872 | tf_op jit(solution)/shard_map/ppermute | solution.py:297
  32.9 0.1 pad_maximum_fusion
  33.0 2.4 %collective-permute-start.6 = (bf16[2,768,256]{2,1,0:T(8,128)(2,1)S(1)}, bf16[2,768,256]{2,1,0:T(8,128)(2,1)S(1)}, u32[]{:S(2)}, u32[]{:S(2)}) collective-permute-start(bf16[2,768,256]{2,1,0:T(8,128)(2,1)S(1)} %copy-done), channel_id=1, source_target_pairs={{0,1},{1,0},{2,3},{3,2},{4,5},{5,4},{6,7},{7,6},{8,9},{9,8},{10,11... | collective-permute-start | bytes 2359304 | tf_op jit(solution)/shard_map/ppermute | solution.py:297
  35.4 3.5 %collective-permute-done.11.refs_3_ = bf16[768,256]{1,0:T(8,128)(2,1)S(1)} collective-permute-done((bf16[768,256]{1,0:T(8,128)(2,1)S(1)}, bf16[768,256]{1,0:T(8,128)(2,1)S(1)}, u32[]{:S(2)}, u32[]{:S(2)}) %collective-permute-start.11) | collective-permute-done | bytes 393248 | tf_op jit(solution)/shard_map/ppermute | solution.py:285
  38.9 2.6 %collective-permute-start.12 = (bf16[2,768,256]{2,1,0:T(8,128)(2,1)S(1)}, bf16[2,768,256]{2,1,0:T(8,128)(2,1)S(1)}, u32[]{:S(2)}, u32[]{:S(2)}) collective-permute-start(bf16[2,768,256]{2,1,0:T(8,128)(2,1)S(1)} %pad_maximum_fusion), channel_id=1, source_target_pairs={{0,1},{1,0},{2,3},{3,2},{4,5},{5,4},{6,7},{7,6},{8,9},{9,8},{10,11... | collective-permute-start | bytes 2359304 | tf_op jit(solution)/shard_map/ppermute | solution.py:285
  41.5 0.1 pad_maximum_fusion.1
  41.8 0.5 collective-permute-start.5
  42.3 2.7 %collective-permute-done.5.refs_3_ = bf16[4,64,512]{2,1,0:T(8,128)(2,1)S(1)} collective-permute-done((bf16[4,64,512]{2,1,0:T(8,128)(2,1)S(1)}, bf16[4,64,512]{2,1,0:T(8,128)(2,1)S(1)}, u32[]{:S(2)}, u32[]{:S(2)}) %collective-permute-start.5) | collective-permute-done | bytes 262176 | tf_op jit(solution)/shard_map/ppermute | solution.py:297
  45.0 4.2 %shard_map.104 = (bf16[512,256]{1,0:T(8,128)(2,1)}, bf16[1024,1024]{1,0:T(8,128)(2,1)S(1)}) custom-call(bf16[4,64,1024]{2,1,0:T(8,128)(2,1)S(1)} %pad_maximum_fusion.2.refs_0_, bf16[4,64,1024]{2,1,0:T(8,128)(2,1)S(1)} %collective-permute-done.3.refs_1_, bf16[4,64,512]{2,1,0:T(8,128)(2,1)S(1)} %collective-permute-done.4.refs_2_, ...), custom_call_target="tpu_custom_call" | custom-call | flops 805306368 | bytes 8388608 | tf_op jit(solution)/shard_map/pallas_call | solution.py:302
  49.2 6.5 %shard_map.105 = (bf16[2,1536,256]{2,1,0:T(8,128)(2,1)}, bf16[2,512,256]{2,1,0:T(8,128)(2,1)}) custom-call(s32[2]{0:T(128)S(1)} %copy-done.5, s32[2,2]{1,0:T(2,128)S(1)} %copy-done.4, bf16[1024,1024]{1,0:T(8,128)(2,1)S(1)} %get-tuple-element.23.a, bf16[2,1536,256]{2,1,0:T(8,128)(2,1)S(1)} %copy-done.1, bf16[2,1536,256]{2,1,0:T(8,128)(2,1)} %collective-permute-done.7.lc_o, ...), custom_call_target="tpu_custom_call" | custom-call | tf_op jit(solution)/shard_map/pallas_call | solution.py:322
  (34 shorter events, 0.6 us)
Async XLA Ops:
  3.5 16.0 %collective-permute-start.2 = (bf16[64,1024]{1,0:T(8,128)(2,1)}, bf16[64,1024]{1,0:T(8,128)(2,1)S(1)}, u32[]{:S(2)}, u32[]{:S(2)}) collective-permute-start(bf16[64,1024]{1,0:T(8,128)(2,1)} %param.8), channel_id=1, source_target_pairs={{0,12},{2,14},{4,0},{6,2},{8,4},{10,6},{12,8},{14,10},{1,13},{3,15... | collective-permute-start | bytes 393224 | tf_op jit(solution)/shard_map/ppermute | solution.py:285
  6.9 11.2 %collective-permute-start.1 = (bf16[64,1024]{1,0:T(8,128)(2,1)}, bf16[64,1024]{1,0:T(8,128)(2,1)S(1)}, u32[]{:S(2)}, u32[]{:S(2)}) collective-permute-start(bf16[64,1024]{1,0:T(8,128)(2,1)} %param.8), channel_id=1, source_target_pairs={{0,8},{2,10},{4,12},{6,14},{8,0},{10,2},{12,4},{14,6},{1,9},{3,11}... | collective-permute-start | bytes 393224 | tf_op jit(solution)/shard_map/ppermute | solution.py:285
  6.9 12.4 %collective-permute-start = (bf16[64,1024]{1,0:T(8,128)(2,1)}, bf16[64,1024]{1,0:T(8,128)(2,1)S(1)}, u32[]{:S(2)}, u32[]{:S(2)}) collective-permute-start(bf16[64,1024]{1,0:T(8,128)(2,1)} %param.8), channel_id=1, source_target_pairs={{0,4},{2,6},{4,8},{6,10},{8,12},{10,14},{12,0},{14,2},{1,5},{3,7},... | collective-permute-start | bytes 393224 | tf_op jit(solution)/shard_map/ppermute | solution.py:285
  7.3 12.4 %collective-permute-start.8 = (bf16[768,256]{1,0:T(8,128)(2,1)}, bf16[768,256]{1,0:T(8,128)(2,1)S(1)}, u32[]{:S(2)}, u32[]{:S(2)}) collective-permute-start(bf16[768,256]{1,0:T(8,128)(2,1)} %get-tuple-element.25), channel_id=1, source_target_pairs={{0,2},{2,0},{4,6},{6,4},{8,10},{10,8},{12,14},{14,12},{1,3},{3,1},... | collective-permute-start | bytes 1179656 | tf_op jit(solution)/shard_map/ppermute | solution.py:285
  7.6 17.5 %collective-permute-start.9 = (bf16[768,256]{1,0:T(8,128)(2,1)}, bf16[768,256]{1,0:T(8,128)(2,1)S(1)}, u32[]{:S(2)}, u32[]{:S(2)}) collective-permute-start(bf16[768,256]{1,0:T(8,128)(2,1)} %get-tuple-element.26), channel_id=1, source_target_pairs={{0,2},{2,0},{4,6},{6,4},{8,10},{10,8},{12,14},{14,12},{1,3},{3,1},... | collective-permute-start | bytes 1179656 | tf_op jit(solution)/shard_map/ppermute | solution.py:285
  9.8 20.0 %copy-start.6 = (bf16[64,1024]{1,0:T(8,128)(2,1)S(1)}, bf16[64,1024]{1,0:T(8,128)(2,1)}, u32[]{:S(2)}) copy-start(bf16[64,1024]{1,0:T(8,128)(2,1)} %param.8) | copy-start | bytes 393220
  18.1 31.1 %collective-permute-start.7 = (bf16[2,1536,256]{2,1,0:T(8,128)(2,1)}, bf16[2,1536,256]{2,1,0:T(8,128)(2,1)}, u32[]{:S(2)}, u32[]{:S(2)}) collective-permute-start(bf16[2,1536,256]{2,1,0:T(8,128)(2,1)} %lc.1), channel_id=1, source_target_pairs={{0,1},{1,0},{2,3},{3,2},{4,5},{5,4},{6,7},{7,6},{8,9},{9,8},{10,11... | collective-permute-start | bytes 4718600 | tf_op jit(solution)/shard_map/ppermute | solution.py:297
  19.7 13.3 %collective-permute-start.10 = (bf16[768,256]{1,0:T(8,128)(2,1)S(1)}, bf16[768,256]{1,0:T(8,128)(2,1)S(1)}, u32[]{:S(2)}, u32[]{:S(2)}) collective-permute-start(bf16[768,256]{1,0:T(8,128)(2,1)S(1)} %collective-permute-done.8.refs_0_), channel_id=1, source_target_pairs={{0,4},{4,8},{6,2},{8,12},{10,6},{14,10},{1,5},{5,9},{7,3},{9,13},{... | collective-permute-start | bytes 1179656 | tf_op jit(solution)/shard_map/ppermute | solution.py:285
  25.0 13.8 %collective-permute-start.11 = (bf16[768,256]{1,0:T(8,128)(2,1)S(1)}, bf16[768,256]{1,0:T(8,128)(2,1)S(1)}, u32[]{:S(2)}, u32[]{:S(2)}) collective-permute-start(bf16[768,256]{1,0:T(8,128)(2,1)S(1)} %collective-permute-done.9.refs_1_), channel_id=1, source_target_pairs={{0,4},{4,8},{6,2},{8,12},{10,6},{14,10},{1,5},{5,9},{7,3},{9,13},{... | collective-permute-start | bytes 1179656 | tf_op jit(solution)/shard_map/ppermute | solution.py:285
  26.5 6.5 %copy-start = (bf16[2,768,256]{2,1,0:T(8,128)(2,1)S(1)}, bf16[2,768,256]{2,1,0:T(8,128)(2,1)}, u32[]{:S(2)}) copy-start(bf16[2,768,256]{2,1,0:T(8,128)(2,1)} %get-tuple-element.21.refs_4_.own) | copy-start | bytes 2359300
  26.6 15.1 %collective-permute-start.4 = (bf16[4,64,512]{2,1,0:T(8,128)(2,1)S(1)}, bf16[4,64,512]{2,1,0:T(8,128)(2,1)S(1)}, u32[]{:S(2)}, u32[]{:S(2)}) collective-permute-start(bf16[4,64,512]{2,1,0:T(8,128)(2,1)S(1)} %select_n.22), channel_id=1, source_target_pairs={{0,2},{2,0},{4,6},{6,4},{8,10},{10,8},{12,14},{14,12},{1,3},{3,1},... | collective-permute-start | bytes 786440 | tf_op jit(solution)/shard_map/ppermute | solution.py:285
  29.8 11.9 %collective-permute-start.3 = (bf16[4,64,1024]{2,1,0:T(8,128)(2,1)S(1)}, bf16[4,64,1024]{2,1,0:T(8,128)(2,1)S(1)}, u32[]{:S(2)}, u32[]{:S(2)}) collective-permute-start(bf16[4,64,1024]{2,1,0:T(8,128)(2,1)S(1)} %pad_maximum_fusion.2.refs_0_), channel_id=1, source_target_pairs={{0,1},{1,0},{2,3},{3,2},{4,5},{5,4},{6,7},{7,6},{8,9},{9,8},{10,11... | collective-permute-start | bytes 1572872 | tf_op jit(solution)/shard_map/ppermute | solution.py:297
  32.9 12.1 %copy-start.2 = (bf16[1,512,256]{2,1,0:T(8,128)(2,1)S(1)}, bf16[1,512,256]{2,1,0:T(8,128)(2,1)}, u32[]{:S(2)}) copy-start(bf16[1,512,256]{2,1,0:T(8,128)(2,1)} %param.10) | copy-start | bytes 786436
  33.0 12.0 %collective-permute-start.6 = (bf16[2,768,256]{2,1,0:T(8,128)(2,1)S(1)}, bf16[2,768,256]{2,1,0:T(8,128)(2,1)S(1)}, u32[]{:S(2)}, u32[]{:S(2)}) collective-permute-start(bf16[2,768,256]{2,1,0:T(8,128)(2,1)S(1)} %copy-done), channel_id=1, source_target_pairs={{0,1},{1,0},{2,3},{3,2},{4,5},{5,4},{6,7},{7,6},{8,9},{9,8},{10,11... | collective-permute-start | bytes 2359304 | tf_op jit(solution)/shard_map/ppermute | solution.py:297
  38.9 10.2 %collective-permute-start.12 = (bf16[2,768,256]{2,1,0:T(8,128)(2,1)S(1)}, bf16[2,768,256]{2,1,0:T(8,128)(2,1)S(1)}, u32[]{:S(2)}, u32[]{:S(2)}) collective-permute-start(bf16[2,768,256]{2,1,0:T(8,128)(2,1)S(1)} %pad_maximum_fusion), channel_id=1, source_target_pairs={{0,1},{1,0},{2,3},{3,2},{4,5},{5,4},{6,7},{7,6},{8,9},{9,8},{10,11... | collective-permute-start | bytes 2359304 | tf_op jit(solution)/shard_map/ppermute | solution.py:285
  41.6 7.5 %copy-start.1 = (bf16[2,1536,256]{2,1,0:T(8,128)(2,1)S(1)}, bf16[2,1536,256]{2,1,0:T(8,128)(2,1)}, u32[]{:S(2)}) copy-start(bf16[2,1536,256]{2,1,0:T(8,128)(2,1)} %lc.1) | copy-start | bytes 4718596
  41.6 7.5 %copy-start.3 = (bf16[2,512,256]{2,1,0:T(8,128)(2,1)S(1)}, bf16[2,512,256]{2,1,0:T(8,128)(2,1)}, u32[]{:S(2)}) copy-start(bf16[2,512,256]{2,1,0:T(8,128)(2,1)} %dc.1) | copy-start | bytes 1572868
  41.6 7.5 %copy-start.4 = (s32[2,2]{1,0:T(2,128)S(1)}, s32[2,2]{1,0:T(2,128)}, u32[]{:S(2)}) copy-start(s32[2,2]{1,0:T(2,128)} %keep_ref.3) | copy-start | bytes 52
  41.7 7.5 %copy-start.5 = (s32[2]{0:T(128)S(1)}, s32[2]{0:T(128)}, u32[]{:S(2)}) copy-start(s32[2]{0:T(128)} %parent_ref.1) | copy-start | bytes 28
  41.7 7.5 %collective-permute-start.13 = (bf16[2,768,256]{2,1,0:T(8,128)(2,1)S(1)}, bf16[2,768,256]{2,1,0:T(8,128)(2,1)S(1)}, u32[]{:S(2)}, u32[]{:S(2)}) collective-permute-start(bf16[2,768,256]{2,1,0:T(8,128)(2,1)S(1)} %pad_maximum_fusion.1), channel_id=1, source_target_pairs={{0,1},{1,0},{2,3},{3,2},{4,5},{5,4},{6,7},{7,6},{8,9},{9,8},{10,11... | collective-permute-start | bytes 2359304 | tf_op jit(solution)/shard_map/ppermute | solution.py:285
  41.8 3.2 %collective-permute-start.5 = (bf16[4,64,512]{2,1,0:T(8,128)(2,1)S(1)}, bf16[4,64,512]{2,1,0:T(8,128)(2,1)S(1)}, u32[]{:S(2)}, u32[]{:S(2)}) collective-permute-start(bf16[4,64,512]{2,1,0:T(8,128)(2,1)S(1)} %collective-permute-done.4.refs_2_), channel_id=1, source_target_pairs={{0,1},{1,0},{2,3},{3,2},{4,5},{5,4},{6,7},{7,6},{8,9},{9,8},{10,11... | collective-permute-start | bytes 786440 | tf_op jit(solution)/shard_map/ppermute | solution.py:297

commit v5 on v4

--- a/solution.py
+++ b/solution.py
@@ -17,10 +17,10 @@
     )),
     (1, (
         "a 2",
-        "c other",
+        "far other",
     )),
     (1, (
-        "a 2",
+        "beyond 0",
         "own other",
     )),
 )

time: 55.9 us -> 54.6 us (0.977)
  starting transfers between devices: 20.8 us -> 19.1 us
    ppermute x10, starting transfers between devices: 13.7 us -> 12.1 us  [value(): got[name] = lax.ppermute(value(source), axis, pairs)]
  transfers between devices with their start and end apart: 14 -> 14, of which waited for: 4 -> 5; matrix products, arithmetic and copies ran while one was open for 3% -> 3% of each run, Pallas kernels for 7% -> 8%
where the time goes in v5:
time: 54.6 us; the launch traced here: 54.2 us
  starting transfers between devices  19.1 us (35%)
  waiting for transfers between devices  18.9 us (35%)
  Pallas kernels  13.5 us (25%)
  local copies, waits for them, and re-layouts  1.55 us (3%)
  between operations  0.88 us (2%)
    ppermute x10, waiting for transfers between devices, value(): got[name] = lax.ppermute(value(source), axis, pairs)  16.2 us
    ppermute x10, starting transfers between devices, value(): got[name] = lax.ppermute(value(source), axis, pairs)  12.1 us
    ppermute x4, starting transfers between devices, local(): got[name] = lax.ppermute(sent, axis, pairs)  7 us
    pallas_call x1, Pallas kernels, local(): pl.pallas_call(child_kernel, out_shape=(jax.ShapeDtypeStruct(l_child.shap...  6.45 us
    pallas_call x1, Pallas kernels, local(): pl.pallas_call(functools.partial(parent_kernel, direct=direct), out_shape...  4.16 us
    pallas_call x1, Pallas kernels, local(): pl.pallas_call(pack_kernel, out_shape=(packed,) * parts + (jax.ShapeDtype...  2.86 us
    ppermute x4, waiting for transfers between devices, local(): got[name] = lax.ppermute(sent, axis, pairs)  2.7 us
    another operation x5, local copies, waits for them, and re-layouts, value(): near = jnp.stack([got['a'], *(value(f'a {k}') for k in range(1, planes))])  1.25 us
  transfers between devices with their start and end apart: 14, of which 5 were waited for; matrix products, arithmetic and copies ran while one was open for 3% of the time, Pallas kernels for 8%

profile of v5, /device:TPU:3, one launch (start us, length us, event | category | flops | bytes accessed | tf_op | source)
XLA Modules:
  0.0 54.2 jit_solution(14536883318878973590)
XLA Ops:
  0.6 2.9 %shard_map.103 = (bf16[768,256]{1,0:T(8,128)(2,1)}, bf16[768,256]{1,0:T(8,128)(2,1)}, bf16[2,768,256]{2,1,0:T(8,128)(2,1)}) custom-call(s32[1,2]{1,0:T(1,128)} %keep_ref.2, bf16[1024,256]{1,0:T(8,128)(2,1)} %bitcast.19, bf16[512,256]{1,0:T(8,128)(2,1)} %bitcast.17), custom_call_target="tpu_custom_call" | custom-call | tf_op jit(solution)/shard_map/pallas_call | solution.py:244
  3.5 3.4 %collective-permute-start.2 = (bf16[64,1024]{1,0:T(8,128)(2,1)}, bf16[64,1024]{1,0:T(8,128)(2,1)S(1)}, u32[]{:S(2)}, u32[]{:S(2)}) collective-permute-start(bf16[64,1024]{1,0:T(8,128)(2,1)} %param.8), channel_id=1, source_target_pairs={{0,12},{2,14},{4,0},{6,2},{8,4},{10,6},{12,8},{14,10},{1,13},{3,15... | collective-permute-start | bytes 393224 | tf_op jit(solution)/shard_map/ppermute | solution.py:285
  6.9 0.5 collective-permute-start
  7.3 0.3 collective-permute-start.6
  7.6 1.2 %collective-permute-start.10 = (bf16[768,256]{1,0:T(8,128)(2,1)}, bf16[768,256]{1,0:T(8,128)(2,1)S(1)}, u32[]{:S(2)}, u32[]{:S(2)}) collective-permute-start(bf16[768,256]{1,0:T(8,128)(2,1)} %get-tuple-element.24), channel_id=1, source_target_pairs={{0,2},{2,0},{4,6},{6,4},{8,10},{10,8},{12,14},{14,12},{1,3},{3,1},... | collective-permute-start | bytes 1179656 | tf_op jit(solution)/shard_map/ppermute | solution.py:285
  8.8 1.0 %stack.48 = bf16[1,64,4,2,128]{4,3,2,1,0:T(2,128)(2,1)S(1)} reshape(bf16[64,1024]{1,0:T(8,128)(2,1)} %param.8) | data formatting | bytes 262144 | tf_op jit(solution)/shard_map/stack | solution.py:278
  9.8 2.2 %collective-permute-start.9 = (bf16[2,1536,256]{2,1,0:T(8,128)(2,1)}, bf16[2,1536,256]{2,1,0:T(8,128)(2,1)}, u32[]{:S(2)}, u32[]{:S(2)}) collective-permute-start(bf16[2,1536,256]{2,1,0:T(8,128)(2,1)} %lc.1), channel_id=1, source_target_pairs={{0,1},{1,0},{2,3},{3,2},{4,5},{5,4},{6,7},{7,6},{8,9},{9,8},{10,11... | collective-permute-start | bytes 4718600 | tf_op jit(solution)/shard_map/ppermute | solution.py:285
  12.1 3.7 %collective-permute-done = bf16[64,1024]{1,0:T(8,128)(2,1)S(1)} collective-permute-done((bf16[64,1024]{1,0:T(8,128)(2,1)}, bf16[64,1024]{1,0:T(8,128)(2,1)S(1)}, u32[]{:S(2)}, u32[]{:S(2)}) %collective-permute-start) | collective-permute-done | bytes 131104 | tf_op jit(solution)/shard_map/ppermute | solution.py:285
  15.9 2.1 %collective-permute-done.1 = bf16[64,1024]{1,0:T(8,128)(2,1)S(1)} collective-permute-done((bf16[64,1024]{1,0:T(8,128)(2,1)}, bf16[64,1024]{1,0:T(8,128)(2,1)S(1)}, u32[]{:S(2)}, u32[]{:S(2)}) %collective-permute-start.1) | collective-permute-done | bytes 131104 | tf_op jit(solution)/shard_map/ppermute | solution.py:285
  18.3 1.3 %collective-permute-start.7 = (bf16[768,256]{1,0:T(8,128)(2,1)S(1)}, bf16[768,256]{1,0:T(8,128)(2,1)S(1)}, u32[]{:S(2)}, u32[]{:S(2)}) collective-permute-start(bf16[768,256]{1,0:T(8,128)(2,1)S(1)} %collective-permute-done.6.refs_0_), channel_id=1, source_target_pairs={{0,4},{4,8},{6,2},{8,12},{10,6},{14,10},{1,5},{5,9},{7,3},{9,13},{... | collective-permute-start | bytes 1179656 | tf_op jit(solution)/shard_map/ppermute | solution.py:297
  19.6 5.5 %collective-permute-done.10.refs_1_ = bf16[768,256]{1,0:T(8,128)(2,1)S(1)} collective-permute-done((bf16[768,256]{1,0:T(8,128)(2,1)}, bf16[768,256]{1,0:T(8,128)(2,1)S(1)}, u32[]{:S(2)}, u32[]{:S(2)}) %collective-permute-start.10) | collective-permute-done | bytes 393248 | tf_op jit(solution)/shard_map/ppermute | solution.py:285
  25.0 1.3 %collective-permute-start.11 = (bf16[768,256]{1,0:T(8,128)(2,1)S(1)}, bf16[768,256]{1,0:T(8,128)(2,1)S(1)}, u32[]{:S(2)}, u32[]{:S(2)}) collective-permute-start(bf16[768,256]{1,0:T(8,128)(2,1)S(1)} %collective-permute-done.10.refs_1_), channel_id=1, source_target_pairs={{0,4},{4,8},{6,2},{8,12},{10,6},{14,10},{1,5},{5,9},{7,3},{9,13},{... | collective-permute-start | bytes 1179656 | tf_op jit(solution)/shard_map/ppermute | solution.py:285
  26.3 0.1 slice_select_fusion
  26.5 0.1 select_n.22
  26.6 3.2 %collective-permute-start.4 = (bf16[4,64,512]{2,1,0:T(8,128)(2,1)S(1)}, bf16[4,64,512]{2,1,0:T(8,128)(2,1)S(1)}, u32[]{:S(2)}, u32[]{:S(2)}) collective-permute-start(bf16[4,64,512]{2,1,0:T(8,128)(2,1)S(1)} %select_n.22), channel_id=1, source_target_pairs={{0,2},{2,0},{4,6},{6,4},{8,10},{10,8},{12,14},{14,12},{1,3},{3,1},... | collective-permute-start | bytes 786440 | tf_op jit(solution)/shard_map/ppermute | solution.py:285
  29.8 3.1 %collective-permute-start.3 = (bf16[4,64,1024]{2,1,0:T(8,128)(2,1)S(1)}, bf16[4,64,1024]{2,1,0:T(8,128)(2,1)S(1)}, u32[]{:S(2)}, u32[]{:S(2)}) collective-permute-start(bf16[4,64,1024]{2,1,0:T(8,128)(2,1)S(1)} %pad_maximum_fusion.2.refs_0_), channel_id=1, source_target_pairs={{0,1},{1,0},{2,3},{3,2},{4,5},{5,4},{6,7},{7,6},{8,9},{9,8},{10,11... | collective-permute-start | bytes 1572872 | tf_op jit(solution)/shard_map/ppermute | solution.py:297
  32.9 0.1 pad_maximum_fusion
  33.0 0.1 collective-permute-start.12
  33.1 4.9 %collective-permute-done.11.refs_3_ = bf16[768,256]{1,0:T(8,128)(2,1)S(1)} collective-permute-done((bf16[768,256]{1,0:T(8,128)(2,1)S(1)}, bf16[768,256]{1,0:T(8,128)(2,1)S(1)}, u32[]{:S(2)}, u32[]{:S(2)}) %collective-permute-start.11) | collective-permute-done | bytes 393248 | tf_op jit(solution)/shard_map/ppermute | solution.py:285
  38.0 2.2 %collective-permute-start.8 = (bf16[2,768,256]{2,1,0:T(8,128)(2,1)S(1)}, bf16[2,768,256]{2,1,0:T(8,128)(2,1)S(1)}, u32[]{:S(2)}, u32[]{:S(2)}) collective-permute-start(bf16[2,768,256]{2,1,0:T(8,128)(2,1)S(1)} %copy-done), channel_id=1, source_target_pairs={{0,1},{1,0},{2,3},{3,2},{4,5},{5,4},{6,7},{7,6},{8,9},{9,8},{10,11... | collective-permute-start | bytes 2359304 | tf_op jit(solution)/shard_map/ppermute | solution.py:297
  40.4 0.5 collective-permute-start.5
  40.9 2.7 %collective-permute-done.5.refs_3_ = bf16[4,64,512]{2,1,0:T(8,128)(2,1)S(1)} collective-permute-done((bf16[4,64,512]{2,1,0:T(8,128)(2,1)S(1)}, bf16[4,64,512]{2,1,0:T(8,128)(2,1)S(1)}, u32[]{:S(2)}, u32[]{:S(2)}) %collective-permute-start.5) | collective-permute-done | bytes 262176 | tf_op jit(solution)/shard_map/ppermute | solution.py:297
  43.6 4.2 %shard_map.104 = (bf16[512,256]{1,0:T(8,128)(2,1)}, bf16[1024,1024]{1,0:T(8,128)(2,1)S(1)}) custom-call(bf16[4,64,1024]{2,1,0:T(8,128)(2,1)S(1)} %pad_maximum_fusion.2.refs_0_, bf16[4,64,1024]{2,1,0:T(8,128)(2,1)S(1)} %collective-permute-done.3.refs_1_, bf16[4,64,512]{2,1,0:T(8,128)(2,1)S(1)} %collective-permute-done.4.refs_2_, ...), custom_call_target="tpu_custom_call" | custom-call | flops 805306368 | bytes 8388608 | tf_op jit(solution)/shard_map/pallas_call | solution.py:302
  47.8 6.5 %shard_map.105 = (bf16[2,1536,256]{2,1,0:T(8,128)(2,1)}, bf16[2,512,256]{2,1,0:T(8,128)(2,1)}) custom-call(s32[2]{0:T(128)S(1)} %copy-done.5, s32[2,2]{1,0:T(2,128)S(1)} %copy-done.4, bf16[1024,1024]{1,0:T(8,128)(2,1)S(1)} %get-tuple-element.23.a, bf16[2,1536,256]{2,1,0:T(8,128)(2,1)S(1)} %copy-done.1, bf16[2,1536,256]{2,1,0:T(8,128)(2,1)} %collective-permute-done.9.lc_o, ...), custom_call_target="tpu_custom_call" | custom-call | tf_op jit(solution)/shard_map/pallas_call | solution.py:322
  (34 shorter events, 0.7 us)
Async XLA Ops:
  3.5 6.3 %collective-permute-start.2 = (bf16[64,1024]{1,0:T(8,128)(2,1)}, bf16[64,1024]{1,0:T(8,128)(2,1)S(1)}, u32[]{:S(2)}, u32[]{:S(2)}) collective-permute-start(bf16[64,1024]{1,0:T(8,128)(2,1)} %param.8), channel_id=1, source_target_pairs={{0,12},{2,14},{4,0},{6,2},{8,4},{10,6},{12,8},{14,10},{1,13},{3,15... | collective-permute-start | bytes 393224 | tf_op jit(solution)/shard_map/ppermute | solution.py:285
  6.9 11.2 %collective-permute-start.1 = (bf16[64,1024]{1,0:T(8,128)(2,1)}, bf16[64,1024]{1,0:T(8,128)(2,1)S(1)}, u32[]{:S(2)}, u32[]{:S(2)}) collective-permute-start(bf16[64,1024]{1,0:T(8,128)(2,1)} %param.8), channel_id=1, source_target_pairs={{0,8},{2,10},{4,12},{6,14},{8,0},{10,2},{12,4},{14,6},{1,9},{3,11}... | collective-permute-start | bytes 393224 | tf_op jit(solution)/shard_map/ppermute | solution.py:285
  6.9 8.9 %collective-permute-start = (bf16[64,1024]{1,0:T(8,128)(2,1)}, bf16[64,1024]{1,0:T(8,128)(2,1)S(1)}, u32[]{:S(2)}, u32[]{:S(2)}) collective-permute-start(bf16[64,1024]{1,0:T(8,128)(2,1)} %param.8), channel_id=1, source_target_pairs={{0,4},{2,6},{4,8},{6,10},{8,12},{10,14},{12,0},{14,2},{1,5},{3,7},... | collective-permute-start | bytes 393224 | tf_op jit(solution)/shard_map/ppermute | solution.py:285
  7.3 11.0 %collective-permute-start.6 = (bf16[768,256]{1,0:T(8,128)(2,1)}, bf16[768,256]{1,0:T(8,128)(2,1)S(1)}, u32[]{:S(2)}, u32[]{:S(2)}) collective-permute-start(bf16[768,256]{1,0:T(8,128)(2,1)} %get-tuple-element.20), channel_id=1, source_target_pairs={{0,2},{2,0},{4,6},{6,4},{8,10},{10,8},{12,14},{14,12},{1,3},{3,1},... | collective-permute-start | bytes 1179656 | tf_op jit(solution)/shard_map/ppermute | solution.py:285
  7.6 17.5 %collective-permute-start.10 = (bf16[768,256]{1,0:T(8,128)(2,1)}, bf16[768,256]{1,0:T(8,128)(2,1)S(1)}, u32[]{:S(2)}, u32[]{:S(2)}) collective-permute-start(bf16[768,256]{1,0:T(8,128)(2,1)} %get-tuple-element.24), channel_id=1, source_target_pairs={{0,2},{2,0},{4,6},{6,4},{8,10},{10,8},{12,14},{14,12},{1,3},{3,1},... | collective-permute-start | bytes 1179656 | tf_op jit(solution)/shard_map/ppermute | solution.py:285
  9.8 20.0 %copy-start.6 = (bf16[64,1024]{1,0:T(8,128)(2,1)S(1)}, bf16[64,1024]{1,0:T(8,128)(2,1)}, u32[]{:S(2)}) copy-start(bf16[64,1024]{1,0:T(8,128)(2,1)} %param.8) | copy-start | bytes 393220
  9.8 37.9 %collective-permute-start.9 = (bf16[2,1536,256]{2,1,0:T(8,128)(2,1)}, bf16[2,1536,256]{2,1,0:T(8,128)(2,1)}, u32[]{:S(2)}, u32[]{:S(2)}) collective-permute-start(bf16[2,1536,256]{2,1,0:T(8,128)(2,1)} %lc.1), channel_id=1, source_target_pairs={{0,1},{1,0},{2,3},{3,2},{4,5},{5,4},{6,7},{7,6},{8,9},{9,8},{10,11... | collective-permute-start | bytes 4718600 | tf_op jit(solution)/shard_map/ppermute | solution.py:285
  18.3 14.7 %collective-permute-start.7 = (bf16[768,256]{1,0:T(8,128)(2,1)S(1)}, bf16[768,256]{1,0:T(8,128)(2,1)S(1)}, u32[]{:S(2)}, u32[]{:S(2)}) collective-permute-start(bf16[768,256]{1,0:T(8,128)(2,1)S(1)} %collective-permute-done.6.refs_0_), channel_id=1, source_target_pairs={{0,4},{4,8},{6,2},{8,12},{10,6},{14,10},{1,5},{5,9},{7,3},{9,13},{... | collective-permute-start | bytes 1179656 | tf_op jit(solution)/shard_map/ppermute | solution.py:297
  25.0 12.9 %collective-permute-start.11 = (bf16[768,256]{1,0:T(8,128)(2,1)S(1)}, bf16[768,256]{1,0:T(8,128)(2,1)S(1)}, u32[]{:S(2)}, u32[]{:S(2)}) collective-permute-start(bf16[768,256]{1,0:T(8,128)(2,1)S(1)} %collective-permute-done.10.refs_1_), channel_id=1, source_target_pairs={{0,4},{4,8},{6,2},{8,12},{10,6},{14,10},{1,5},{5,9},{7,3},{9,13},{... | collective-permute-start | bytes 1179656 | tf_op jit(solution)/shard_map/ppermute | solution.py:285
  26.5 11.5 %copy-start = (bf16[2,768,256]{2,1,0:T(8,128)(2,1)S(1)}, bf16[2,768,256]{2,1,0:T(8,128)(2,1)}, u32[]{:S(2)}) copy-start(bf16[2,768,256]{2,1,0:T(8,128)(2,1)} %get-tuple-element.21.refs_4_.own) | copy-start | bytes 2359300
  26.6 13.7 %collective-permute-start.4 = (bf16[4,64,512]{2,1,0:T(8,128)(2,1)S(1)}, bf16[4,64,512]{2,1,0:T(8,128)(2,1)S(1)}, u32[]{:S(2)}, u32[]{:S(2)}) collective-permute-start(bf16[4,64,512]{2,1,0:T(8,128)(2,1)S(1)} %select_n.22), channel_id=1, source_target_pairs={{0,2},{2,0},{4,6},{6,4},{8,10},{10,8},{12,14},{14,12},{1,3},{3,1},... | collective-permute-start | bytes 786440 | tf_op jit(solution)/shard_map/ppermute | solution.py:285
  29.8 10.5 %collective-permute-start.3 = (bf16[4,64,1024]{2,1,0:T(8,128)(2,1)S(1)}, bf16[4,64,1024]{2,1,0:T(8,128)(2,1)S(1)}, u32[]{:S(2)}, u32[]{:S(2)}) collective-permute-start(bf16[4,64,1024]{2,1,0:T(8,128)(2,1)S(1)} %pad_maximum_fusion.2.refs_0_), channel_id=1, source_target_pairs={{0,1},{1,0},{2,3},{3,2},{4,5},{5,4},{6,7},{7,6},{8,9},{9,8},{10,11... | collective-permute-start | bytes 1572872 | tf_op jit(solution)/shard_map/ppermute | solution.py:297
  32.9 10.6 %copy-start.2 = (bf16[1,512,256]{2,1,0:T(8,128)(2,1)S(1)}, bf16[1,512,256]{2,1,0:T(8,128)(2,1)}, u32[]{:S(2)}) copy-start(bf16[1,512,256]{2,1,0:T(8,128)(2,1)} %param.10) | copy-start | bytes 786436
  33.0 14.7 %collective-permute-start.12 = (bf16[2,768,256]{2,1,0:T(8,128)(2,1)S(1)}, bf16[2,768,256]{2,1,0:T(8,128)(2,1)S(1)}, u32[]{:S(2)}, u32[]{:S(2)}) collective-permute-start(bf16[2,768,256]{2,1,0:T(8,128)(2,1)S(1)} %pad_maximum_fusion), channel_id=1, source_target_pairs={{0,1},{1,0},{2,3},{3,2},{4,5},{5,4},{6,7},{7,6},{8,9},{9,8},{10,11... | collective-permute-start | bytes 2359304 | tf_op jit(solution)/shard_map/ppermute | solution.py:285
  38.0 5.6 %collective-permute-start.8 = (bf16[2,768,256]{2,1,0:T(8,128)(2,1)S(1)}, bf16[2,768,256]{2,1,0:T(8,128)(2,1)S(1)}, u32[]{:S(2)}, u32[]{:S(2)}) collective-permute-start(bf16[2,768,256]{2,1,0:T(8,128)(2,1)S(1)} %copy-done), channel_id=1, source_target_pairs={{0,1},{1,0},{2,3},{3,2},{4,5},{5,4},{6,7},{7,6},{8,9},{9,8},{10,11... | collective-permute-start | bytes 2359304 | tf_op jit(solution)/shard_map/ppermute | solution.py:297
  40.2 7.5 %copy-start.1 = (bf16[2,1536,256]{2,1,0:T(8,128)(2,1)S(1)}, bf16[2,1536,256]{2,1,0:T(8,128)(2,1)}, u32[]{:S(2)}) copy-start(bf16[2,1536,256]{2,1,0:T(8,128)(2,1)} %lc.1) | copy-start | bytes 4718596
  40.2 7.5 %copy-start.3 = (bf16[2,512,256]{2,1,0:T(8,128)(2,1)S(1)}, bf16[2,512,256]{2,1,0:T(8,128)(2,1)}, u32[]{:S(2)}) copy-start(bf16[2,512,256]{2,1,0:T(8,128)(2,1)} %dc.1) | copy-start | bytes 1572868
  40.2 7.5 %copy-start.4 = (s32[2,2]{1,0:T(2,128)S(1)}, s32[2,2]{1,0:T(2,128)}, u32[]{:S(2)}) copy-start(s32[2,2]{1,0:T(2,128)} %keep_ref.3) | copy-start | bytes 52
  40.3 7.5 %copy-start.5 = (s32[2]{0:T(128)S(1)}, s32[2]{0:T(128)}, u32[]{:S(2)}) copy-start(s32[2]{0:T(128)} %parent_ref.1) | copy-start | bytes 28
  40.3 7.5 %collective-permute-start.13 = (bf16[2,768,256]{2,1,0:T(8,128)(2,1)S(1)}, bf16[2,768,256]{2,1,0:T(8,128)(2,1)S(1)}, u32[]{:S(2)}, u32[]{:S(2)}) collective-permute-start(bf16[2,768,256]{2,1,0:T(8,128)(2,1)S(1)} %pad_maximum_fusion.1), channel_id=1, source_target_pairs={{0,1},{1,0},{2,3},{3,2},{4,5},{5,4},{6,7},{7,6},{8,9},{9,8},{10,11... | collective-permute-start | bytes 2359304 | tf_op jit(solution)/shard_map/ppermute | solution.py:285
  40.4 3.2 %collective-permute-start.5 = (bf16[4,64,512]{2,1,0:T(8,128)(2,1)S(1)}, bf16[4,64,512]{2,1,0:T(8,128)(2,1)S(1)}, u32[]{:S(2)}, u32[]{:S(2)}) collective-permute-start(bf16[4,64,512]{2,1,0:T(8,128)(2,1)S(1)} %collective-permute-done.4.refs_2_), channel_id=1, source_target_pairs={{0,1},{1,0},{2,3},{3,2},{4,5},{5,4},{6,7},{7,6},{8,9},{9,8},{10,11... | collective-permute-start | bytes 786440 | tf_op jit(solution)/shard_map/ppermute | solution.py:297

commit v6 on v5

--- a/solution.py
+++ b/solution.py
@@ -79,20 +79,32 @@
     planes, block = near.shape[:2]
     me, at, pair = place
     copies = []
-    for i, ref in enumerate((far, far_o)):
-        copies.append(loads.start(ref, b.at[i]))
     for ref, core in ((near, me), (near_o, 1 - me)):
         for k in range(planes):
             plane = lax.rem(at + planes - k, planes)
             row = pl.multiple_of(((plane * 2 + pair) * 2 + core) * block, block)
             copies.append(loads.start(ref.at[k], a.at[pl.ds(row, block)]))
-    return copies
-
-
-def place_top(place, a, b):
+    return copies, [loads.start(ref, b.at[i]) for i, ref in enumerate((far, far_o))]
+
+
+def place_top(place, first, second, a, b):
     me, at, mine_at = place
     _, planes, block, _ = b.shape
     span = 2 * block
+    wait(first)
+    for pair in range(2):
+
+        @pl.when(mine_at == pair)
+        def _():
+            for i in range(planes):
+                for j in range(planes):
+                    mine = (2 * i + pair) * span
+                    theirs = (2 * j + 1 - pair) * span
+                    a[theirs : theirs + span, mine : mine + span] = a[
+                        mine : mine + span, theirs : theirs + span
+                    ].T
+
+    wait(second)
     for pair in range(2):
 
         @pl.when(mine_at == pair)
@@ -104,13 +116,6 @@
                     for j in range(planes):
                         col = (2 * j + 1 - pair) * span
                         a[pl.ds(row, block), col : col + span] = b[i, k, :, j * span : (j + 1) * span]
-            for i in range(planes):
-                for j in range(planes):
-                    mine = (2 * i + pair) * span
-                    theirs = (2 * j + 1 - pair) * span
-                    a[theirs : theirs + span, mine : mine + span] = a[
-                        mine : mine + span, theirs : theirs + span
-                    ].T
 
 
 def place_of():
@@ -135,8 +140,7 @@
     parts = own.shape[0]
     loads = Loads(sem)
     if direct:
-        wait(load_top(loads, place, *a_refs, a, b))
-        place_top(place, a, b)
+        place_top(place, *load_top(loads, place, *a_refs, a, b), a, b)
     else:
         loads.start(a_refs[0], a).wait()
     head = pl.ds(0, width)
@@ -218,7 +222,7 @@
         for i, r in enumerate((lc, co)):
             y = dot_t(r[k, below, :], t[k]) + dot_t(r[k, head, :], cc[k])
             cd[k, ends[i], :] = (dc[k, ends[i], :].astype(F32) - y).astype(BF16)
-        outs.append(loads.start(cd.at[k], cd_out.at[k]))
+            outs.append(loads.start(cd.at[k, ends[i]], cd_out.at[k, ends[i]]))
     wait(outs)
 
 

time: 54.6 us -> 54.6 us (level)
  no operation moved by 1% of the time
where the time goes in v6:
time: 54.6 us; the launch traced here: 54.2 us
  starting transfers between devices  19.1 us (35%)
  waiting for transfers between devices  19 us (35%)
  Pallas kernels  13.4 us (25%)
  local copies, waits for them, and re-layouts  1.55 us (3%)
  between operations  0.88 us (2%)
    ppermute x10, waiting for transfers between devices, value(): got[name] = lax.ppermute(value(source), axis, pairs)  16.2 us
    ppermute x10, starting transfers between devices, value(): got[name] = lax.ppermute(value(source), axis, pairs)  12.1 us
    ppermute x4, starting transfers between devices, local(): got[name] = lax.ppermute(sent, axis, pairs)  6.99 us
    pallas_call x1, Pallas kernels, local(): pl.pallas_call(child_kernel, out_shape=(jax.ShapeDtypeStruct(l_child.shap...  6.44 us
    pallas_call x1, Pallas kernels, local(): pl.pallas_call(functools.partial(parent_kernel, direct=direct), out_shape...  4.14 us
    pallas_call x1, Pallas kernels, local(): pl.pallas_call(pack_kernel, out_shape=(packed,) * parts + (jax.ShapeDtype...  2.85 us
    ppermute x4, waiting for transfers between devices, local(): got[name] = lax.ppermute(sent, axis, pairs)  2.7 us
    another operation x5, local copies, waits for them, and re-layouts, value(): near = jnp.stack([got['a'], *(value(f'a {k}') for k in range(1, planes))])  1.25 us
  transfers between devices with their start and end apart: 14, of which 5 were waited for; matrix products, arithmetic and copies ran while one was open for 3% of the time, Pallas kernels for 8%

profile of v6, /device:TPU:3, one launch (start us, length us, event | category | flops | bytes accessed | tf_op | source)
XLA Modules:
  0.0 54.2 jit_solution(4694225210480510653)
XLA Ops:
  0.6 2.9 %shard_map.103 = (bf16[768,256]{1,0:T(8,128)(2,1)}, bf16[768,256]{1,0:T(8,128)(2,1)}, bf16[2,768,256]{2,1,0:T(8,128)(2,1)}) custom-call(s32[1,2]{1,0:T(1,128)} %keep_ref.2, bf16[1024,256]{1,0:T(8,128)(2,1)} %bitcast.19, bf16[512,256]{1,0:T(8,128)(2,1)} %bitcast.17), custom_call_target="tpu_custom_call" | custom-call | tf_op jit(solution)/shard_map/pallas_call | solution.py:248
  3.5 3.4 %collective-permute-start.2 = (bf16[64,1024]{1,0:T(8,128)(2,1)}, bf16[64,1024]{1,0:T(8,128)(2,1)S(1)}, u32[]{:S(2)}, u32[]{:S(2)}) collective-permute-start(bf16[64,1024]{1,0:T(8,128)(2,1)} %param.8), channel_id=1, source_target_pairs={{0,12},{2,14},{4,0},{6,2},{8,4},{10,6},{12,8},{14,10},{1,13},{3,15... | collective-permute-start | bytes 393224 | tf_op jit(solution)/shard_map/ppermute | solution.py:289
  6.9 0.5 collective-permute-start
  7.3 0.2 collective-permute-start.6
  7.6 1.2 %collective-permute-start.10 = (bf16[768,256]{1,0:T(8,128)(2,1)}, bf16[768,256]{1,0:T(8,128)(2,1)S(1)}, u32[]{:S(2)}, u32[]{:S(2)}) collective-permute-start(bf16[768,256]{1,0:T(8,128)(2,1)} %get-tuple-element.24), channel_id=1, source_target_pairs={{0,2},{2,0},{4,6},{6,4},{8,10},{10,8},{12,14},{14,12},{1,3},{3,1},... | collective-permute-start | bytes 1179656 | tf_op jit(solution)/shard_map/ppermute | solution.py:289
  8.8 1.0 %stack.48 = bf16[1,64,4,2,128]{4,3,2,1,0:T(2,128)(2,1)S(1)} reshape(bf16[64,1024]{1,0:T(8,128)(2,1)} %param.8) | data formatting | bytes 262144 | tf_op jit(solution)/shard_map/stack | solution.py:282
  9.9 2.2 %collective-permute-start.9 = (bf16[2,1536,256]{2,1,0:T(8,128)(2,1)}, bf16[2,1536,256]{2,1,0:T(8,128)(2,1)}, u32[]{:S(2)}, u32[]{:S(2)}) collective-permute-start(bf16[2,1536,256]{2,1,0:T(8,128)(2,1)} %lc.1), channel_id=1, source_target_pairs={{0,1},{1,0},{2,3},{3,2},{4,5},{5,4},{6,7},{7,6},{8,9},{9,8},{10,11... | collective-permute-start | bytes 4718600 | tf_op jit(solution)/shard_map/ppermute | solution.py:289
  12.1 3.7 %collective-permute-done = bf16[64,1024]{1,0:T(8,128)(2,1)S(1)} collective-permute-done((bf16[64,1024]{1,0:T(8,128)(2,1)}, bf16[64,1024]{1,0:T(8,128)(2,1)S(1)}, u32[]{:S(2)}, u32[]{:S(2)}) %collective-permute-start) | collective-permute-done | bytes 131104 | tf_op jit(solution)/shard_map/ppermute | solution.py:289
  16.0 2.1 %collective-permute-done.1 = bf16[64,1024]{1,0:T(8,128)(2,1)S(1)} collective-permute-done((bf16[64,1024]{1,0:T(8,128)(2,1)}, bf16[64,1024]{1,0:T(8,128)(2,1)S(1)}, u32[]{:S(2)}, u32[]{:S(2)}) %collective-permute-start.1) | collective-permute-done | bytes 131104 | tf_op jit(solution)/shard_map/ppermute | solution.py:289
  18.3 1.3 %collective-permute-start.7 = (bf16[768,256]{1,0:T(8,128)(2,1)S(1)}, bf16[768,256]{1,0:T(8,128)(2,1)S(1)}, u32[]{:S(2)}, u32[]{:S(2)}) collective-permute-start(bf16[768,256]{1,0:T(8,128)(2,1)S(1)} %collective-permute-done.6.refs_0_), channel_id=1, source_target_pairs={{0,4},{4,8},{6,2},{8,12},{10,6},{14,10},{1,5},{5,9},{7,3},{9,13},{... | collective-permute-start | bytes 1179656 | tf_op jit(solution)/shard_map/ppermute | solution.py:301
  19.6 5.5 %collective-permute-done.10.refs_1_ = bf16[768,256]{1,0:T(8,128)(2,1)S(1)} collective-permute-done((bf16[768,256]{1,0:T(8,128)(2,1)}, bf16[768,256]{1,0:T(8,128)(2,1)S(1)}, u32[]{:S(2)}, u32[]{:S(2)}) %collective-permute-start.10) | collective-permute-done | bytes 393248 | tf_op jit(solution)/shard_map/ppermute | solution.py:289
  25.1 1.3 %collective-permute-start.11 = (bf16[768,256]{1,0:T(8,128)(2,1)S(1)}, bf16[768,256]{1,0:T(8,128)(2,1)S(1)}, u32[]{:S(2)}, u32[]{:S(2)}) collective-permute-start(bf16[768,256]{1,0:T(8,128)(2,1)S(1)} %collective-permute-done.10.refs_1_), channel_id=1, source_target_pairs={{0,4},{4,8},{6,2},{8,12},{10,6},{14,10},{1,5},{5,9},{7,3},{9,13},{... | collective-permute-start | bytes 1179656 | tf_op jit(solution)/shard_map/ppermute | solution.py:289
  26.4 0.1 slice_select_fusion
  26.5 0.1 select_n.22
  26.6 3.1 %collective-permute-start.4 = (bf16[4,64,512]{2,1,0:T(8,128)(2,1)S(1)}, bf16[4,64,512]{2,1,0:T(8,128)(2,1)S(1)}, u32[]{:S(2)}, u32[]{:S(2)}) collective-permute-start(bf16[4,64,512]{2,1,0:T(8,128)(2,1)S(1)} %select_n.22), channel_id=1, source_target_pairs={{0,2},{2,0},{4,6},{6,4},{8,10},{10,8},{12,14},{14,12},{1,3},{3,1},... | collective-permute-start | bytes 786440 | tf_op jit(solution)/shard_map/ppermute | solution.py:289
  29.8 3.1 %collective-permute-start.3 = (bf16[4,64,1024]{2,1,0:T(8,128)(2,1)S(1)}, bf16[4,64,1024]{2,1,0:T(8,128)(2,1)S(1)}, u32[]{:S(2)}, u32[]{:S(2)}) collective-permute-start(bf16[4,64,1024]{2,1,0:T(8,128)(2,1)S(1)} %pad_maximum_fusion.2.refs_0_), channel_id=1, source_target_pairs={{0,1},{1,0},{2,3},{3,2},{4,5},{5,4},{6,7},{7,6},{8,9},{9,8},{10,11... | collective-permute-start | bytes 1572872 | tf_op jit(solution)/shard_map/ppermute | solution.py:301
  32.9 0.1 pad_maximum_fusion
  33.0 0.1 collective-permute-start.12
  33.1 4.9 %collective-permute-done.11.refs_3_ = bf16[768,256]{1,0:T(8,128)(2,1)S(1)} collective-permute-done((bf16[768,256]{1,0:T(8,128)(2,1)S(1)}, bf16[768,256]{1,0:T(8,128)(2,1)S(1)}, u32[]{:S(2)}, u32[]{:S(2)}) %collective-permute-start.11) | collective-permute-done | bytes 393248 | tf_op jit(solution)/shard_map/ppermute | solution.py:289
  38.0 2.1 %collective-permute-start.8 = (bf16[2,768,256]{2,1,0:T(8,128)(2,1)S(1)}, bf16[2,768,256]{2,1,0:T(8,128)(2,1)S(1)}, u32[]{:S(2)}, u32[]{:S(2)}) collective-permute-start(bf16[2,768,256]{2,1,0:T(8,128)(2,1)S(1)} %copy-done), channel_id=1, source_target_pairs={{0,1},{1,0},{2,3},{3,2},{4,5},{5,4},{6,7},{7,6},{8,9},{9,8},{10,11... | collective-permute-start | bytes 2359304 | tf_op jit(solution)/shard_map/ppermute | solution.py:301
  40.4 0.5 collective-permute-start.5
  40.9 2.7 %collective-permute-done.5.refs_3_ = bf16[4,64,512]{2,1,0:T(8,128)(2,1)S(1)} collective-permute-done((bf16[4,64,512]{2,1,0:T(8,128)(2,1)S(1)}, bf16[4,64,512]{2,1,0:T(8,128)(2,1)S(1)}, u32[]{:S(2)}, u32[]{:S(2)}) %collective-permute-start.5) | collective-permute-done | bytes 262176 | tf_op jit(solution)/shard_map/ppermute | solution.py:301
  43.6 4.1 %shard_map.104 = (bf16[512,256]{1,0:T(8,128)(2,1)}, bf16[1024,1024]{1,0:T(8,128)(2,1)S(1)}) custom-call(bf16[4,64,1024]{2,1,0:T(8,128)(2,1)S(1)} %pad_maximum_fusion.2.refs_0_, bf16[4,64,1024]{2,1,0:T(8,128)(2,1)S(1)} %collective-permute-done.3.refs_1_, bf16[4,64,512]{2,1,0:T(8,128)(2,1)S(1)} %collective-permute-done.4.refs_2_, ...), custom_call_target="tpu_custom_call" | custom-call | flops 805306368 | bytes 8388608 | tf_op jit(solution)/shard_map/pallas_call | solution.py:306
  47.8 6.4 %shard_map.105 = (bf16[2,1536,256]{2,1,0:T(8,128)(2,1)}, bf16[2,512,256]{2,1,0:T(8,128)(2,1)}) custom-call(s32[2]{0:T(128)S(1)} %copy-done.5, s32[2,2]{1,0:T(2,128)S(1)} %copy-done.4, bf16[1024,1024]{1,0:T(8,128)(2,1)S(1)} %get-tuple-element.23.a, bf16[2,1536,256]{2,1,0:T(8,128)(2,1)S(1)} %copy-done.1, bf16[2,1536,256]{2,1,0:T(8,128)(2,1)} %collective-permute-done.9.lc_o, ...), custom_call_target="tpu_custom_call" | custom-call | tf_op jit(solution)/shard_map/pallas_call | solution.py:326
  (34 shorter events, 0.7 us)
Async XLA Ops:
  3.5 6.4 %collective-permute-start.2 = (bf16[64,1024]{1,0:T(8,128)(2,1)}, bf16[64,1024]{1,0:T(8,128)(2,1)S(1)}, u32[]{:S(2)}, u32[]{:S(2)}) collective-permute-start(bf16[64,1024]{1,0:T(8,128)(2,1)} %param.8), channel_id=1, source_target_pairs={{0,12},{2,14},{4,0},{6,2},{8,4},{10,6},{12,8},{14,10},{1,13},{3,15... | collective-permute-start | bytes 393224 | tf_op jit(solution)/shard_map/ppermute | solution.py:289
  6.9 11.2 %collective-permute-start.1 = (bf16[64,1024]{1,0:T(8,128)(2,1)}, bf16[64,1024]{1,0:T(8,128)(2,1)S(1)}, u32[]{:S(2)}, u32[]{:S(2)}) collective-permute-start(bf16[64,1024]{1,0:T(8,128)(2,1)} %param.8), channel_id=1, source_target_pairs={{0,8},{2,10},{4,12},{6,14},{8,0},{10,2},{12,4},{14,6},{1,9},{3,11}... | collective-permute-start | bytes 393224 | tf_op jit(solution)/shard_map/ppermute | solution.py:289
  6.9 9.0 %collective-permute-start = (bf16[64,1024]{1,0:T(8,128)(2,1)}, bf16[64,1024]{1,0:T(8,128)(2,1)S(1)}, u32[]{:S(2)}, u32[]{:S(2)}) collective-permute-start(bf16[64,1024]{1,0:T(8,128)(2,1)} %param.8), channel_id=1, source_target_pairs={{0,4},{2,6},{4,8},{6,10},{8,12},{10,14},{12,0},{14,2},{1,5},{3,7},... | collective-permute-start | bytes 393224 | tf_op jit(solution)/shard_map/ppermute | solution.py:289
  7.3 10.9 %collective-permute-start.6 = (bf16[768,256]{1,0:T(8,128)(2,1)}, bf16[768,256]{1,0:T(8,128)(2,1)S(1)}, u32[]{:S(2)}, u32[]{:S(2)}) collective-permute-start(bf16[768,256]{1,0:T(8,128)(2,1)} %get-tuple-element.20), channel_id=1, source_target_pairs={{0,2},{2,0},{4,6},{6,4},{8,10},{10,8},{12,14},{14,12},{1,3},{3,1},... | collective-permute-start | bytes 1179656 | tf_op jit(solution)/shard_map/ppermute | solution.py:289
  7.6 17.5 %collective-permute-start.10 = (bf16[768,256]{1,0:T(8,128)(2,1)}, bf16[768,256]{1,0:T(8,128)(2,1)S(1)}, u32[]{:S(2)}, u32[]{:S(2)}) collective-permute-start(bf16[768,256]{1,0:T(8,128)(2,1)} %get-tuple-element.24), channel_id=1, source_target_pairs={{0,2},{2,0},{4,6},{6,4},{8,10},{10,8},{12,14},{14,12},{1,3},{3,1},... | collective-permute-start | bytes 1179656 | tf_op jit(solution)/shard_map/ppermute | solution.py:289
  9.8 20.0 %copy-start.6 = (bf16[64,1024]{1,0:T(8,128)(2,1)S(1)}, bf16[64,1024]{1,0:T(8,128)(2,1)}, u32[]{:S(2)}) copy-start(bf16[64,1024]{1,0:T(8,128)(2,1)} %param.8) | copy-start | bytes 393220
  9.9 37.9 %collective-permute-start.9 = (bf16[2,1536,256]{2,1,0:T(8,128)(2,1)}, bf16[2,1536,256]{2,1,0:T(8,128)(2,1)}, u32[]{:S(2)}, u32[]{:S(2)}) collective-permute-start(bf16[2,1536,256]{2,1,0:T(8,128)(2,1)} %lc.1), channel_id=1, source_target_pairs={{0,1},{1,0},{2,3},{3,2},{4,5},{5,4},{6,7},{7,6},{8,9},{9,8},{10,11... | collective-permute-start | bytes 4718600 | tf_op jit(solution)/shard_map/ppermute | solution.py:289
  18.3 14.7 %collective-permute-start.7 = (bf16[768,256]{1,0:T(8,128)(2,1)S(1)}, bf16[768,256]{1,0:T(8,128)(2,1)S(1)}, u32[]{:S(2)}, u32[]{:S(2)}) collective-permute-start(bf16[768,256]{1,0:T(8,128)(2,1)S(1)} %collective-permute-done.6.refs_0_), channel_id=1, source_target_pairs={{0,4},{4,8},{6,2},{8,12},{10,6},{14,10},{1,5},{5,9},{7,3},{9,13},{... | collective-permute-start | bytes 1179656 | tf_op jit(solution)/shard_map/ppermute | solution.py:301
  25.1 12.9 %collective-permute-start.11 = (bf16[768,256]{1,0:T(8,128)(2,1)S(1)}, bf16[768,256]{1,0:T(8,128)(2,1)S(1)}, u32[]{:S(2)}, u32[]{:S(2)}) collective-permute-start(bf16[768,256]{1,0:T(8,128)(2,1)S(1)} %collective-permute-done.10.refs_1_), channel_id=1, source_target_pairs={{0,4},{4,8},{6,2},{8,12},{10,6},{14,10},{1,5},{5,9},{7,3},{9,13},{... | collective-permute-start | bytes 1179656 | tf_op jit(solution)/shard_map/ppermute | solution.py:289
  26.5 11.5 %copy-start = (bf16[2,768,256]{2,1,0:T(8,128)(2,1)S(1)}, bf16[2,768,256]{2,1,0:T(8,128)(2,1)}, u32[]{:S(2)}) copy-start(bf16[2,768,256]{2,1,0:T(8,128)(2,1)} %get-tuple-element.21.refs_4_.own) | copy-start | bytes 2359300
  26.6 13.7 %collective-permute-start.4 = (bf16[4,64,512]{2,1,0:T(8,128)(2,1)S(1)}, bf16[4,64,512]{2,1,0:T(8,128)(2,1)S(1)}, u32[]{:S(2)}, u32[]{:S(2)}) collective-permute-start(bf16[4,64,512]{2,1,0:T(8,128)(2,1)S(1)} %select_n.22), channel_id=1, source_target_pairs={{0,2},{2,0},{4,6},{6,4},{8,10},{10,8},{12,14},{14,12},{1,3},{3,1},... | collective-permute-start | bytes 786440 | tf_op jit(solution)/shard_map/ppermute | solution.py:289
  29.8 10.5 %collective-permute-start.3 = (bf16[4,64,1024]{2,1,0:T(8,128)(2,1)S(1)}, bf16[4,64,1024]{2,1,0:T(8,128)(2,1)S(1)}, u32[]{:S(2)}, u32[]{:S(2)}) collective-permute-start(bf16[4,64,1024]{2,1,0:T(8,128)(2,1)S(1)} %pad_maximum_fusion.2.refs_0_), channel_id=1, source_target_pairs={{0,1},{1,0},{2,3},{3,2},{4,5},{5,4},{6,7},{7,6},{8,9},{9,8},{10,11... | collective-permute-start | bytes 1572872 | tf_op jit(solution)/shard_map/ppermute | solution.py:301
  32.9 10.7 %copy-start.2 = (bf16[1,512,256]{2,1,0:T(8,128)(2,1)S(1)}, bf16[1,512,256]{2,1,0:T(8,128)(2,1)}, u32[]{:S(2)}) copy-start(bf16[1,512,256]{2,1,0:T(8,128)(2,1)} %param.10) | copy-start | bytes 786436
  33.0 14.7 %collective-permute-start.12 = (bf16[2,768,256]{2,1,0:T(8,128)(2,1)S(1)}, bf16[2,768,256]{2,1,0:T(8,128)(2,1)S(1)}, u32[]{:S(2)}, u32[]{:S(2)}) collective-permute-start(bf16[2,768,256]{2,1,0:T(8,128)(2,1)S(1)} %pad_maximum_fusion), channel_id=1, source_target_pairs={{0,1},{1,0},{2,3},{3,2},{4,5},{5,4},{6,7},{7,6},{8,9},{9,8},{10,11... | collective-permute-start | bytes 2359304 | tf_op jit(solution)/shard_map/ppermute | solution.py:289
  38.0 5.6 %collective-permute-start.8 = (bf16[2,768,256]{2,1,0:T(8,128)(2,1)S(1)}, bf16[2,768,256]{2,1,0:T(8,128)(2,1)S(1)}, u32[]{:S(2)}, u32[]{:S(2)}) collective-permute-start(bf16[2,768,256]{2,1,0:T(8,128)(2,1)S(1)} %copy-done), channel_id=1, source_target_pairs={{0,1},{1,0},{2,3},{3,2},{4,5},{5,4},{6,7},{7,6},{8,9},{9,8},{10,11... | collective-permute-start | bytes 2359304 | tf_op jit(solution)/shard_map/ppermute | solution.py:301
  40.2 7.5 %copy-start.1 = (bf16[2,1536,256]{2,1,0:T(8,128)(2,1)S(1)}, bf16[2,1536,256]{2,1,0:T(8,128)(2,1)}, u32[]{:S(2)}) copy-start(bf16[2,1536,256]{2,1,0:T(8,128)(2,1)} %lc.1) | copy-start | bytes 4718596
  40.2 7.5 %copy-start.3 = (bf16[2,512,256]{2,1,0:T(8,128)(2,1)S(1)}, bf16[2,512,256]{2,1,0:T(8,128)(2,1)}, u32[]{:S(2)}) copy-start(bf16[2,512,256]{2,1,0:T(8,128)(2,1)} %dc.1) | copy-start | bytes 1572868
  40.3 7.5 %copy-start.4 = (s32[2,2]{1,0:T(2,128)S(1)}, s32[2,2]{1,0:T(2,128)}, u32[]{:S(2)}) copy-start(s32[2,2]{1,0:T(2,128)} %keep_ref.3) | copy-start | bytes 52
  40.3 7.5 %copy-start.5 = (s32[2]{0:T(128)S(1)}, s32[2]{0:T(128)}, u32[]{:S(2)}) copy-start(s32[2]{0:T(128)} %parent_ref.1) | copy-start | bytes 28
  40.3 7.4 %collective-permute-start.13 = (bf16[2,768,256]{2,1,0:T(8,128)(2,1)S(1)}, bf16[2,768,256]{2,1,0:T(8,128)(2,1)S(1)}, u32[]{:S(2)}, u32[]{:S(2)}) collective-permute-start(bf16[2,768,256]{2,1,0:T(8,128)(2,1)S(1)} %pad_maximum_fusion.1), channel_id=1, source_target_pairs={{0,1},{1,0},{2,3},{3,2},{4,5},{5,4},{6,7},{7,6},{8,9},{9,8},{10,11... | collective-permute-start | bytes 2359304 | tf_op jit(solution)/shard_map/ppermute | solution.py:289
  40.4 3.2 %collective-permute-start.5 = (bf16[4,64,512]{2,1,0:T(8,128)(2,1)S(1)}, bf16[4,64,512]{2,1,0:T(8,128)(2,1)S(1)}, u32[]{:S(2)}, u32[]{:S(2)}) collective-permute-start(bf16[4,64,512]{2,1,0:T(8,128)(2,1)S(1)} %collective-permute-done.4.refs_2_), channel_id=1, source_target_pairs={{0,1},{1,0},{2,3},{3,2},{4,5},{5,4},{6,7},{7,6},{8,9},{9,8},{10,11... | collective-permute-start | bytes 786440 | tf_op jit(solution)/shard_map/ppermute | solution.py:301
